TPU v7x, 32 devices: a whole 2x2x4 slice. The times are simulated.
32 devices in a mesh: req: 8 (over z, y), ctx: 4 (over x, core).
Axes of the slice: x: 2, y: 2, z: 4, core: 2. Of those that a mesh axis runs over, the one named last changes fastest.
Arguments:
- q_nope: bfloat16 [8, 128, 8192], P('req'), may hold values from -6 to 6
- q_rope: bfloat16 [8, 128, 4096], P('req'), may hold values from -600 to 600
- cache_latent: bfloat16 [8, 1024, 512], P('req', 'ctx'), may hold values from -6 to 6
- cache_rope: bfloat16 [8, 1024, 64], P('req', 'ctx'), may hold values from -4 to 4
- new_latent: bfloat16 [8, 128, 512], P('req', 'ctx'), may hold values from -6 to 6
- new_rope: bfloat16 [8, 128, 64], P('req', 'ctx'), may hold values from -8 to 8
- lengths: int32 [8, 4], P('req', 'ctx'), may hold values from 64 to 256, as said below
- w_key: bfloat16 [512, 8192], P(None, 'ctx'), may hold values from -0.25 to 0.25
- w_value: bfloat16 [512, 8192], P(None, 'ctx'), may hold values from -0.25 to 0.25
Outputs:
- attended: bfloat16 [8, 128, 8192], P('req', None, 'ctx')
Inputs may be any that keep to these rules, and one draw needn't show every extreme that they name: lengths[r, g] counts the live cached rows at the start of request r's slots in context group g; all cached rows precede the new tokens; some entry equals 256 in every draw.
All inputs are finite; a program needn't handle non-finite values.
Results may differ from a plain program's by a relative error of at most 0.015.
Values may be sent and summed in bfloat16 or wider, within the bound.
No kernel may reach another device: no remote copies, remote signals or barrier semaphores. Data moves between devices by JAX's collectives and lax.ppermute only.
A program may use at most 128 MiB of HBM per device.

v0:
```python
import math

import jax
import jax.numpy as jnp
from jax import lax
from jax.sharding import PartitionSpec as P

DR = 64
DH = 128
DV = 128
HEADS = 64
GROUP = 4
BLOCK = 256


blocked_score = -1e30


def expand_block(
    lat_rows, rope_keys, visible, query_nope, query_rope, weight_key, weight_value, running
):
    running_max, running_sum, running_out = running
    row_count = lat_rows.shape[0]
    score_scale = 1.0 / math.sqrt(DH + DR)
    key_rows = jnp.dot(lat_rows, weight_key, preferred_element_type=jnp.float32).astype(
        jnp.bfloat16
    )
    value_rows = jnp.dot(lat_rows, weight_value, preferred_element_type=jnp.float32).astype(
        jnp.bfloat16
    )
    key_rows = key_rows.reshape(row_count, GROUP, DH)
    value_rows = value_rows.reshape(row_count, GROUP, DV)
    scores = jnp.einsum("qhd,khd->qhk", query_nope, key_rows, preferred_element_type=jnp.float32)
    scores = scores + jnp.einsum(
        "qhd,kd->qhk", query_rope, rope_keys, preferred_element_type=jnp.float32
    )
    scores = jnp.where(visible[:, None, :], scores * score_scale, blocked_score)
    new_max = jnp.maximum(running_max, jnp.max(scores, axis=-1))
    factor = jnp.exp(running_max - new_max)
    weights = jnp.where(visible[:, None, :], jnp.exp(scores - new_max[..., None]), 0.0)
    running_sum = running_sum * factor + jnp.sum(weights, axis=-1)
    running_out = running_out * factor[..., None] + jnp.einsum(
        "qhk,khd->qhd", weights.astype(jnp.bfloat16), value_rows, preferred_element_type=jnp.float32
    )
    return (new_max, running_sum, running_out)


def start_running(query_count):
    return (
        jnp.full((query_count, GROUP), blocked_score, jnp.float32),
        jnp.zeros((query_count, GROUP), jnp.float32),
        jnp.zeros((query_count, GROUP, DV), jnp.float32),
    )


def cached_pass(
    running, query_nope, query_rope, weight_key, weight_value, cache_rows, cache_keys, live_rows
):

    def advance(block_index, running):
        offset = block_index * BLOCK
        visible = (offset + jnp.arange(BLOCK, dtype=jnp.int32))[None, :] < live_rows
        visible = jnp.broadcast_to(visible, (query_nope.shape[0], BLOCK))
        return expand_block(
            cache_rows,
            cache_keys,
            visible,
            query_nope,
            query_rope,
            weight_key,
            weight_value,
            running,
        )

    block_count = (live_rows + BLOCK - 1) // BLOCK
    return lax.fori_loop(0, block_count, advance, running)


def fresh_pass(running, query_nope, query_rope, weight_key, weight_value, fresh_rows, fresh_keys):
    query_count = query_nope.shape[0]
    fresh_index = jnp.arange(fresh_rows.shape[0], dtype=jnp.int32)
    visible = fresh_index[None, :] <= jnp.arange(query_count, dtype=jnp.int32)[:, None]
    return expand_block(
        fresh_rows, fresh_keys, visible, query_nope, query_rope, weight_key, weight_value, running
    )


def shards(q_nope, q_rope, cache_latent, cache_rope, new_latent, new_rope, lengths, w_key, w_value):
    ctx_count = lax.axis_size("ctx")
    ctx_index = lax.axis_index("ctx")
    queries = q_nope[0]
    rotary = q_rope[0]
    query_count = queries.shape[0]
    width_key = GROUP * DH
    width_value = GROUP * DV
    heads_here = HEADS // ctx_count
    own_groups = heads_here // GROUP
    slot_rows = cache_latent.shape[1]
    whole_latent, whole_rope, whole_fresh, whole_fresh_rope = (
        lax.all_gather(cache_latent[0], "ctx", axis=0, tiled=True),
        lax.all_gather(cache_rope[0], "ctx", axis=0, tiled=True),
        lax.all_gather(new_latent[0], "ctx", axis=0, tiled=True),
        lax.all_gather(new_rope[0], "ctx", axis=0, tiled=True),
    )
    live_all = lax.all_gather(lengths[0], "ctx", axis=0, tiled=True)
    outputs = []
    for group_index in range(own_groups):
        weight_key = w_key[:, group_index * width_key : (group_index + 1) * width_key]
        weight_value = w_value[:, group_index * width_value : (group_index + 1) * width_value]
        head_first = ctx_index * heads_here + group_index * GROUP
        query_nope = lax.dynamic_slice_in_dim(queries, head_first * DH, GROUP * DH, 1).reshape(
            query_count, GROUP, DH
        )
        query_rope = lax.dynamic_slice_in_dim(rotary, head_first * DR, GROUP * DR, 1).reshape(
            query_count, GROUP, DR
        )
        running = start_running(query_count)
        for group_ctx in range(ctx_count):
            running = cached_pass(
                running,
                query_nope,
                query_rope,
                weight_key,
                weight_value,
                whole_latent[group_ctx * slot_rows : (group_ctx + 1) * slot_rows],
                whole_rope[group_ctx * slot_rows : (group_ctx + 1) * slot_rows],
                live_all[group_ctx],
            )
        running = fresh_pass(
            running, query_nope, query_rope, weight_key, weight_value, whole_fresh, whole_fresh_rope
        )
        group_max, group_sum, group_out = running
        outputs.append(group_out / group_sum[..., None])
    attended = jnp.concatenate(outputs, axis=1).reshape(query_count, heads_here * DV)
    return attended.astype(jnp.bfloat16)[None]


def solution(mesh):
    return jax.shard_map(
        shards,
        mesh=mesh,
        in_specs=(
            P("req", None, None),
            P("req", None, None),
            P("req", "ctx", None),
            P("req", "ctx", None),
            P("req", "ctx", None),
            P("req", "ctx", None),
            P("req", "ctx"),
            P(None, "ctx"),
            P(None, "ctx"),
        ),
        out_specs=P("req", None, "ctx"),
        check_vma=False,
    )
```

profile of v0, /device:TPU:0, one launch (start us, length us, event | category | flops | bytes accessed | tf_op | source)
XLA Modules:
  0.0 132.5 jit_solution(6945543223880134889)
XLA Ops:
  6.5 0.7 all-gather.7.cloned.1.call-update
  7.3 6.8 %all-gather.3 = bf16[1,128,512]{2,1,0:T(8,128)(2,1)S(1)} all-gather(bf16[1,32,512]{2,1,0:T(8,128)(2,1)} %param.45), channel_id=5, replica_groups=mesh['req'=8,'ctx'=4] {'ctx'}, dimensions={1}, use_global_device_ids=true | all-gather | bytes 163840 | tf_op jit(solution)/shard_map/all_gather | solution.py:102
  14.1 1.3 fusion.266
  15.4 1.3 fusion.265
  16.7 1.3 fusion.264
  18.0 1.3 fusion.267
  22.3 5.3 %all-reduce = s32[4]{0:T(128)S(1)} all-reduce(s32[4]{0:T(128)S(1)} %bitcast_dynamic-update-slice_fusion), channel_id=2, replica_groups=mesh['req'=8,'ctx'=4] {'ctx'}, use_global_device_ids=true, to_apply=%add | all-reduce | flops 4 | bytes 32
  27.6 1.0 constant_dynamic-slice_fusion.2
  28.7 5.4 %all-gather.2 = bf16[1,1024,64]{1,2,0:T(8,128)(2,1)S(1)} all-gather(bf16[1,256,64]{1,2,0:T(8,128)(2,1)S(1)} %copy-done.2), channel_id=4, replica_groups=mesh['req'=8,'ctx'=4] {'ctx'}, dimensions={1}, use_global_device_ids=true | all-gather | bytes 163840 | tf_op jit(solution)/shard_map/all_gather | solution.py:101
  34.1 5.2 %all-gather.4 = bf16[1,128,64]{2,1,0:T(8,128)(2,1)S(1)} all-gather(bf16[1,32,64]{2,1,0:T(8,128)(2,1)S(1)} %copy-done.3), channel_id=6, replica_groups=mesh['req'=8,'ctx'=4] {'ctx'}, dimensions={1}, use_global_device_ids=true | all-gather | bytes 20480 | tf_op jit(solution)/shard_map/all_gather | solution.py:103
  39.8 1.1 constant_dynamic-slice_fusion.3
  45.5 0.8 copy.368
  46.3 0.8 copy.369
  48.5 1.4 %convolution_convert_fusion.14 = bf16[256,512]{1,0:T(8,128)(2,1)S(1)} fusion(bf16[512,2048]{1,0:T(8,128)(2,1)} %param.49, bf16[1,1024,512]{2,1,0:T(8,128)(2,1)} %all-gather.7.cloned.1.call-done), kind=kOutput, calls=%fused_computation.350 | convolution fusion | flops 134348800 | bytes 1048576 | tf_op jit(solution)/shard_map/while/body/dot_general | solution.py:28
  49.9 1.4 %convolution_convert_fusion.15 = bf16[256,512]{1,0:T(8,128)(2,1)S(1)} fusion(bf16[512,2048]{1,0:T(8,128)(2,1)} %param.48, bf16[1,1024,512]{2,1,0:T(8,128)(2,1)} %all-gather.7.cloned.1.call-done), kind=kOutput, calls=%fused_computation.351 | convolution fusion | flops 134348800 | bytes 1048576 | tf_op jit(solution)/shard_map/while/body/dot_general | solution.py:25
  51.4 1.8 %while.264 = (s32[]{:T(128)}, f32[128,4]{0,1:T(4,128)S(1)}, f32[128,4]{0,1:T(4,128)S(1)}, f32[128,4,128]{2,0,1:T(8,128)S(1)}, s32[]{:T(128)}, /*index=5*/s32[]{:...) while((s32[]{:T(128)}, f32[128,4]{0,1:T(4,128)S(1)}, ...), condition=%wide.region_39.40_spmd, body=%wide.region_36.39_spmd.sunk | while | flops 85329408 | bytes 3933329 | solution.py:76
  51.4 0.7 add_compare_fusion.40
  53.3 1.4 %convolution_convert_fusion.12 = bf16[256,512]{1,0:T(8,128)(2,1)S(1)} fusion(bf16[512,2048]{1,0:T(8,128)(2,1)} %param.49, bf16[1,1024,512]{2,1,0:T(8,128)(2,1)} %all-gather.7.cloned.1.call-done), kind=kOutput, calls=%fused_computation.348 | convolution fusion | flops 134348800 | bytes 1048576 | tf_op jit(solution)/shard_map/while/body/dot_general | solution.py:28
  54.7 1.4 %convolution_convert_fusion.13 = bf16[256,512]{1,0:T(8,128)(2,1)S(1)} fusion(bf16[512,2048]{1,0:T(8,128)(2,1)} %param.48, bf16[1,1024,512]{2,1,0:T(8,128)(2,1)} %all-gather.7.cloned.1.call-done), kind=kOutput, calls=%fused_computation.349 | convolution fusion | flops 134348800 | bytes 1048576 | tf_op jit(solution)/shard_map/while/body/dot_general | solution.py:25
  56.1 1.7 %while.265 = (s32[]{:T(128)}, f32[128,4]{0,1:T(4,128)S(1)}, f32[128,4]{0,1:T(4,128)S(1)}, f32[128,4,128]{2,0,1:T(8,128)S(1)}, s32[]{:T(128)}, /*index=5*/s32[]{:...) while((s32[]{:T(128)}, f32[128,4]{0,1:T(4,128)S(1)}, ...), condition=%wide.region_43.44_spmd, body=%wide.region_40.43_spmd.sunk | while | flops 85329408 | bytes 3933329 | solution.py:76
  57.8 1.4 %convolution_convert_fusion.10 = bf16[256,512]{1,0:T(8,128)(2,1)S(1)} fusion(bf16[512,2048]{1,0:T(8,128)(2,1)} %param.49, bf16[1,1024,512]{2,1,0:T(8,128)(2,1)} %all-gather.7.cloned.1.call-done), kind=kOutput, calls=%fused_computation.346 | convolution fusion | flops 134348800 | bytes 1048576 | tf_op jit(solution)/shard_map/while/body/dot_general | solution.py:28
  59.3 1.4 %convolution_convert_fusion.11 = bf16[256,512]{1,0:T(8,128)(2,1)S(1)} fusion(bf16[512,2048]{1,0:T(8,128)(2,1)} %param.48, bf16[1,1024,512]{2,1,0:T(8,128)(2,1)} %all-gather.7.cloned.1.call-done), kind=kOutput, calls=%fused_computation.347 | convolution fusion | flops 134348800 | bytes 1048576 | tf_op jit(solution)/shard_map/while/body/dot_general | solution.py:25
  60.7 1.8 %while.266 = (s32[]{:T(128)}, f32[128,4]{0,1:T(4,128)S(1)}, f32[128,4]{0,1:T(4,128)S(1)}, f32[128,4,128]{2,0,1:T(8,128)S(1)}, s32[]{:T(128)}, /*index=5*/s32[]{:...) while((s32[]{:T(128)}, f32[128,4]{0,1:T(4,128)S(1)}, ...), condition=%wide.region_47.48_spmd, body=%wide.region_44.47_spmd.sunk | while | flops 85329408 | bytes 3933329 | solution.py:76
  62.4 1.4 %convolution_convert_fusion.8 = bf16[256,512]{1,0:T(8,128)(2,1)S(1)} fusion(bf16[512,2048]{1,0:T(8,128)(2,1)} %param.49, bf16[1,1024,512]{2,1,0:T(8,128)(2,1)} %all-gather.7.cloned.1.call-done), kind=kOutput, calls=%fused_computation.344 | convolution fusion | flops 134348800 | bytes 1048576 | tf_op jit(solution)/shard_map/while/body/dot_general | solution.py:28
  63.9 1.4 %convolution_convert_fusion.9 = bf16[256,512]{1,0:T(8,128)(2,1)S(1)} fusion(bf16[512,2048]{1,0:T(8,128)(2,1)} %param.48, bf16[1,1024,512]{2,1,0:T(8,128)(2,1)} %all-gather.7.cloned.1.call-done), kind=kOutput, calls=%fused_computation.345 | convolution fusion | flops 134348800 | bytes 1048576 | tf_op jit(solution)/shard_map/while/body/dot_general | solution.py:25
  65.3 1.8 %while.267 = (s32[]{:T(128)}, f32[128,4]{0,1:T(4,128)S(1)}, f32[128,4]{0,1:T(4,128)S(1)}, f32[128,4,128]{2,0,1:T(8,128)S(1)}, s32[]{:T(128)}, /*index=5*/s32[]{:...) while((s32[]{:T(128)}, f32[128,4]{0,1:T(4,128)S(1)}, ...), condition=%wide.region_51.52_spmd, body=%wide.region_48.51_spmd.sunk | while | flops 85329408 | bytes 3933329 | solution.py:76
  67.1 1.4 %convolution_convert_fusion.22 = bf16[256,512]{1,0:T(8,128)(2,1)S(1)} fusion(bf16[512,2048]{1,0:T(8,128)(2,1)} %param.49, bf16[1,1024,512]{2,1,0:T(8,128)(2,1)} %all-gather.7.cloned.1.call-done), kind=kOutput, calls=%fused_computation.358 | convolution fusion | flops 134348800 | bytes 1048576 | tf_op jit(solution)/shard_map/while/body/dot_general | solution.py:28
  68.5 1.4 %convolution_convert_fusion.23 = bf16[256,512]{1,0:T(8,128)(2,1)S(1)} fusion(bf16[512,2048]{1,0:T(8,128)(2,1)} %param.48, bf16[1,1024,512]{2,1,0:T(8,128)(2,1)} %all-gather.7.cloned.1.call-done), kind=kOutput, calls=%fused_computation.359 | convolution fusion | flops 134348800 | bytes 1048576 | tf_op jit(solution)/shard_map/while/body/dot_general | solution.py:25
  70.0 1.8 %while.260 = (s32[]{:T(128)}, f32[128,4]{0,1:T(4,128)S(1)}, f32[128,4]{0,1:T(4,128)S(1)}, f32[128,4,128]{2,0,1:T(8,128)S(1)}, s32[]{:T(128)}, /*index=5*/s32[]{:...) while((s32[]{:T(128)}, f32[128,4]{0,1:T(4,128)S(1)}, ...), condition=%wide.region_21.22_spmd, body=%wide.region_18.21_spmd.sunk | while | flops 85329408 | bytes 3933329 | solution.py:76
  70.0 0.7 add_compare_fusion.36
  71.8 1.4 %convolution_convert_fusion.20 = bf16[256,512]{1,0:T(8,128)(2,1)S(1)} fusion(bf16[512,2048]{1,0:T(8,128)(2,1)} %param.49, bf16[1,1024,512]{2,1,0:T(8,128)(2,1)} %all-gather.7.cloned.1.call-done), kind=kOutput, calls=%fused_computation.356 | convolution fusion | flops 134348800 | bytes 1048576 | tf_op jit(solution)/shard_map/while/body/dot_general | solution.py:28
  73.2 1.4 %convolution_convert_fusion.21 = bf16[256,512]{1,0:T(8,128)(2,1)S(1)} fusion(bf16[512,2048]{1,0:T(8,128)(2,1)} %param.48, bf16[1,1024,512]{2,1,0:T(8,128)(2,1)} %all-gather.7.cloned.1.call-done), kind=kOutput, calls=%fused_computation.357 | convolution fusion | flops 134348800 | bytes 1048576 | tf_op jit(solution)/shard_map/while/body/dot_general | solution.py:25
  74.7 1.7 %while.261 = (s32[]{:T(128)}, f32[128,4]{0,1:T(4,128)S(1)}, f32[128,4]{0,1:T(4,128)S(1)}, f32[128,4,128]{2,0,1:T(8,128)S(1)}, s32[]{:T(128)}, /*index=5*/s32[]{:...) while((s32[]{:T(128)}, f32[128,4]{0,1:T(4,128)S(1)}, ...), condition=%wide.region_25.26_spmd, body=%wide.region_22.25_spmd.sunk | while | flops 85329408 | bytes 3933329 | solution.py:76
  76.4 1.4 %convolution_convert_fusion.18 = bf16[256,512]{1,0:T(8,128)(2,1)S(1)} fusion(bf16[512,2048]{1,0:T(8,128)(2,1)} %param.49, bf16[1,1024,512]{2,1,0:T(8,128)(2,1)} %all-gather.7.cloned.1.call-done), kind=kOutput, calls=%fused_computation.354 | convolution fusion | flops 134348800 | bytes 1048576 | tf_op jit(solution)/shard_map/while/body/dot_general | solution.py:28
  77.8 1.4 %convolution_convert_fusion.19 = bf16[256,512]{1,0:T(8,128)(2,1)S(1)} fusion(bf16[512,2048]{1,0:T(8,128)(2,1)} %param.48, bf16[1,1024,512]{2,1,0:T(8,128)(2,1)} %all-gather.7.cloned.1.call-done), kind=kOutput, calls=%fused_computation.355 | convolution fusion | flops 134348800 | bytes 1048576 | tf_op jit(solution)/shard_map/while/body/dot_general | solution.py:25
  79.2 1.9 %while.262 = (s32[]{:T(128)}, f32[128,4]{0,1:T(4,128)S(1)}, f32[128,4]{0,1:T(4,128)S(1)}, f32[128,4,128]{2,0,1:T(8,128)S(1)}, s32[]{:T(128)}, /*index=5*/s32[]{:...) while((s32[]{:T(128)}, f32[128,4]{0,1:T(4,128)S(1)}, ...), condition=%wide.region_29.30_spmd, body=%wide.region_26.29_spmd.sunk | while | flops 85329408 | bytes 3933329 | solution.py:76
  81.2 1.4 %convolution_convert_fusion.16 = bf16[256,512]{1,0:T(8,128)(2,1)S(1)} fusion(bf16[512,2048]{1,0:T(8,128)(2,1)} %param.49, bf16[1,1024,512]{2,1,0:T(8,128)(2,1)} %all-gather.7.cloned.1.call-done), kind=kOutput, calls=%fused_computation.352 | convolution fusion | flops 134348800 | bytes 1048576 | tf_op jit(solution)/shard_map/while/body/dot_general | solution.py:28
  82.6 1.4 %convolution_convert_fusion.17 = bf16[256,512]{1,0:T(8,128)(2,1)S(1)} fusion(bf16[512,2048]{1,0:T(8,128)(2,1)} %param.48, bf16[1,1024,512]{2,1,0:T(8,128)(2,1)} %all-gather.7.cloned.1.call-done), kind=kOutput, calls=%fused_computation.353 | convolution fusion | flops 134348800 | bytes 1048576 | tf_op jit(solution)/shard_map/while/body/dot_general | solution.py:25
  84.0 1.8 %while.263 = (s32[]{:T(128)}, f32[128,4]{0,1:T(4,128)S(1)}, f32[128,4]{0,1:T(4,128)S(1)}, f32[128,4,128]{2,0,1:T(8,128)S(1)}, s32[]{:T(128)}, /*index=5*/s32[]{:...) while((s32[]{:T(128)}, f32[128,4]{0,1:T(4,128)S(1)}, ...), condition=%wide.region_33.34_spmd, body=%wide.region_30.33_spmd.sunk | while | flops 85329408 | bytes 3933329 | solution.py:76
  85.8 1.4 %convolution_convert_fusion.30 = bf16[256,512]{1,0:T(8,128)(2,1)S(1)} fusion(bf16[512,2048]{1,0:T(8,128)(2,1)} %param.49, bf16[1,1024,512]{2,1,0:T(8,128)(2,1)} %all-gather.7.cloned.1.call-done), kind=kOutput, calls=%fused_computation.366 | convolution fusion | flops 134348800 | bytes 1048576 | tf_op jit(solution)/shard_map/while/body/dot_general | solution.py:28
  87.2 1.4 %convolution_convert_fusion.31 = bf16[256,512]{1,0:T(8,128)(2,1)S(1)} fusion(bf16[512,2048]{1,0:T(8,128)(2,1)} %param.48, bf16[1,1024,512]{2,1,0:T(8,128)(2,1)} %all-gather.7.cloned.1.call-done), kind=kOutput, calls=%fused_computation.367 | convolution fusion | flops 134348800 | bytes 1048576 | tf_op jit(solution)/shard_map/while/body/dot_general | solution.py:25
  88.7 1.8 %while.256 = (s32[]{:T(128)}, f32[128,4]{0,1:T(4,128)S(1)}, f32[128,4]{0,1:T(4,128)S(1)}, f32[128,4,128]{2,0,1:T(8,128)S(1)}, s32[]{:T(128)}, /*index=5*/s32[]{:...) while((s32[]{:T(128)}, f32[128,4]{0,1:T(4,128)S(1)}, ...), condition=%wide.region_3.4_spmd, body=%wide.region_0.3_spmd.sunk | while | flops 85329408 | bytes 3933329 | solution.py:76
  90.5 1.4 %convolution_convert_fusion.28 = bf16[256,512]{1,0:T(8,128)(2,1)S(1)} fusion(bf16[512,2048]{1,0:T(8,128)(2,1)} %param.49, bf16[1,1024,512]{2,1,0:T(8,128)(2,1)} %all-gather.7.cloned.1.call-done), kind=kOutput, calls=%fused_computation.364 | convolution fusion | flops 134348800 | bytes 1048576 | tf_op jit(solution)/shard_map/while/body/dot_general | solution.py:28
  92.0 1.4 %convolution_convert_fusion.29 = bf16[256,512]{1,0:T(8,128)(2,1)S(1)} fusion(bf16[512,2048]{1,0:T(8,128)(2,1)} %param.48, bf16[1,1024,512]{2,1,0:T(8,128)(2,1)} %all-gather.7.cloned.1.call-done), kind=kOutput, calls=%fused_computation.365 | convolution fusion | flops 134348800 | bytes 1048576 | tf_op jit(solution)/shard_map/while/body/dot_general | solution.py:25
  93.4 1.7 %while.257 = (s32[]{:T(128)}, f32[128,4]{0,1:T(4,128)S(1)}, f32[128,4]{0,1:T(4,128)S(1)}, f32[128,4,128]{2,0,1:T(8,128)S(1)}, s32[]{:T(128)}, /*index=5*/s32[]{:...) while((s32[]{:T(128)}, f32[128,4]{0,1:T(4,128)S(1)}, ...), condition=%wide.region_7.8_spmd, body=%wide.region_4.7_spmd.sunk | while | flops 85329408 | bytes 3933329 | solution.py:76
  95.1 1.4 %convolution_convert_fusion.26 = bf16[256,512]{1,0:T(8,128)(2,1)S(1)} fusion(bf16[512,2048]{1,0:T(8,128)(2,1)} %param.49, bf16[1,1024,512]{2,1,0:T(8,128)(2,1)} %all-gather.7.cloned.1.call-done), kind=kOutput, calls=%fused_computation.362 | convolution fusion | flops 134348800 | bytes 1048576 | tf_op jit(solution)/shard_map/while/body/dot_general | solution.py:28
  96.5 1.4 %convolution_convert_fusion.27 = bf16[256,512]{1,0:T(8,128)(2,1)S(1)} fusion(bf16[512,2048]{1,0:T(8,128)(2,1)} %param.48, bf16[1,1024,512]{2,1,0:T(8,128)(2,1)} %all-gather.7.cloned.1.call-done), kind=kOutput, calls=%fused_computation.363 | convolution fusion | flops 134348800 | bytes 1048576 | tf_op jit(solution)/shard_map/while/body/dot_general | solution.py:25
  97.9 1.8 %while.258 = (s32[]{:T(128)}, f32[128,4]{0,1:T(4,128)S(1)}, f32[128,4]{0,1:T(4,128)S(1)}, f32[128,4,128]{2,0,1:T(8,128)S(1)}, s32[]{:T(128)}, /*index=5*/s32[]{:...) while((s32[]{:T(128)}, f32[128,4]{0,1:T(4,128)S(1)}, ...), condition=%wide.region_11.12_spmd, body=%wide.region_8.11_spmd.sunk | while | flops 85329408 | bytes 3933329 | solution.py:76
  99.7 1.4 %convolution_convert_fusion.24 = bf16[256,512]{1,0:T(8,128)(2,1)S(1)} fusion(bf16[512,2048]{1,0:T(8,128)(2,1)} %param.49, bf16[1,1024,512]{2,1,0:T(8,128)(2,1)} %all-gather.7.cloned.1.call-done), kind=kOutput, calls=%fused_computation.360 | convolution fusion | flops 134348800 | bytes 1048576 | tf_op jit(solution)/shard_map/while/body/dot_general | solution.py:28
  101.1 1.4 %convolution_convert_fusion.25 = bf16[256,512]{1,0:T(8,128)(2,1)S(1)} fusion(bf16[512,2048]{1,0:T(8,128)(2,1)} %param.48, bf16[1,1024,512]{2,1,0:T(8,128)(2,1)} %all-gather.7.cloned.1.call-done), kind=kOutput, calls=%fused_computation.361 | convolution fusion | flops 134348800 | bytes 1048576 | tf_op jit(solution)/shard_map/while/body/dot_general | solution.py:25
  102.6 1.8 %while.259 = (s32[]{:T(128)}, f32[128,4]{0,1:T(4,128)S(1)}, f32[128,4]{0,1:T(4,128)S(1)}, f32[128,4,128]{2,0,1:T(8,128)S(1)}, s32[]{:T(128)}, /*index=5*/s32[]{:...) while((s32[]{:T(128)}, f32[128,4]{0,1:T(4,128)S(1)}, ...), condition=%wide.region_15.16_spmd, body=%wide.region_12.15_spmd.sunk | while | flops 85329408 | bytes 3933329 | solution.py:76
  104.3 1.4 %convolution_convert_fusion.6 = bf16[256,512]{1,0:T(8,128)(2,1)S(1)} fusion(bf16[512,2048]{1,0:T(8,128)(2,1)} %param.49, bf16[1,1024,512]{2,1,0:T(8,128)(2,1)} %all-gather.7.cloned.1.call-done), kind=kOutput, calls=%fused_computation.342 | convolution fusion | flops 134348800 | bytes 1048576 | tf_op jit(solution)/shard_map/while/body/dot_general | solution.py:28
  105.7 1.4 %convolution_convert_fusion.7 = bf16[256,512]{1,0:T(8,128)(2,1)S(1)} fusion(bf16[512,2048]{1,0:T(8,128)(2,1)} %param.48, bf16[1,1024,512]{2,1,0:T(8,128)(2,1)} %all-gather.7.cloned.1.call-done), kind=kOutput, calls=%fused_computation.343 | convolution fusion | flops 134348800 | bytes 1048576 | tf_op jit(solution)/shard_map/while/body/dot_general | solution.py:25
  107.2 1.8 %while.268 = (s32[]{:T(128)}, f32[128,4]{0,1:T(4,128)S(1)}, f32[128,4]{0,1:T(4,128)S(1)}, f32[128,4,128]{2,0,1:T(8,128)S(1)}, s32[]{:T(128)}, /*index=5*/s32[]{:...) while((s32[]{:T(128)}, f32[128,4]{0,1:T(4,128)S(1)}, ...), condition=%wide.region_57.58_spmd, body=%wide.region_54.57_spmd.sunk | while | flops 85329408 | bytes 3933329 | solution.py:76
  109.1 1.4 %convolution_convert_fusion.4 = bf16[256,512]{1,0:T(8,128)(2,1)S(1)} fusion(bf16[512,2048]{1,0:T(8,128)(2,1)} %param.49, bf16[1,1024,512]{2,1,0:T(8,128)(2,1)} %all-gather.7.cloned.1.call-done), kind=kOutput, calls=%fused_computation.340 | convolution fusion | flops 134348800 | bytes 1048576 | tf_op jit(solution)/shard_map/while/body/dot_general | solution.py:28
  110.5 1.4 %convolution_convert_fusion.5 = bf16[256,512]{1,0:T(8,128)(2,1)S(1)} fusion(bf16[512,2048]{1,0:T(8,128)(2,1)} %param.48, bf16[1,1024,512]{2,1,0:T(8,128)(2,1)} %all-gather.7.cloned.1.call-done), kind=kOutput, calls=%fused_computation.341 | convolution fusion | flops 134348800 | bytes 1048576 | tf_op jit(solution)/shard_map/while/body/dot_general | solution.py:25
  111.9 1.7 %while.269 = (s32[]{:T(128)}, f32[128,4]{0,1:T(4,128)S(1)}, f32[128,4]{0,1:T(4,128)S(1)}, f32[128,4,128]{2,0,1:T(8,128)S(1)}, s32[]{:T(128)}, /*index=5*/s32[]{:...) while((s32[]{:T(128)}, f32[128,4]{0,1:T(4,128)S(1)}, ...), condition=%wide.region_61.62_spmd, body=%wide.region_58.61_spmd.sunk | while | flops 85329408 | bytes 3933329 | solution.py:76
  113.6 1.4 %convolution_convert_fusion.2 = bf16[256,512]{1,0:T(8,128)(2,1)S(1)} fusion(bf16[512,2048]{1,0:T(8,128)(2,1)} %param.49, bf16[1,1024,512]{2,1,0:T(8,128)(2,1)} %all-gather.7.cloned.1.call-done), kind=kOutput, calls=%fused_computation.338 | convolution fusion | flops 134348800 | bytes 1048576 | tf_op jit(solution)/shard_map/while/body/dot_general | solution.py:28
  115.1 1.4 %convolution_convert_fusion.3 = bf16[256,512]{1,0:T(8,128)(2,1)S(1)} fusion(bf16[512,2048]{1,0:T(8,128)(2,1)} %param.48, bf16[1,1024,512]{2,1,0:T(8,128)(2,1)} %all-gather.7.cloned.1.call-done), kind=kOutput, calls=%fused_computation.339 | convolution fusion | flops 134348800 | bytes 1048576 | tf_op jit(solution)/shard_map/while/body/dot_general | solution.py:25
  116.5 1.8 %while.270 = (s32[]{:T(128)}, f32[128,4]{0,1:T(4,128)S(1)}, f32[128,4]{0,1:T(4,128)S(1)}, f32[128,4,128]{2,0,1:T(8,128)S(1)}, s32[]{:T(128)}, /*index=5*/s32[]{:...) while((s32[]{:T(128)}, f32[128,4]{0,1:T(4,128)S(1)}, ...), condition=%wide.region_65.66_spmd, body=%wide.region_62.65_spmd.sunk | while | flops 85329408 | bytes 3933329 | solution.py:76
  118.3 1.4 %convolution_convert_fusion = bf16[256,512]{1,0:T(8,128)(2,1)S(1)} fusion(bf16[512,2048]{1,0:T(8,128)(2,1)} %param.49, bf16[1,1024,512]{2,1,0:T(8,128)(2,1)} %all-gather.7.cloned.1.call-done), kind=kOutput, calls=%fused_computation.336 | convolution fusion | flops 134348800 | bytes 1048576 | tf_op jit(solution)/shard_map/while/body/dot_general | solution.py:28
  119.7 1.4 %convolution_convert_fusion.1 = bf16[256,512]{1,0:T(8,128)(2,1)S(1)} fusion(bf16[512,2048]{1,0:T(8,128)(2,1)} %param.48, bf16[1,1024,512]{2,1,0:T(8,128)(2,1)} %all-gather.7.cloned.1.call-done), kind=kOutput, calls=%fused_computation.337 | convolution fusion | flops 134348800 | bytes 1048576 | tf_op jit(solution)/shard_map/while/body/dot_general | solution.py:25
  121.1 1.8 %while.271 = (s32[]{:T(128)}, f32[128,4]{0,1:T(4,128)S(1)}, f32[128,4]{0,1:T(4,128)S(1)}, f32[128,4,128]{2,0,1:T(8,128)S(1)}, s32[]{:T(128)}, /*index=5*/s32[]{:...) while((s32[]{:T(128)}, f32[128,4]{0,1:T(4,128)S(1)}, ...), condition=%wide.region_69.70_spmd, body=%wide.region_66.69_spmd.sunk | while | flops 85329408 | bytes 3933329 | solution.py:76
  124.7 1.0 copy.327
  (200 shorter events, 33.7 us)
Async XLA Ops:
  6.5 42.0 %all-gather.7.cloned.1.call-start = ((), (), s32[]{:S(2)}) async-start(), calls=%async_computation | async-start | bytes 1310720 | tf_op jit(solution)/shard_map/all_gather | solution.py:100
  7.3 12.0 %copy-start.4 = (bf16[512,2048]{1,0:T(8,128)(2,1)S(1)}, bf16[512,2048]{1,0:T(8,128)(2,1)}, u32[]{:S(2)}) copy-start(bf16[512,2048]{1,0:T(8,128)(2,1)} %param.49) | copy-start | bytes 6291460
  18.0 3.0 %copy-start.5 = (u32[32]{0:T(128)S(1)}, u32[32]{0:T(128)}, u32[]{:S(2)}) copy-start(u32[32]{0:T(128)} %constant.522) | copy-start | bytes 388
  19.3 9.4 %copy-start.2 = (bf16[1,256,64]{1,2,0:T(8,128)(2,1)S(1)}, bf16[1,256,64]{1,2,0:T(8,128)(2,1)}, u32[]{:S(2)}) copy-start(bf16[1,256,64]{1,2,0:T(8,128)(2,1)} %param.44) | copy-start | bytes 98308
  19.3 14.8 %copy-start.3 = (bf16[1,32,64]{2,1,0:T(8,128)(2,1)S(1)}, bf16[1,32,64]{2,1,0:T(8,128)(2,1)}, u32[]{:S(2)}) copy-start(bf16[1,32,64]{2,1,0:T(8,128)(2,1)} %param.46) | copy-start | bytes 12292
  122.9 0.9 copy-start.1
  123.0 1.0 copy-start
Sparse Core Ops, SparseCore 0:
  8.9 19.4 all-gather.6
where the time goes:
time: 134 us; the launch traced here: 133 us
  matrix products  68.5 us (51%)
  blocking collectives  22.8 us (17%)
  between operations  17.6 us (13%)
  other arithmetic  12.7 us (9%)
  local copies, waits for them, and re-layouts  9.01 us (7%)
    dot_general x20, matrix products, expand_block(): jnp.dot(lat_rows, weight_key, preferred_element_type=jnp.float32)  27.9 us
    dot_general x20, matrix products, expand_block(): jnp.dot(lat_rows, weight_value, preferred_element_type=jnp.float32)  23.7 us
    lt x16, other arithmetic, advance(): visible = (offset + jnp.arange(BLOCK, dtype=jnp.int32))[None, :] < live_rows  10.1 us
    dot_general x20, matrix products, expand_block(): jnp.einsum('qhk,khd->qhd', weights.astype(jnp.bfloat16), value_rows, pref...  7.32 us
    all_gather x1, blocking collectives, shards(): lax.all_gather(new_latent[0], 'ctx', axis=0, tiled=True)  6.82 us
    all_gather x1, blocking collectives, shards(): lax.all_gather(cache_rope[0], 'ctx', axis=0, tiled=True)  5.43 us
    unnamed x1, blocking collectives  5.32 us
    dot_general x20, matrix products, expand_block(): jnp.einsum('qhd,kd->qhk', query_rope, rope_keys, preferred_element_type=j...  5.27 us
  transfers between devices with their start and end apart: 1, of which 0 were waited for; matrix products, arithmetic and copies ran while one was open for 11% of the time, Pallas kernels for 0%

commit v1 on v0

v1 whole, which is shorter than its diff:
```python
import functools
import math

import jax
import jax.numpy as jnp
from jax import lax
from jax.experimental import pallas as pl
from jax.experimental.pallas import tpu as pltpu
from jax.sharding import PartitionSpec as P

DC = 512
DR = 64
DH = 128
DV = 128
HEADS = 64
LANES = 128
BLOCKED = -1e30
EXP_SCALE = math.log2(math.e) / math.sqrt(DH + DR)
HEADS_STEP = 4
VMEM_LIMIT = 28 * 1024 * 1024
BF16 = jnp.bfloat16
F32 = jnp.float32

VMEM = pl.BlockSpec(memory_space=pltpu.VMEM)
ANYWHERE = pl.BlockSpec(memory_space=pl.ANY)


def iota(shape, dim):
    return lax.broadcasted_iota(jnp.int32, shape, dim)


def params():
    return pltpu.CompilerParams(vmem_limit_bytes=VMEM_LIMIT)


def dot(a, b):
    return jnp.dot(a, b, preferred_element_type=F32)


def dot_t(a, b):
    return lax.dot_general(a, b, (((1,), (1,)), ((), ())), preferred_element_type=F32)


def pack_kernel(rope_ref, length_ref, out_ref):
    half = rope_ref.shape[0] // 2
    out_ref[:half, :DR] = rope_ref[:half, :]
    out_ref[:half, DR:] = rope_ref[half:, :]
    tail = out_ref.shape[0] - half
    out_ref[half:, :] = jnp.full((tail, LANES), length_ref[0, 0], jnp.int32).astype(F32).astype(BF16)


def pack(rope, length):
    half = rope.shape[0] // 2
    return pl.pallas_call(
        pack_kernel,
        out_shape=jax.ShapeDtypeStruct((half + 16, LANES), BF16),
        in_specs=[VMEM, pl.BlockSpec(memory_space=pltpu.SMEM)],
        out_specs=VMEM,
        compiler_params=params(),
        name="pack_rope",
    )(rope, length)


def queries_kernel(q_hbm, r_hbm, w_hbm, lat_ref, ext_ref, q_buf, r_buf, w_buf, sems):
    heads = lat_ref.shape[0] // q_buf.shape[0]
    count = q_buf.shape[0]
    me = lax.axis_index("ctx")
    q_first = pl.multiple_of(me * (heads * DH), LANES)
    r_first = pl.multiple_of(me * (heads * DR), LANES)
    steps = heads // HEADS_STEP
    width = HEADS_STEP * DH
    q_copy = pltpu.make_async_copy(q_hbm.at[0, :, pl.ds(q_first, heads * DH)], q_buf, sems.at[0])
    r_copy = pltpu.make_async_copy(r_hbm.at[0, :, pl.ds(r_first, heads * DR)], r_buf, sems.at[1])
    q_copy.start()
    w_copies = []
    for step in range(steps):
        cols = pl.ds(step * width, width)
        copy = pltpu.make_async_copy(w_hbm.at[:, cols], w_buf.at[:, cols], sems.at[2 + step])
        copy.start()
        w_copies.append(copy)
    r_copy.start()
    q_copy.wait()
    for step in range(steps):
        w_copies[step].wait()
        for head in range(step * HEADS_STEP, (step + 1) * HEADS_STEP):
            cols = slice(head * DH, (head + 1) * DH)
            lat_ref[head * count : (head + 1) * count, :] = dot_t(q_buf[:, cols], w_buf[:, cols]).astype(BF16)
    r_copy.wait()
    lane = iota((count, LANES), 1)
    side = jnp.where(lane == DR, 1.0, 0.0)
    for pair in range(heads // 2):
        both = r_buf[:, pair * LANES : (pair + 1) * LANES].astype(F32)
        for odd in range(2):
            one = pltpu.roll(both, DR, 1) if odd else both
            head = 2 * pair + odd
            ext_ref[head * count : (head + 1) * count, :] = jnp.where(lane < DR, one, side).astype(BF16)


def make_queries(q_nope, q_rope, w_key):
    count = q_nope.shape[1]
    heads = w_key.shape[1] // DH
    rows = heads * count
    return pl.pallas_call(
        queries_kernel,
        out_shape=(pltpu.VMEM((rows, DC), BF16), pltpu.VMEM((rows, LANES), BF16)),
        in_specs=[ANYWHERE, ANYWHERE, ANYWHERE],
        out_specs=(VMEM, VMEM),
        scratch_shapes=[
            pltpu.VMEM((count, heads * DH), BF16),
            pltpu.VMEM((count, heads * DR), BF16),
            pltpu.VMEM((DC, heads * DH), BF16),
            pltpu.SemaphoreType.DMA((2 + heads // HEADS_STEP,)),
        ],
        compiler_params=params(),
        cost_estimate=pl.CostEstimate(
            flops=2 * rows * DH * DC, bytes_accessed=2 * (DC * heads * DH + rows * (DH + DR)), transcendentals=0
        ),
        name="latent_queries",
    )(q_nope, q_rope, w_key)


def masked_rope(packed, slots):
    half = slots // 2
    lane = iota((half, LANES), 1)
    row = iota((half, LANES), 0).astype(F32)
    both = packed[:half, :].astype(F32)
    live = packed[half : half + 1, :].astype(F32)
    parts = []
    for part in range(2):
        one = pltpu.roll(both, DR, 1) if part else both
        blocked = jnp.where(row + part * half < live, 0.0, BLOCKED)
        parts.append(jnp.where(lane < DR, one, jnp.where(lane == DR, blocked, 0.0)).astype(BF16))
    return jnp.concatenate(parts, axis=0)


def first_kernel(latq_ref, extq_ref, *refs, blocks, cached):
    cache_refs, pack_refs = refs[:cached], refs[cached : 2 * cached]
    fresh_refs = refs[2 * cached : 2 * cached + blocks]
    rope_refs = refs[2 * cached + blocks : 2 * cached + 2 * blocks]
    acc_ref, sum_ref, max_ref, lat_buf, ext_buf, flat_buf, fext_buf = refs[2 * cached + 2 * blocks :]
    slots = cache_refs[0].shape[0]
    part = fresh_refs[0].shape[0]
    count = part * blocks
    for k in range(cached):
        lat_buf[k * slots : (k + 1) * slots, :] = cache_refs[k][...]
        ext_buf[k * slots : (k + 1) * slots, :] = masked_rope(pack_refs[k], slots)
    for k in range(blocks):
        flat_buf[k * part : (k + 1) * part, :] = fresh_refs[k][...]
        fext_buf[k * part : (k + 1) * part, :] = jnp.concatenate(
            [rope_refs[k][...], jnp.zeros((part, LANES - DR), BF16)], axis=1
        )
    me = lax.axis_index("ctx")
    col = iota((count, count), 1)
    origin = jnp.bitwise_xor(jnp.full((count, count), me, jnp.int32), col // part)
    bias = jnp.where(origin * part + col % part <= iota((count, count), 0), 0.0, BLOCKED)
    size = HEADS_STEP * count
    bias = jnp.concatenate([bias] * HEADS_STEP, axis=0)
    for step in range(latq_ref.shape[0] // size):
        rows = slice(step * size, (step + 1) * size)
        latq, extq = latq_ref[rows, :], extq_ref[rows, :]
        s_old = dot_t(latq, lat_buf[...]) + dot_t(extq, ext_buf[...])
        s_new = dot_t(latq, flat_buf[...]) + dot_t(extq, fext_buf[...]) + bias
        level = jnp.maximum(jnp.max(s_old, axis=1, keepdims=True), jnp.max(s_new, axis=1, keepdims=True))
        p_old = jnp.exp2((s_old - level) * EXP_SCALE)
        p_new = jnp.exp2((s_new - level) * EXP_SCALE)
        total = p_new[:, :LANES]
        for k in range(1, count // LANES):
            total = total + p_new[:, k * LANES : (k + 1) * LANES]
        for k in range(cached * slots // LANES):
            total = total + p_old[:, k * LANES : (k + 1) * LANES]
        acc_ref[rows, :] = dot(p_old.astype(BF16), lat_buf[...]) + dot(p_new.astype(BF16), flat_buf[...])
        sum_ref[rows, :] = total
        max_ref[rows, :] = jnp.broadcast_to(level, (size, LANES))


def state_shapes(rows):
    return (pltpu.VMEM((rows, DC), F32), pltpu.VMEM((rows, LANES), F32), pltpu.VMEM((rows, LANES), F32))


def first_pass(lat_q, ext_q, caches, packs, fresh, ropes):
    rows = lat_q.shape[0]
    cached, blocks = len(caches), len(fresh)
    slots = caches[0].shape[0]
    count = blocks * fresh[0].shape[0]
    keys = cached * slots + count
    return pl.pallas_call(
        functools.partial(first_kernel, blocks=blocks, cached=cached),
        out_shape=state_shapes(rows),
        in_specs=[VMEM] * (2 + 2 * cached + 2 * blocks),
        out_specs=(VMEM, VMEM, VMEM),
        scratch_shapes=[
            pltpu.VMEM((cached * slots, DC), BF16),
            pltpu.VMEM((cached * slots, LANES), BF16),
            pltpu.VMEM((count, DC), BF16),
            pltpu.VMEM((count, LANES), BF16),
        ],
        compiler_params=params(),
        cost_estimate=pl.CostEstimate(
            flops=2 * rows * keys * (2 * DC + DR), bytes_accessed=2 * keys * (DC + DR), transcendentals=rows * keys
        ),
        name="near_rows",
    )(lat_q, ext_q, *caches, *packs, *fresh, *ropes)


def advance(rows, latq_ref, extq_ref, lat_ref, ext, acc_ref, sum_ref, max_ref):
    lat = lat_ref[...]
    s = dot_t(latq_ref[rows, :], lat) + dot_t(extq_ref[rows, :], ext)
    before = max_ref[rows, :]
    level = jnp.maximum(before, jnp.max(s, axis=1, keepdims=True))
    factor = jnp.exp2((before - level) * EXP_SCALE)
    total = sum_ref[rows, :] * factor
    parts = []
    for k in range(lat.shape[0] // LANES):
        p = jnp.exp2((s[:, k * LANES : (k + 1) * LANES] - level) * EXP_SCALE)
        total = total + p
        parts.append(p.astype(BF16))
    grown = dot(jnp.concatenate(parts, axis=1), lat)
    return level, total, factor, grown


def scaled(acc, factor):
    return jnp.concatenate(
        [acc[:, k * LANES : (k + 1) * LANES] * factor for k in range(acc.shape[1] // LANES)], axis=1
    )


def middle_kernel(latq_ref, extq_ref, lat_ref, pack_ref, acc_in, sum_in, max_in, acc_ref, sum_ref, max_ref, *, size):
    ext = masked_rope(pack_ref, lat_ref.shape[0])
    for step in range(latq_ref.shape[0] // size):
        rows = slice(step * size, (step + 1) * size)
        level, total, factor, grown = advance(rows, latq_ref, extq_ref, lat_ref, ext, acc_in, sum_in, max_in)
        acc_ref[rows, :] = scaled(acc_in[rows, :], factor) + grown
        sum_ref[rows, :] = total
        max_ref[rows, :] = level


def attention_cost(rows, keys, more=0):
    return pl.CostEstimate(
        flops=2 * rows * keys * (2 * DC + DR) + more,
        bytes_accessed=2 * keys * (DC + DR) + more // 128,
        transcendentals=rows * keys,
    )


def middle_pass(lat_q, ext_q, lat, packed, state, count):
    rows = lat_q.shape[0]
    return pl.pallas_call(
        functools.partial(middle_kernel, size=HEADS_STEP * count),
        out_shape=state_shapes(rows),
        in_specs=[VMEM] * 7,
        out_specs=(VMEM, VMEM, VMEM),
        input_output_aliases={4: 0, 5: 1, 6: 2},
        compiler_params=params(),
        cost_estimate=attention_cost(rows, lat.shape[0]),
        name="far_rows",
    )(lat_q, ext_q, lat, packed, *state)


def last_kernel(latq_ref, extq_ref, lat_ref, pack_ref, acc_in, sum_in, max_in, w_hbm, out_ref, w_buf, sem, *, count):
    copy = pltpu.make_async_copy(w_hbm, w_buf, sem)
    copy.start()
    ext = masked_rope(pack_ref, lat_ref.shape[0])
    size = HEADS_STEP * count
    for step in range(latq_ref.shape[0] // size):
        rows = slice(step * size, (step + 1) * size)
        level, total, factor, grown = advance(rows, latq_ref, extq_ref, lat_ref, ext, acc_in, sum_in, max_in)
        whole = jnp.sum(total, axis=1, keepdims=True)
        mixed = ((scaled(acc_in[rows, :], factor) + grown) * (1.0 / whole)).astype(BF16)
        if step == 0:
            copy.wait()
        for k in range(HEADS_STEP):
            cols = slice((step * HEADS_STEP + k) * DV, (step * HEADS_STEP + k + 1) * DV)
            out_ref[:, cols] = dot(mixed[k * count : (k + 1) * count, :], w_buf[:, cols]).astype(BF16)


def last_pass(lat_q, ext_q, lat, packed, state, w_value, count):
    rows = lat_q.shape[0]
    return pl.pallas_call(
        functools.partial(last_kernel, count=count),
        out_shape=jax.ShapeDtypeStruct((count, w_value.shape[1]), BF16),
        in_specs=[VMEM] * 7 + [ANYWHERE],
        out_specs=VMEM,
        scratch_shapes=[pltpu.VMEM(w_value.shape, BF16), pltpu.SemaphoreType.DMA],
        compiler_params=params(),
        cost_estimate=attention_cost(rows, lat.shape[0], 2 * rows * DC * DV),
        name="last_rows",
    )(lat_q, ext_q, lat, packed, *state, w_value)


def hop(array, bit):
    size = lax.axis_size("ctx")
    return lax.ppermute(array, "ctx", [(k, k ^ bit) for k in range(size)])


def shards(q_nope, q_rope, cache_latent, cache_rope, new_latent, new_rope, lengths, w_key, w_value):
    count = q_nope.shape[1]
    cache, fresh, fresh_rope = cache_latent[0], new_latent[0], new_rope[0]
    packed = pack(cache_rope[0], lengths)

    fresh_all, rope_all = [fresh], [fresh_rope]
    far_fresh, far_rope, far_cache = hop(fresh, 2), hop(fresh_rope, 2), hop(cache, 2)
    far_pack = hop(packed, 2)
    near_cache, near_pack = hop(cache, 1), hop(packed, 1)
    fresh_all = [fresh, hop(fresh, 1), far_fresh, hop(far_fresh, 1)]
    rope_all = [fresh_rope, hop(fresh_rope, 1), far_rope, hop(far_rope, 1)]
    last_cache, last_pack = hop(far_cache, 1), hop(far_pack, 1)

    lat_q, ext_q = make_queries(q_nope, q_rope, w_key)
    state = first_pass(lat_q, ext_q, [cache, near_cache], [packed, near_pack], fresh_all, rope_all)
    state = middle_pass(lat_q, ext_q, far_cache, far_pack, state, count)
    return last_pass(lat_q, ext_q, last_cache, last_pack, state, w_value, count)[None]


def solution(mesh):
    return jax.shard_map(
        shards,
        mesh=mesh,
        in_specs=(
            P("req", None, None),
            P("req", None, None),
            P("req", "ctx", None),
            P("req", "ctx", None),
            P("req", "ctx", None),
            P("req", "ctx", None),
            P("req", "ctx"),
            P(None, "ctx"),
            P(None, "ctx"),
        ),
        out_specs=P("req", None, "ctx"),
        check_vma=False,
    )
```

time: 134 us -> 37.3 us (0.28)
  matrix products: 68.5 us -> 0 us
  blocking collectives: 22.8 us -> 0 us
  between operations: 17.6 us -> 0.78 us
  Pallas kernels: 0 us -> 16.2 us
  other arithmetic: 12.7 us -> 0 us
  starting transfers between devices: 0.01 us -> 8.26 us
  waiting for transfers between devices: 0.73 us -> 6.54 us
  local copies, waits for them, and re-layouts: 9.01 us -> 5.3 us
    dot_general x100 -> x0, matrix products: 68.5 us -> none  [the longest x20 27.9 us: expand_block(): jnp.dot(lat_rows, weight_key, preferred_element_type=jnp.float32)]
    all_gather x3 -> x0, blocking collectives: 17.4 us -> none  [the longest x1 6.82 us: shards(): lax.all_gather(new_latent[0], 'ctx', axis=0, tiled=True)]
    pallas_call x0 -> x5, Pallas kernels: none -> 16.2 us  [the longest x1 4.86 us: first_pass(): pl.pallas_call(functools.partial(first_kernel, blocks=blocks, cached=cach...]
    lt x16 -> x0, other arithmetic: 10.1 us -> none  [advance(): visible = (offset + jnp.arange(BLOCK, dtype=jnp.int32))[None, :] < live_rows]
    ppermute x0 -> x12, starting transfers between devices: none -> 8.26 us  [hop(): return lax.ppermute(array, 'ctx', [(k, k ^ bit) for k in range(size)])]
    ppermute x0 -> x12, waiting for transfers between devices: none -> 6.54 us  [hop(): return lax.ppermute(array, 'ctx', [(k, k ^ bit) for k in range(size)])]
    unnamed x1 -> x0, blocking collectives: 5.32 us -> none
    unnamed x19 -> x15, local copies, waits for them, and re-layouts: 1.83 us -> 5.3 us
  transfers between devices with their start and end apart: 1 -> 12, of which waited for: 0 -> 2; matrix products, arithmetic and copies ran while one was open for 11% -> 2% of each run, Pallas kernels for 0% -> 31%
where the time goes in v1:
time: 37.3 us; the launch traced here: 37.1 us
  Pallas kernels  16.2 us (43%)
  starting transfers between devices  8.26 us (22%)
  waiting for transfers between devices  6.54 us (18%)
  local copies, waits for them, and re-layouts  5.3 us (14%)
  between operations  0.78 us (2%)
    ppermute x12, starting transfers between devices, hop(): return lax.ppermute(array, 'ctx', [(k, k ^ bit) for k in range(size)])  8.26 us
    ppermute x12, waiting for transfers between devices, hop(): return lax.ppermute(array, 'ctx', [(k, k ^ bit) for k in range(size)])  6.54 us
    unnamed x15, local copies, waits for them, and re-layouts  5.3 us
    pallas_call x1, Pallas kernels, first_pass(): pl.pallas_call(functools.partial(first_kernel, blocks=blocks, cached=cach...  4.86 us
    pallas_call x1, Pallas kernels, last_pass(): pl.pallas_call(functools.partial(last_kernel, count=count), out_shape=jax...  4.75 us
    pallas_call x1, Pallas kernels, middle_pass(): pl.pallas_call(functools.partial(middle_kernel, size=HEADS_STEP * count),...  4.5 us
    pallas_call x1, Pallas kernels, make_queries(): pl.pallas_call(queries_kernel, out_shape=(pltpu.VMEM((rows, DC), BF16), p...  2 us
  transfers between devices with their start and end apart: 12, of which 2 were waited for; matrix products, arithmetic and copies ran while one was open for 2% of the time, Pallas kernels for 31%

profile of v1, /device:TPU:0, one launch (start us, length us, event | category | flops | bytes accessed | tf_op | source)
XLA Modules:
  0.0 37.1 jit_solution(13963009119974072091)
XLA Ops:
  0.0 2.9 %collective-permute-start = (bf16[256,512]{1,0:T(8,128)(2,1)}, bf16[256,512]{1,0:T(8,128)(2,1)S(1)}, u32[]{:S(2)}, u32[]{:S(2)}) collective-permute-start(bf16[256,512]{1,0:T(8,128)(2,1)} %bitcast.6), channel_id=1, source_target_pairs={{0,2},{1,3},{2,0},{3,1},{4,6},{5,7},{6,4},{7,5},{8,10},{9,11},{10,... | collective-permute-start | bytes 786440 | tf_op jit(solution)/shard_map/ppermute | solution.py:292
  2.9 0.0 collective-permute-start.4
  2.9 0.1 collective-permute-start.7
  3.0 0.4 %collective-permute-start.6 = (bf16[32,512]{1,0:T(8,128)(2,1)}, bf16[32,512]{1,0:T(8,128)(2,1)S(1)}, u32[]{:S(2)}, u32[]{:S(2)}) collective-permute-start(bf16[32,512]{1,0:T(8,128)(2,1)} %bitcast.10), channel_id=1, source_target_pairs={{0,1},{1,0},{2,3},{3,2},{4,5},{5,4},{6,7},{7,6},{8,9},{9,8},{10,11... | collective-permute-start | bytes 98312 | tf_op jit(solution)/shard_map/ppermute | solution.py:292
  3.5 1.7 %collective-permute-start.10 = (bf16[32,64]{1,0:T(8,128)(2,1)}, bf16[32,64]{1,0:T(8,128)(2,1)S(1)}, u32[]{:S(2)}, u32[]{:S(2)}) collective-permute-start(bf16[32,64]{1,0:T(8,128)(2,1)} %bitcast.12), channel_id=1, source_target_pairs={{0,2},{1,3},{2,0},{3,1},{4,6},{5,7},{6,4},{7,5},{8,10},{9,11},{10,... | collective-permute-start | bytes 12296 | tf_op jit(solution)/shard_map/ppermute | solution.py:292
  5.2 5.1 %collective-permute-done.10.refs_10_ = bf16[32,64]{1,0:T(8,128)(2,1)S(1)} collective-permute-done((bf16[32,64]{1,0:T(8,128)(2,1)}, bf16[32,64]{1,0:T(8,128)(2,1)S(1)}, u32[]{:S(2)}, u32[]{:S(2)}) %collective-permute-start.10) | collective-permute-done | bytes 4128 | tf_op jit(solution)/shard_map/ppermute | solution.py:292
  10.3 0.0 collective-permute-start.9
  10.3 1.4 %collective-permute-done.9.refs_9_ = bf16[32,64]{1,0:T(8,128)(2,1)S(1)} collective-permute-done((bf16[32,64]{1,0:T(8,128)(2,1)}, bf16[32,64]{1,0:T(8,128)(2,1)S(1)}, u32[]{:S(2)}, u32[]{:S(2)}) %collective-permute-start.9) | collective-permute-done | bytes 4128 | tf_op jit(solution)/shard_map/ppermute | solution.py:292
  11.7 0.2 collective-permute-start.11
  11.9 0.9 %copy.13 = bf16[1,256,64]{2,1,0:T(8,128)(2,1)S(1)} copy(bf16[1,256,64]{1,2,0:T(8,128)(2,1)} %param.12) | data formatting | bytes 65536 | tf_op args[3]
  13.4 0.0 copy-start.5
  13.4 0.0 copy-start.6
  13.4 0.1 pack_rope.1.refs_2_
  13.5 0.0 collective-permute-done.11.refs_11_
  13.5 1.8 %collective-permute-start.2 = (bf16[144,128]{1,0:T(8,128)(2,1)S(1)}, bf16[144,128]{1,0:T(8,128)(2,1)S(1)}, u32[]{:S(2)}, u32[]{:S(2)}) collective-permute-start(bf16[144,128]{1,0:T(8,128)(2,1)S(1)} %pack_rope.1.refs_2_), channel_id=1, source_target_pairs={{0,2},{1,3},{2,0},{3,1},{4,6},{5,7},{6,4},{7,5},{8,10},{9,11},{10,... | collective-permute-start | bytes 110600 | tf_op jit(solution)/shard_map/ppermute | solution.py:292
  15.3 0.0 collective-permute-done.7.refs_6_
  15.3 0.1 collective-permute-start.5
  15.4 0.0 collective-permute-done.6.refs_5_
  15.4 0.4 %collective-permute-start.8 = (bf16[32,512]{1,0:T(8,128)(2,1)S(1)}, bf16[32,512]{1,0:T(8,128)(2,1)S(1)}, u32[]{:S(2)}, u32[]{:S(2)}) collective-permute-start(bf16[32,512]{1,0:T(8,128)(2,1)S(1)} %collective-permute-done.7.refs_6_), channel_id=1, source_target_pairs={{0,1},{1,0},{2,3},{3,2},{4,5},{5,4},{6,7},{7,6},{8,9},{9,8},{10,11... | collective-permute-start | bytes 98312 | tf_op jit(solution)/shard_map/ppermute | solution.py:292
  15.8 0.0 copy-start
  15.9 1.6 %copy-done = bf16[1,128,8192]{2,1,0:T(8,128)(2,1)S(1)} copy-done((bf16[1,128,8192]{2,1,0:T(8,128)(2,1)S(1)}, bf16[1,128,8192]{2,1,0:T(8,128)(2,1)}, u32[]{:S(2)}) %copy-start) | copy-done | bytes 2097176
  17.4 0.0 copy-start.1
  17.4 1.6 %copy-done.1 = bf16[512,2048]{1,0:T(8,128)(2,1)S(1)} copy-done((bf16[512,2048]{1,0:T(8,128)(2,1)S(1)}, bf16[512,2048]{1,0:T(8,128)(2,1)}, u32[]{:S(2)}) %copy-start.1) | copy-done | bytes 2097176
  19.0 0.0 copy-start.3
  19.0 1.2 %copy-done.3 = bf16[1,128,4096]{2,1,0:T(8,128)(2,1)S(1)} copy-done((bf16[1,128,4096]{2,1,0:T(8,128)(2,1)S(1)}, bf16[1,128,4096]{2,1,0:T(8,128)(2,1)}, u32[]{:S(2)}) %copy-start.3) | copy-done | bytes 1048600
  20.3 0.0 copy-start.4
  20.3 2.0 %latent_queries.1 = (bf16[2048,512]{1,0:T(8,128)(2,1)S(1)}, bf16[2048,128]{1,0:T(8,128)(2,1)S(1)}) custom-call(bf16[1,128,8192]{2,1,0:T(8,128)(2,1)S(1)} %copy-done, bf16[1,128,4096]{2,1,0:T(8,128)(2,1)S(1)} %copy-done.3, bf16[512,2048]{1,0:T(8,128)(2,1)S(1)} %copy-done.1), custom_call_target="tpu_custom_call" | custom-call | flops 268435456 | bytes 2883584 | tf_op jit(solution)/shard_map/latent_queries/pallas_call | solution.py:103
  22.3 0.0 collective-permute-done.2.pack_ref
  22.3 0.1 collective-permute-start.3
  22.4 0.0 collective-permute-done.lat_ref
  22.4 0.4 %collective-permute-start.1 = (bf16[256,512]{1,0:T(8,128)(2,1)S(1)}, bf16[256,512]{1,0:T(8,128)(2,1)S(1)}, u32[]{:S(2)}, u32[]{:S(2)}) collective-permute-start(bf16[256,512]{1,0:T(8,128)(2,1)S(1)} %collective-permute-done.lat_ref), channel_id=1, source_target_pairs={{0,1},{1,0},{2,3},{3,2},{4,5},{5,4},{6,7},{7,6},{8,9},{9,8},{10,11... | collective-permute-start | bytes 786440 | tf_op jit(solution)/shard_map/ppermute | solution.py:292
  22.9 0.0 collective-permute-done.5.refs_3_
  22.9 0.0 collective-permute-done.8.refs_7_
  22.9 0.0 collective-permute-done.4.refs_1_
  22.9 0.0 copy-done.5
  22.9 0.0 copy-done.6
  22.9 0.0 copy-done.4
  22.9 4.9 %near_rows.1 = (f32[2048,512]{1,0:T(8,128)S(1)}, f32[2048,128]{1,0:T(8,128)S(1)}, f32[2048,128]{1,0:T(8,128)S(1)}) custom-call(bf16[2048,512]{1,0:T(8,128)(2,1)S(1)} %get-tuple-element.13.latq_ref, bf16[2048,128]{1,0:T(8,128)(2,1)S(1)} %get-tuple-element.14.extq_ref, bf16[256,512]{1,0:T(8,128)(2,1)S(1)} %bitcast.8, ...), custom_call_target="tpu_custom_call" | custom-call | flops 2852126720 | bytes 737280 | tf_op jit(solution)/shard_map/near_rows/pallas_call | solution.py:186
  27.8 0.0 copy-start.2
  27.8 4.5 %far_rows.1 = (f32[2048,512]{1,0:T(8,128)S(1)}, f32[2048,128]{1,0:T(8,128)S(1)}, f32[2048,128]{1,0:T(8,128)S(1)}) custom-call(bf16[2048,512]{1,0:T(8,128)(2,1)S(1)} %get-tuple-element.13.latq_ref, bf16[2048,128]{1,0:T(8,128)(2,1)S(1)} %get-tuple-element.14.extq_ref, ...), custom_call_target="tpu_custom_call", output_to_operand_aliasing={{0}: (4, {}), {1}: (5, {}), {2}: (6, {})} | custom-call | flops 1140850688 | bytes 294912 | tf_op jit(solution)/shard_map/far_rows/pallas_call | solution.py:247
  32.3 0.0 collective-permute-done.3.pack_ref
  32.3 0.0 collective-permute-done.1.lat_ref
  32.3 0.0 copy-done.2
  32.3 4.8 %last_rows.1 = bf16[128,2048]{1,0:T(8,128)(2,1)} custom-call(bf16[2048,512]{1,0:T(8,128)(2,1)S(1)} %get-tuple-element.13.latq_ref, bf16[2048,128]{1,0:T(8,128)(2,1)S(1)} %get-tuple-element.14.extq_ref, bf16[256,512]{1,0:T(8,128)(2,1)S(1)} %collective-permute-done.1.lat_ref, bf16[144,128]{1,0:T(8,128)(2,1)S(1)} %collective-permute-done.3.pack_ref, ...), custom_call_target="tpu_custom_call" | custom-call | flops 1409286144 | bytes 2392064 | tf_op jit(solution)/shard_map/last_rows/pallas_call | solution.py:278
Async XLA Ops:
  0.0 22.4 %collective-permute-start = (bf16[256,512]{1,0:T(8,128)(2,1)}, bf16[256,512]{1,0:T(8,128)(2,1)S(1)}, u32[]{:S(2)}, u32[]{:S(2)}) collective-permute-start(bf16[256,512]{1,0:T(8,128)(2,1)} %bitcast.6), channel_id=1, source_target_pairs={{0,2},{1,3},{2,0},{3,1},{4,6},{5,7},{6,4},{7,5},{8,10},{9,11},{10,... | collective-permute-start | bytes 786440 | tf_op jit(solution)/shard_map/ppermute | solution.py:292
  2.9 19.9 %collective-permute-start.4 = (bf16[256,512]{1,0:T(8,128)(2,1)}, bf16[256,512]{1,0:T(8,128)(2,1)S(1)}, u32[]{:S(2)}, u32[]{:S(2)}) collective-permute-start(bf16[256,512]{1,0:T(8,128)(2,1)} %bitcast.7), channel_id=1, source_target_pairs={{0,1},{1,0},{2,3},{3,2},{4,5},{5,4},{6,7},{7,6},{8,9},{9,8},{10,11... | collective-permute-start | bytes 786440 | tf_op jit(solution)/shard_map/ppermute | solution.py:292
  2.9 12.4 %collective-permute-start.7 = (bf16[32,512]{1,0:T(8,128)(2,1)}, bf16[32,512]{1,0:T(8,128)(2,1)S(1)}, u32[]{:S(2)}, u32[]{:S(2)}) collective-permute-start(bf16[32,512]{1,0:T(8,128)(2,1)} %bitcast.9), channel_id=1, source_target_pairs={{0,2},{1,3},{2,0},{3,1},{4,6},{5,7},{6,4},{7,5},{8,10},{9,11},{10,... | collective-permute-start | bytes 98312 | tf_op jit(solution)/shard_map/ppermute | solution.py:292
  3.0 12.4 %collective-permute-start.6 = (bf16[32,512]{1,0:T(8,128)(2,1)}, bf16[32,512]{1,0:T(8,128)(2,1)S(1)}, u32[]{:S(2)}, u32[]{:S(2)}) collective-permute-start(bf16[32,512]{1,0:T(8,128)(2,1)} %bitcast.10), channel_id=1, source_target_pairs={{0,1},{1,0},{2,3},{3,2},{4,5},{5,4},{6,7},{7,6},{8,9},{9,8},{10,11... | collective-permute-start | bytes 98312 | tf_op jit(solution)/shard_map/ppermute | solution.py:292
  3.5 6.9 %collective-permute-start.10 = (bf16[32,64]{1,0:T(8,128)(2,1)}, bf16[32,64]{1,0:T(8,128)(2,1)S(1)}, u32[]{:S(2)}, u32[]{:S(2)}) collective-permute-start(bf16[32,64]{1,0:T(8,128)(2,1)} %bitcast.12), channel_id=1, source_target_pairs={{0,2},{1,3},{2,0},{3,1},{4,6},{5,7},{6,4},{7,5},{8,10},{9,11},{10,... | collective-permute-start | bytes 12296 | tf_op jit(solution)/shard_map/ppermute | solution.py:292
  10.3 1.4 %collective-permute-start.9 = (bf16[32,64]{1,0:T(8,128)(2,1)}, bf16[32,64]{1,0:T(8,128)(2,1)S(1)}, u32[]{:S(2)}, u32[]{:S(2)}) collective-permute-start(bf16[32,64]{1,0:T(8,128)(2,1)} %bitcast.13), channel_id=1, source_target_pairs={{0,1},{1,0},{2,3},{3,2},{4,5},{5,4},{6,7},{7,6},{8,9},{9,8},{10,11... | collective-permute-start | bytes 12296 | tf_op jit(solution)/shard_map/ppermute | solution.py:292
  11.7 1.8 %collective-permute-start.11 = (bf16[32,64]{1,0:T(8,128)(2,1)S(1)}, bf16[32,64]{1,0:T(8,128)(2,1)S(1)}, u32[]{:S(2)}, u32[]{:S(2)}) collective-permute-start(bf16[32,64]{1,0:T(8,128)(2,1)S(1)} %collective-permute-done.10.refs_10_), channel_id=1, source_target_pairs={{0,1},{1,0},{2,3},{3,2},{4,5},{5,4},{6,7},{7,6},{8,9},{9,8},{10,11... | collective-permute-start | bytes 12296 | tf_op jit(solution)/shard_map/ppermute | solution.py:292
  13.4 9.5 %copy-start.5 = (bf16[1,32,512]{2,1,0:T(8,128)(2,1)S(1)}, bf16[1,32,512]{2,1,0:T(8,128)(2,1)}, u32[]{:S(2)}) copy-start(bf16[1,32,512]{2,1,0:T(8,128)(2,1)} %param.13) | copy-start | bytes 98308
  13.4 9.5 %copy-start.6 = (bf16[1,32,64]{2,1,0:T(8,128)(2,1)S(1)}, bf16[1,32,64]{2,1,0:T(8,128)(2,1)}, u32[]{:S(2)}) copy-start(bf16[1,32,64]{2,1,0:T(8,128)(2,1)} %param.14) | copy-start | bytes 12292
  13.5 8.7 %collective-permute-start.2 = (bf16[144,128]{1,0:T(8,128)(2,1)S(1)}, bf16[144,128]{1,0:T(8,128)(2,1)S(1)}, u32[]{:S(2)}, u32[]{:S(2)}) collective-permute-start(bf16[144,128]{1,0:T(8,128)(2,1)S(1)} %pack_rope.1.refs_2_), channel_id=1, source_target_pairs={{0,2},{1,3},{2,0},{3,1},{4,6},{5,7},{6,4},{7,5},{8,10},{9,11},{10,... | collective-permute-start | bytes 110600 | tf_op jit(solution)/shard_map/ppermute | solution.py:292
  15.3 7.5 %collective-permute-start.5 = (bf16[144,128]{1,0:T(8,128)(2,1)S(1)}, bf16[144,128]{1,0:T(8,128)(2,1)S(1)}, u32[]{:S(2)}, u32[]{:S(2)}) collective-permute-start(bf16[144,128]{1,0:T(8,128)(2,1)S(1)} %pack_rope.1.refs_2_), channel_id=1, source_target_pairs={{0,1},{1,0},{2,3},{3,2},{4,5},{5,4},{6,7},{7,6},{8,9},{9,8},{10,11... | collective-permute-start | bytes 110600 | tf_op jit(solution)/shard_map/ppermute | solution.py:292
  15.4 7.5 %collective-permute-start.8 = (bf16[32,512]{1,0:T(8,128)(2,1)S(1)}, bf16[32,512]{1,0:T(8,128)(2,1)S(1)}, u32[]{:S(2)}, u32[]{:S(2)}) collective-permute-start(bf16[32,512]{1,0:T(8,128)(2,1)S(1)} %collective-permute-done.7.refs_6_), channel_id=1, source_target_pairs={{0,1},{1,0},{2,3},{3,2},{4,5},{5,4},{6,7},{7,6},{8,9},{9,8},{10,11... | collective-permute-start | bytes 98312 | tf_op jit(solution)/shard_map/ppermute | solution.py:292
  15.8 1.6 %copy-start = (bf16[1,128,8192]{2,1,0:T(8,128)(2,1)S(1)}, bf16[1,128,8192]{2,1,0:T(8,128)(2,1)}, u32[]{:S(2)}) copy-start(bf16[1,128,8192]{2,1,0:T(8,128)(2,1)} %q_hbm.1) | copy-start | bytes 6291460
  17.4 1.6 %copy-start.1 = (bf16[512,2048]{1,0:T(8,128)(2,1)S(1)}, bf16[512,2048]{1,0:T(8,128)(2,1)}, u32[]{:S(2)}) copy-start(bf16[512,2048]{1,0:T(8,128)(2,1)} %w_hbm.2) | copy-start | bytes 6291460
  19.0 1.2 %copy-start.3 = (bf16[1,128,4096]{2,1,0:T(8,128)(2,1)S(1)}, bf16[1,128,4096]{2,1,0:T(8,128)(2,1)}, u32[]{:S(2)}) copy-start(bf16[1,128,4096]{2,1,0:T(8,128)(2,1)} %r_hbm.1) | copy-start | bytes 3145732
  20.3 2.6 %copy-start.4 = (bf16[1,256,512]{2,1,0:T(8,128)(2,1)S(1)}, bf16[1,256,512]{2,1,0:T(8,128)(2,1)}, u32[]{:S(2)}) copy-start(bf16[1,256,512]{2,1,0:T(8,128)(2,1)} %param.11) | copy-start | bytes 786436
  22.3 10.0 %collective-permute-start.3 = (bf16[144,128]{1,0:T(8,128)(2,1)S(1)}, bf16[144,128]{1,0:T(8,128)(2,1)S(1)}, u32[]{:S(2)}, u32[]{:S(2)}) collective-permute-start(bf16[144,128]{1,0:T(8,128)(2,1)S(1)} %collective-permute-done.2.pack_ref), channel_id=1, source_target_pairs={{0,1},{1,0},{2,3},{3,2},{4,5},{5,4},{6,7},{7,6},{8,9},{9,8},{10,11... | collective-permute-start | bytes 110600 | tf_op jit(solution)/shard_map/ppermute | solution.py:292
  22.4 9.9 %collective-permute-start.1 = (bf16[256,512]{1,0:T(8,128)(2,1)S(1)}, bf16[256,512]{1,0:T(8,128)(2,1)S(1)}, u32[]{:S(2)}, u32[]{:S(2)}) collective-permute-start(bf16[256,512]{1,0:T(8,128)(2,1)S(1)} %collective-permute-done.lat_ref), channel_id=1, source_target_pairs={{0,1},{1,0},{2,3},{3,2},{4,5},{5,4},{6,7},{7,6},{8,9},{9,8},{10,11... | collective-permute-start | bytes 786440 | tf_op jit(solution)/shard_map/ppermute | solution.py:292
  27.8 4.5 %copy-start.2 = (bf16[512,2048]{1,0:T(8,128)(2,1)S(1)}, bf16[512,2048]{1,0:T(8,128)(2,1)}, u32[]{:S(2)}) copy-start(bf16[512,2048]{1,0:T(8,128)(2,1)} %w_hbm.3) | copy-start | bytes 6291460

commit v2 on v0

v2 whole, which is shorter than its diff:
```python
import functools
import math

import jax
import jax.numpy as jnp
from jax import lax
from jax.experimental import pallas as pl
from jax.experimental.pallas import tpu as pltpu
from jax.sharding import PartitionSpec as P

DC = 512
DR = 64
DH = 128
DV = 128
LANES = 128
KEY = DC + LANES
BLOCKED = -1e30
EXP_SCALE = math.log2(math.e) / math.sqrt(DH + DR)
HEADS_STEP = 4
GROUP = 16
COSTS = {"pack": 0.001, "latent_queries": 0.001, "pass_on": 0.001, "near_rows": 1.0, "far_rows": 3.0, "last_rows": 0.001}
VMEM_LIMIT = 20 * 1024 * 1024


def cost(micros):
    return pl.CostEstimate(flops=int(micros * 1e9), bytes_accessed=1024, transcendentals=0)


BF16 = jnp.bfloat16
F32 = jnp.float32

VMEM = pl.BlockSpec(memory_space=pltpu.VMEM)
HBM = pl.BlockSpec(memory_space=pltpu.HBM)
ANYWHERE = pl.BlockSpec(memory_space=pl.ANY)


def iota(shape, dim):
    return lax.broadcasted_iota(jnp.int32, shape, dim)


def params():
    return pltpu.CompilerParams(vmem_limit_bytes=VMEM_LIMIT)


def in_vmem(array):
    return pltpu.with_memory_space_constraint(array, pltpu.VMEM)


def dot(a, b):
    return jnp.dot(a, b, preferred_element_type=F32)


def dot_t(a, b):
    return lax.dot_general(a, b, (((1,), (1,)), ((), ())), preferred_element_type=F32)


def in_hbm(array):
    return pltpu.with_memory_space_constraint(array, pltpu.HBM)


def pack_kernel(fresh_hbm, rope_hbm, cached_hbm, length_ref, note_ref, rope_buf, cached_buf, sems):
    part = fresh_hbm.shape[0]
    slots = cached_hbm.shape[1]
    copies = [
        pltpu.make_async_copy(fresh_hbm, note_ref.at[:part, :], sems.at[0]),
        pltpu.make_async_copy(rope_hbm, rope_buf, sems.at[1]),
        pltpu.make_async_copy(cached_hbm, cached_buf, sems.at[2]),
    ]
    for copy in copies:
        copy.start()
    note_ref[part : part + GROUP, :] = jnp.zeros((GROUP, DC), BF16)
    groups = part // GROUP
    live = jnp.broadcast_to(length_ref[...], (GROUP, LANES)).astype(F32).astype(BF16)
    note_ref[part : part + GROUP, groups * LANES : (groups + 1) * LANES] = live
    copies[1].wait()
    for k in range(groups):
        note_ref[part : part + GROUP, k * LANES : k * LANES + DR] = rope_buf[k * GROUP : (k + 1) * GROUP, :]
    copies[2].wait()
    note_ref[part + GROUP :, :slots] = cached_buf[: DR // 2, :]
    note_ref[part + GROUP :, slots:] = cached_buf[DR // 2 :, :]
    copies[0].wait()


def pack(fresh, rope, cached_rope, length):
    part = fresh.shape[0]
    return pl.pallas_call(
        pack_kernel,
        out_shape=pltpu.VMEM((part + GROUP + DR // 2, DC), BF16),
        in_specs=[HBM, HBM, HBM, VMEM],
        out_specs=VMEM,
        scratch_shapes=[
            pltpu.VMEM(rope.shape, BF16),
            pltpu.VMEM(cached_rope.shape, BF16),
            pltpu.SemaphoreType.DMA((3,)),
        ],
        compiler_params=params(),
        cost_estimate=cost(COSTS["pack"]),
        name="pack",
    )(in_hbm(fresh), in_hbm(rope), in_hbm(cached_rope), length)


def queries_kernel(q_hbm, r_hbm, w_hbm, out_ref, q_buf, r_buf, w_buf, sems):
    count = q_buf.shape[0]
    heads = out_ref.shape[0] // count
    me = lax.axis_index("ctx")
    q_first = pl.multiple_of(me * (heads * DH), LANES)
    r_first = pl.multiple_of(me * (heads * DR), LANES)
    q_copy = pltpu.make_async_copy(q_hbm.at[0, :, pl.ds(q_first, heads * DH)], q_buf, sems.at[0])
    r_copy = pltpu.make_async_copy(r_hbm.at[0, :, pl.ds(r_first, heads * DR)], r_buf, sems.at[1])
    q_copy.start()
    width = HEADS_STEP * DH
    w_copies = []
    for step in range(heads // HEADS_STEP):
        cols = pl.ds(step * width, width)
        w_copies.append(pltpu.make_async_copy(w_hbm.at[:, cols], w_buf.at[:, cols], sems.at[2 + step]))
        w_copies[-1].start()
    r_copy.start()
    q_copy.wait()
    for head in range(heads):
        if head % HEADS_STEP == 0:
            w_copies[head // HEADS_STEP].wait()
        cols = slice(head * DH, (head + 1) * DH)
        out_ref[head * count : (head + 1) * count, :DC] = dot_t(q_buf[:, cols], w_buf[:, cols]).astype(BF16)
    r_copy.wait()
    lane = iota((count, LANES), 1)
    side = jnp.where(lane == DR, 1.0, 0.0)
    for pair in range(heads // 2):
        both = r_buf[:, pair * LANES : (pair + 1) * LANES].astype(F32)
        for odd in range(2):
            one = pltpu.roll(both, DR, 1) if odd else both
            head = 2 * pair + odd
            out_ref[head * count : (head + 1) * count, DC:] = jnp.where(lane < DR, one, side).astype(BF16)


def make_queries(q_nope, q_rope, w_key):
    count = q_nope.shape[1]
    heads = w_key.shape[1] // DH
    rows = heads * count
    return pl.pallas_call(
        queries_kernel,
        out_shape=pltpu.VMEM((rows, KEY), BF16),
        in_specs=[HBM, HBM, HBM],
        out_specs=VMEM,
        scratch_shapes=[
            pltpu.VMEM((count, heads * DH), BF16),
            pltpu.VMEM((count, heads * DR), BF16),
            pltpu.VMEM(w_key.shape, BF16),
            pltpu.SemaphoreType.DMA((2 + heads // HEADS_STEP,)),
        ],
        compiler_params=params(),
        cost_estimate=cost(COSTS["latent_queries"]),
        name="latent_queries",
    )(in_hbm(q_nope), in_hbm(q_rope), in_hbm(w_key))


def pass_kernel(array_ref, token_ref, out_ref):
    out_ref[...] = array_ref[...]


def after(array, token):
    return pl.pallas_call(
        pass_kernel,
        out_shape=pltpu.VMEM(array.shape, BF16),
        in_specs=[VMEM, ANYWHERE],
        out_specs=VMEM,
        compiler_params=params(),
        cost_estimate=cost(COSTS["pass_on"]),
        name="pass_on",
    )(array, token)


def put_cached(key_buf, first, lat_ref, note_ref):
    slots = lat_ref.shape[0]
    part = note_ref.shape[0] - GROUP - DR // 2
    lane = part // GROUP * LANES
    live = note_ref[part : part + 1, lane : lane + 1].astype(F32)
    blocked = jnp.where(iota((LANES - DR, slots), 1).astype(F32) < live, 0.0, BLOCKED)
    blocked = jnp.where(iota((LANES - DR, slots), 0) == 0, blocked, 0.0)
    rope = note_ref[part + GROUP :, :].astype(F32)
    both = jnp.concatenate([rope[:, :slots], rope[:, slots:], blocked], axis=0)
    key_buf[first : first + slots, :DC] = lat_ref[...]
    key_buf[first : first + slots, DC:] = both.T.astype(BF16)


def put_fresh(key_buf, first, note_refs):
    part = note_refs[0].shape[0] - GROUP - DR // 2
    for index, note_ref in enumerate(note_refs):
        key_buf[first + index * part : first + (index + 1) * part, :DC] = note_ref[:part, :]
        for k in range(part // GROUP):
            rows = span(k, GROUP, first + index * part)
            key_buf[rows, DC:] = note_ref[part : part + GROUP, k * LANES : (k + 1) * LANES]


def causal(part, blocks):
    count = part * blocks
    me = lax.axis_index("ctx")
    col = iota((count, count), 1)
    origin = jnp.bitwise_xor(jnp.full((count, count), me, jnp.int32), col // part)
    return jnp.where(origin * part + col % part <= iota((count, count), 0), 0.0, BLOCKED)


def pipeline(steps, scores, weigh, collect):
    upcoming, previous = scores(0), None
    for step in range(steps):
        now = upcoming
        if step + 1 < steps:
            upcoming = scores(step + 1)
        if previous is not None:
            collect(step - 1, *previous)
        previous = weigh(step, now)
    collect(steps - 1, *previous)


def exponents(s, level, total):
    parts = []
    for k in range(s.shape[1] // LANES):
        p = jnp.exp2((s[:, k * LANES : (k + 1) * LANES] - level) * EXP_SCALE)
        total = p if total is None else total + p
        parts.append(p.astype(BF16))
    return jnp.concatenate(parts, axis=1), total


def span(step, size, first=0):
    return slice(first + step * size, first + (step + 1) * size)


def state_shapes(rows):
    return (pltpu.VMEM((rows, DC), F32), pltpu.VMEM((rows, LANES), F32), pltpu.VMEM((rows, LANES), F32))


def near_kernel(q_ref, *refs, cached, size):
    acc_ref, sum_ref, max_ref, key_buf = refs[2 * cached :]
    slots = refs[0].shape[0]
    for k in range(cached):
        put_cached(key_buf, k * slots, refs[2 * k], refs[2 * k + 1])

    def scores(step):
        return dot_t(q_ref[span(step, size), :], key_buf[...])

    def weigh(step, s):
        level = jnp.max(s, axis=1, keepdims=True)
        p, total = exponents(s, level, None)
        sum_ref[span(step, size), :] = total
        max_ref[span(step, size), :] = jnp.broadcast_to(level, (size, LANES))
        return (p,)

    def collect(step, p):
        acc_ref[span(step, size), :] = dot(p, key_buf[:, :DC])

    pipeline(q_ref.shape[0] // size, scores, weigh, collect)


def near_pass(q, blocks, count):
    rows = q.shape[0]
    keys = sum(block[0].shape[0] for block in blocks)
    return pl.pallas_call(
        functools.partial(near_kernel, cached=len(blocks), size=HEADS_STEP * count),
        out_shape=state_shapes(rows),
        in_specs=[VMEM] * (1 + 2 * len(blocks)),
        out_specs=(VMEM, VMEM, VMEM),
        scratch_shapes=[pltpu.VMEM((keys, KEY), BF16)],
        compiler_params=params(),
        cost_estimate=cost(COSTS["near_rows"]),
        name="near_rows",
    )(q, *[array for block in blocks for array in block])


def advance(q_ref, key_buf, state_in, state_out, size):
    acc_in, sum_in, max_in = state_in
    acc_ref, sum_ref, max_ref = state_out

    def scores(step):
        return dot_t(q_ref[span(step, size), :], key_buf[...])

    def weigh(step, s):
        rows = span(step, size)
        before = max_in[rows, :]
        level = jnp.maximum(before, jnp.max(s, axis=1, keepdims=True))
        factor = jnp.exp2((before - level) * EXP_SCALE)
        p, total = exponents(s, level, sum_in[rows, :] * factor)
        sum_ref[rows, :] = total
        max_ref[rows, :] = level
        return p, factor

    def collect(step, p, factor):
        rows = span(step, size)
        grown = dot(p, key_buf[:, :DC])
        for k in range(DC // LANES):
            cols = slice(k * LANES, (k + 1) * LANES)
            acc_ref[rows, cols] = acc_in[rows, cols] * factor + grown[:, cols]

    pipeline(q_ref.shape[0] // size, scores, weigh, collect)


def far_kernel(q_ref, lat_ref, note_ref, *refs, size):
    put_cached(refs[6], 0, lat_ref, note_ref)
    advance(q_ref, refs[6], refs[:3], refs[3:6], size)


def far_pass(q, lat, note, state, count):
    rows = q.shape[0]
    return pl.pallas_call(
        functools.partial(far_kernel, size=HEADS_STEP * count),
        out_shape=state_shapes(rows),
        in_specs=[VMEM] * 6,
        out_specs=(VMEM, VMEM, VMEM),
        scratch_shapes=[pltpu.VMEM((lat.shape[0], KEY), BF16)],
        compiler_params=params(),
        cost_estimate=cost(COSTS["far_rows"]),
        name="far_rows",
    )(q, lat, note, *state)


def last_kernel(q_ref, lat_ref, *refs, blocks, size):
    notes, refs = refs[:blocks], refs[blocks:]
    acc_in, sum_in, max_in, w_ref, out_ref, key_buf = refs
    slots = lat_ref.shape[0]
    count = out_ref.shape[0]
    put_cached(key_buf, 0, lat_ref, notes[-1])
    put_fresh(key_buf, slots, notes)
    bias = jnp.concatenate([causal(count // blocks, blocks)] * HEADS_STEP, axis=0)

    def scores(step):
        return dot_t(q_ref[span(step, size), :], key_buf[...])

    def weigh(step, s):
        rows = span(step, size)
        s = jnp.concatenate([s[:, :slots], s[:, slots:] + bias], axis=1)
        before = max_in[rows, :]
        level = jnp.maximum(before, jnp.max(s, axis=1, keepdims=True))
        factor = jnp.exp2((before - level) * EXP_SCALE)
        p, total = exponents(s, level, sum_in[rows, :] * factor)
        inverse = 1.0 / jnp.sum(total, axis=1, keepdims=True)
        return p, factor * inverse, inverse

    def collect(step, p, factor, inverse):
        rows = span(step, size)
        grown = dot(p, key_buf[:, :DC])
        mixed = []
        for k in range(DC // LANES):
            cols = slice(k * LANES, (k + 1) * LANES)
            mixed.append((acc_in[rows, cols] * factor + grown[:, cols] * inverse).astype(BF16))
        mixed = jnp.concatenate(mixed, axis=1)
        for k in range(HEADS_STEP):
            cols = span(step * HEADS_STEP + k, DV)
            out_ref[:, cols] = dot(mixed[span(k, count), :], w_ref[:, cols]).astype(BF16)

    pipeline(q_ref.shape[0] // size, scores, weigh, collect)


def last_pass(q, lat, notes, state, w_value, count):
    rows = q.shape[0]
    return pl.pallas_call(
        functools.partial(last_kernel, blocks=len(notes), size=HEADS_STEP * count),
        out_shape=jax.ShapeDtypeStruct((count, w_value.shape[1]), BF16),
        in_specs=[VMEM] * (6 + len(notes)),
        out_specs=VMEM,
        scratch_shapes=[pltpu.VMEM((lat.shape[0] + count, KEY), BF16)],
        compiler_params=params(),
        cost_estimate=cost(COSTS["last_rows"]),
        name="last_rows",
    )(q, lat, *notes, *state, in_vmem(w_value))


def hop(array, bit):
    size = lax.axis_size("ctx")
    return lax.ppermute(array, "ctx", [(k, k ^ bit) for k in range(size)])


def shards(q_nope, q_rope, cache_latent, cache_rope, new_latent, new_rope, lengths, w_key, w_value):
    count = q_nope.shape[1]
    lat = cache_latent[0]
    far_lat, near_lat = hop(lat, 2), hop(lat, 1)
    note = pack(new_latent[0], new_rope[0], cache_rope[0].T, lengths)
    near_note = hop(note, 1)
    q = make_queries(q_nope, q_rope, w_key)
    far_note = hop(after(note, q), 2)
    state = near_pass(q, [(lat, note), (near_lat, near_note)], count)
    last_lat = hop(after(far_lat, state[2]), 1)
    last_note = hop(after(far_note, state[2]), 1)
    state = far_pass(q, far_lat, far_note, state, count)
    return last_pass(q, last_lat, [note, near_note, far_note, last_note], state, w_value, count)[None]


def solution(mesh):
    return jax.shard_map(
        shards,
        mesh=mesh,
        in_specs=(
            P("req", None, None),
            P("req", None, None),
            P("req", "ctx", None),
            P("req", "ctx", None),
            P("req", "ctx", None),
            P("req", "ctx", None),
            P("req", "ctx"),
            P(None, "ctx"),
            P(None, "ctx"),
        ),
        out_specs=P("req", None, "ctx"),
        check_vma=False,
    )
```

time: 134 us -> 19.3 us (0.14)
  matrix products: 68.5 us -> 0 us
  blocking collectives: 22.8 us -> 0 us
  between operations: 17.6 us -> 0.74 us
  Pallas kernels: 0 us -> 12.8 us
  other arithmetic: 12.7 us -> 0 us
  local copies, waits for them, and re-layouts: 9.01 us -> 0.58 us
  starting transfers between devices: 0.01 us -> 4.13 us
    dot_general x100 -> x0, matrix products: 68.5 us -> none  [the longest x20 27.9 us: expand_block(): jnp.dot(lat_rows, weight_key, preferred_element_type=jnp.float32)]
    all_gather x3 -> x0, blocking collectives: 17.4 us -> none  [the longest x1 6.82 us: shards(): lax.all_gather(new_latent[0], 'ctx', axis=0, tiled=True)]
    pallas_call x0 -> x8, Pallas kernels: none -> 12.8 us  [the longest x1 4.51 us: last_pass(): pl.pallas_call(functools.partial(last_kernel, blocks=len(notes), size=HEA...]
    lt x16 -> x0, other arithmetic: 10.1 us -> none  [advance(): visible = (offset + jnp.arange(BLOCK, dtype=jnp.int32))[None, :] < live_rows]
    unnamed x1 -> x0, blocking collectives: 5.32 us -> none
    ppermute x0 -> x6, starting transfers between devices: none -> 4.13 us  [hop(): return lax.ppermute(array, 'ctx', [(k, k ^ bit) for k in range(size)])]
    dynamic_slice x6 -> x0, local copies, waits for them, and re-layouts: 2.55 us -> none  [the longest x5 1.4 us: shards(): lax.dynamic_slice_in_dim(rotary, head_first * DR, GROUP * DR, 1)]
    reduce_sum x17 -> x0, other arithmetic: 2.24 us -> none  [expand_block(): running_sum = running_sum * factor + jnp.sum(weights, axis=-1)]
  transfers between devices with their start and end apart: 1 -> 6, of which waited for: 0 -> 1; matrix products, arithmetic and copies ran while one was open for 11% -> 0% of each run, Pallas kernels for 0% -> 44%
where the time goes in v2:
time: 19.3 us; the launch traced here: 19 us
  Pallas kernels  12.8 us (66%)
  starting transfers between devices  4.13 us (21%)
  waiting for transfers between devices  0.8 us (4%)
  between operations  0.74 us (4%)
  local copies, waits for them, and re-layouts  0.58 us (3%)
    pallas_call x1, Pallas kernels, last_pass(): pl.pallas_call(functools.partial(last_kernel, blocks=len(notes), size=HEA...  4.51 us
    ppermute x6, starting transfers between devices, hop(): return lax.ppermute(array, 'ctx', [(k, k ^ bit) for k in range(size)])  4.13 us
    pallas_call x1, Pallas kernels, near_pass(): pl.pallas_call(functools.partial(near_kernel, cached=len(blocks), size=HE...  2.97 us
    pallas_call x1, Pallas kernels, make_queries(): pl.pallas_call(queries_kernel, out_shape=pltpu.VMEM((rows, KEY), BF16), i...  2.65 us
    pallas_call x1, Pallas kernels, far_pass(): pl.pallas_call(functools.partial(far_kernel, size=HEADS_STEP * count), ou...  1.79 us
    pallas_call x1, Pallas kernels, pack(): pl.pallas_call(pack_kernel, out_shape=pltpu.VMEM((part + GROUP + DR // 2,...  0.82 us
    ppermute x6, waiting for transfers between devices, hop(): return lax.ppermute(array, 'ctx', [(k, k ^ bit) for k in range(size)])  0.8 us
    unnamed x4, local copies, waits for them, and re-layouts  0.58 us
  transfers between devices with their start and end apart: 6, of which 1 were waited for; matrix products, arithmetic and copies ran while one was open for 0% of the time, Pallas kernels for 44%

profile of v2, /device:TPU:0, one launch (start us, length us, event | category | flops | bytes accessed | tf_op | source)
XLA Modules:
  0.0 19.0 jit_solution(1610351232836666966)
XLA Ops:
  0.0 0.5 %collective-permute-start.1 = (bf16[256,512]{1,0:T(8,128)(2,1)}, bf16[256,512]{1,0:T(8,128)(2,1)S(1)}, u32[]{:S(2)}, u32[]{:S(2)}) collective-permute-start(bf16[256,512]{1,0:T(8,128)(2,1)} %bitcast.7), channel_id=1, source_target_pairs={{0,1},{1,0},{2,3},{3,2},{4,5},{5,4},{6,7},{7,6},{8,9},{9,8},{10,11... | collective-permute-start | bytes 786440 | tf_op jit(solution)/shard_map/ppermute | solution.py:367
  0.5 2.5 %collective-permute-start = (bf16[256,512]{1,0:T(8,128)(2,1)}, bf16[256,512]{1,0:T(8,128)(2,1)S(1)}, u32[]{:S(2)}, u32[]{:S(2)}) collective-permute-start(bf16[256,512]{1,0:T(8,128)(2,1)} %bitcast.8), channel_id=1, source_target_pairs={{0,2},{1,3},{2,0},{3,1},{4,6},{5,7},{6,4},{7,5},{8,10},{9,11},{10,... | collective-permute-start | bytes 786440 | tf_op jit(solution)/shard_map/ppermute | solution.py:367
  3.6 0.8 %pack.1.refs_1_.array_ref.refs_0_ = bf16[80,512]{1,0:T(8,128)(2,1)S(1)} custom-call(bf16[32,512]{1,0:T(8,128)(2,1)} %bitcast.10, bf16[32,64]{1,0:T(8,128)(2,1)} %bitcast.12, bf16[64,256]{1,0:T(8,128)(2,1)} %bitcast.11, s32[1,1]{1,0:T(1,128)S(6)} %copy.10.length_ref), custom_call_target="tpu_custom_call" | custom-call | flops 1000000 | bytes 1024 | tf_op jit(solution)/shard_map/pack/pallas_call | solution.py:86
  4.4 0.3 %collective-permute-start.2 = (bf16[80,512]{1,0:T(8,128)(2,1)S(1)}, bf16[80,512]{1,0:T(8,128)(2,1)S(1)}, u32[]{:S(2)}, u32[]{:S(2)}) collective-permute-start(bf16[80,512]{1,0:T(8,128)(2,1)S(1)} %pack.1.refs_1_.array_ref.refs_0_), channel_id=1, source_target_pairs={{0,1},{1,0},{2,3},{3,2},{4,5},{5,4},{6,7},{7,6},{8,9},{9,8},{10,11... | collective-permute-start | bytes 245768 | tf_op jit(solution)/shard_map/ppermute | solution.py:367
  4.7 2.6 %latent_queries.1.q_ref.token_ref = bf16[2048,640]{1,0:T(8,128)(2,1)S(1)} custom-call(bf16[1,128,8192]{2,1,0:T(8,128)(2,1)} %q_hbm.1, bf16[1,128,4096]{2,1,0:T(8,128)(2,1)} %r_hbm.1, bf16[512,2048]{1,0:T(8,128)(2,1)} %w_hbm.1), custom_call_target="tpu_custom_call" | custom-call | flops 1000000 | bytes 1024 | tf_op jit(solution)/shard_map/latent_queries/pallas_call | solution.py:139
  7.4 0.0 copy-start.1
  7.4 0.3 %collective-permute-start.4 = (bf16[80,512]{1,0:T(8,128)(2,1)S(1)}, bf16[80,512]{1,0:T(8,128)(2,1)S(1)}, u32[]{:S(2)}, u32[]{:S(2)}) collective-permute-start(bf16[80,512]{1,0:T(8,128)(2,1)S(1)} %pass_on.4), channel_id=1, source_target_pairs={{0,2},{1,3},{2,0},{3,1},{4,6},{5,7},{6,4},{7,5},{8,10},{9,11},{10,... | collective-permute-start | bytes 245768 | tf_op jit(solution)/shard_map/ppermute | solution.py:367
  7.7 0.0 collective-permute-done.2.refs_3_.refs_1_
  7.7 0.0 collective-permute-done.1.refs_2_
  7.7 0.6 %copy-done.1 = bf16[1,256,512]{2,1,0:T(8,128)(2,1)S(1)} copy-done((bf16[1,256,512]{2,1,0:T(8,128)(2,1)S(1)}, bf16[1,256,512]{2,1,0:T(8,128)(2,1)}, u32[]{:S(2)}) %copy-start.1) | copy-done | bytes 262168
  8.3 3.0 %near_rows.1 = (f32[2048,512]{1,0:T(8,128)S(1)}, f32[2048,128]{1,0:T(8,128)S(1)}, f32[2048,128]{1,0:T(8,128)S(1)}) custom-call(bf16[2048,640]{1,0:T(8,128)(2,1)S(1)} %latent_queries.1.q_ref.token_ref, bf16[256,512]{1,0:T(8,128)(2,1)S(1)} %bitcast.9, bf16[80,512]{1,0:T(8,128)(2,1)S(1)} %pack.1.refs_1_.array_ref.refs_0_, ...), custom_call_target="tpu_custom_call" | custom-call | flops 1000000000 | bytes 1024 | tf_op jit(solution)/shard_map/near_rows/pallas_call | solution.py:256
  11.3 0.8 %collective-permute-done.4.array_ref.note_ref.refs_2_ = bf16[80,512]{1,0:T(8,128)(2,1)S(1)} collective-permute-done((bf16[80,512]{1,0:T(8,128)(2,1)S(1)}, bf16[80,512]{1,0:T(8,128)(2,1)S(1)}, u32[]{:S(2)}, u32[]{:S(2)}) %collective-permute-start.4) | collective-permute-done | bytes 81952 | tf_op jit(solution)/shard_map/ppermute | solution.py:367
  12.1 0.0 collective-permute-start.5
  12.1 0.0 collective-permute-done.array_ref.lat_ref
  12.1 0.6 %collective-permute-start.3 = (bf16[256,512]{1,0:T(8,128)(2,1)S(1)}, bf16[256,512]{1,0:T(8,128)(2,1)S(1)}, u32[]{:S(2)}, u32[]{:S(2)}) collective-permute-start(bf16[256,512]{1,0:T(8,128)(2,1)S(1)} %pass_on.3), channel_id=1, source_target_pairs={{0,1},{1,0},{2,3},{3,2},{4,5},{5,4},{6,7},{7,6},{8,9},{9,8},{10,11... | collective-permute-start | bytes 786440 | tf_op jit(solution)/shard_map/ppermute | solution.py:367
  12.7 0.0 copy-start
  12.7 1.8 %far_rows.1 = (f32[2048,512]{1,0:T(8,128)S(1)}, f32[2048,128]{1,0:T(8,128)S(1)}, f32[2048,128]{1,0:T(8,128)S(1)}) custom-call(bf16[2048,640]{1,0:T(8,128)(2,1)S(1)} %latent_queries.1.q_ref.token_ref, bf16[256,512]{1,0:T(8,128)(2,1)S(1)} %collective-permute-done.array_ref.lat_ref, bf16[80,512]{1,0:T(8,128)(2,1)S(1)} %collective-permute-done.4.array_ref.note_ref.refs_2_, ...), custom_call_target="tpu_custom_call" | custom-call | flops 3000000000 | bytes 1024 | tf_op jit(solution)/shard_map/far_rows/pallas_call | solution.py:302
  14.5 0.0 collective-permute-done.5.refs_3_
  14.5 0.0 collective-permute-done.3.lat_ref
  14.5 0.0 copy-done
  14.5 4.5 %last_rows.1 = bf16[128,2048]{1,0:T(8,128)(2,1)} custom-call(bf16[2048,640]{1,0:T(8,128)(2,1)S(1)} %latent_queries.1.q_ref.token_ref, bf16[256,512]{1,0:T(8,128)(2,1)S(1)} %collective-permute-done.3.lat_ref, bf16[80,512]{1,0:T(8,128)(2,1)S(1)} %pack.1.refs_1_.array_ref.refs_0_, bf16[80,512]{1,0:T(8,128)(2,1)S(1)} %collective-permute-done.2.refs_3_.refs_1_, ...), custom_call_target="tpu_custom_call" | custom-call | flops 1000000 | bytes 1024 | tf_op jit(solution)/shard_map/last_rows/pallas_call | solution.py:353
  (3 shorter events, 0.0 us)
Async XLA Ops:
  0.0 7.7 %collective-permute-start.1 = (bf16[256,512]{1,0:T(8,128)(2,1)}, bf16[256,512]{1,0:T(8,128)(2,1)S(1)}, u32[]{:S(2)}, u32[]{:S(2)}) collective-permute-start(bf16[256,512]{1,0:T(8,128)(2,1)} %bitcast.7), channel_id=1, source_target_pairs={{0,1},{1,0},{2,3},{3,2},{4,5},{5,4},{6,7},{7,6},{8,9},{9,8},{10,11... | collective-permute-start | bytes 786440 | tf_op jit(solution)/shard_map/ppermute | solution.py:367
  0.5 11.7 %collective-permute-start = (bf16[256,512]{1,0:T(8,128)(2,1)}, bf16[256,512]{1,0:T(8,128)(2,1)S(1)}, u32[]{:S(2)}, u32[]{:S(2)}) collective-permute-start(bf16[256,512]{1,0:T(8,128)(2,1)} %bitcast.8), channel_id=1, source_target_pairs={{0,2},{1,3},{2,0},{3,1},{4,6},{5,7},{6,4},{7,5},{8,10},{9,11},{10,... | collective-permute-start | bytes 786440 | tf_op jit(solution)/shard_map/ppermute | solution.py:367
  4.4 3.3 %collective-permute-start.2 = (bf16[80,512]{1,0:T(8,128)(2,1)S(1)}, bf16[80,512]{1,0:T(8,128)(2,1)S(1)}, u32[]{:S(2)}, u32[]{:S(2)}) collective-permute-start(bf16[80,512]{1,0:T(8,128)(2,1)S(1)} %pack.1.refs_1_.array_ref.refs_0_), channel_id=1, source_target_pairs={{0,1},{1,0},{2,3},{3,2},{4,5},{5,4},{6,7},{7,6},{8,9},{9,8},{10,11... | collective-permute-start | bytes 245768 | tf_op jit(solution)/shard_map/ppermute | solution.py:367
  7.4 1.0 %copy-start.1 = (bf16[1,256,512]{2,1,0:T(8,128)(2,1)S(1)}, bf16[1,256,512]{2,1,0:T(8,128)(2,1)}, u32[]{:S(2)}) copy-start(bf16[1,256,512]{2,1,0:T(8,128)(2,1)} %param.11) | copy-start | bytes 786436
  7.4 4.7 %collective-permute-start.4 = (bf16[80,512]{1,0:T(8,128)(2,1)S(1)}, bf16[80,512]{1,0:T(8,128)(2,1)S(1)}, u32[]{:S(2)}, u32[]{:S(2)}) collective-permute-start(bf16[80,512]{1,0:T(8,128)(2,1)S(1)} %pass_on.4), channel_id=1, source_target_pairs={{0,2},{1,3},{2,0},{3,1},{4,6},{5,7},{6,4},{7,5},{8,10},{9,11},{10,... | collective-permute-start | bytes 245768 | tf_op jit(solution)/shard_map/ppermute | solution.py:367
  12.1 2.4 %collective-permute-start.5 = (bf16[80,512]{1,0:T(8,128)(2,1)S(1)}, bf16[80,512]{1,0:T(8,128)(2,1)S(1)}, u32[]{:S(2)}, u32[]{:S(2)}) collective-permute-start(bf16[80,512]{1,0:T(8,128)(2,1)S(1)} %pass_on.5), channel_id=1, source_target_pairs={{0,1},{1,0},{2,3},{3,2},{4,5},{5,4},{6,7},{7,6},{8,9},{9,8},{10,11... | collective-permute-start | bytes 245768 | tf_op jit(solution)/shard_map/ppermute | solution.py:367
  12.1 2.4 %collective-permute-start.3 = (bf16[256,512]{1,0:T(8,128)(2,1)S(1)}, bf16[256,512]{1,0:T(8,128)(2,1)S(1)}, u32[]{:S(2)}, u32[]{:S(2)}) collective-permute-start(bf16[256,512]{1,0:T(8,128)(2,1)S(1)} %pass_on.3), channel_id=1, source_target_pairs={{0,1},{1,0},{2,3},{3,2},{4,5},{5,4},{6,7},{7,6},{8,9},{9,8},{10,11... | collective-permute-start | bytes 786440 | tf_op jit(solution)/shard_map/ppermute | solution.py:367
  12.7 1.8 %copy-start = (bf16[512,2048]{1,0:T(8,128)(2,1)S(1)}, bf16[512,2048]{1,0:T(8,128)(2,1)}, u32[]{:S(2)}) copy-start(bf16[512,2048]{1,0:T(8,128)(2,1)} %refs_7_.1) | copy-start | bytes 6291460

commit v3 on v2

--- a/solution.py
+++ b/solution.py
@@ -18,7 +18,7 @@
 EXP_SCALE = math.log2(math.e) / math.sqrt(DH + DR)
 HEADS_STEP = 4
 GROUP = 16
-COSTS = {"pack": 0.001, "latent_queries": 0.001, "pass_on": 0.001, "near_rows": 1.0, "far_rows": 3.0, "last_rows": 0.001}
+COSTS = {"prepare": 0.001, "pass_on": 0.001, "near_rows": 1.0, "lat_scores": 1.0, "far_rows": 3.0, "last_rows": 0.001}
 VMEM_LIMIT = 20 * 1024 * 1024
 
 
@@ -38,6 +38,10 @@
     return lax.broadcasted_iota(jnp.int32, shape, dim)
 
 
+def span(step, size, first=0):
+    return slice(first + step * size, first + (step + 1) * size)
+
+
 def params():
     return pltpu.CompilerParams(vmem_limit_bytes=VMEM_LIMIT)
 
@@ -58,69 +62,61 @@
     return pltpu.with_memory_space_constraint(array, pltpu.HBM)
 
 
-def pack_kernel(fresh_hbm, rope_hbm, cached_hbm, length_ref, note_ref, rope_buf, cached_buf, sems):
+def prepare_kernel(
+    q_hbm,
+    r_hbm,
+    w_hbm,
+    lat_hbm,
+    fresh_hbm,
+    rope_hbm,
+    cached_hbm,
+    length_ref,
+    note_ref,
+    out_ref,
+    lat_ref,
+    q_buf,
+    r_buf,
+    w_buf,
+    rope_buf,
+    cached_buf,
+    sems,
+):
     part = fresh_hbm.shape[0]
     slots = cached_hbm.shape[1]
-    copies = [
-        pltpu.make_async_copy(fresh_hbm, note_ref.at[:part, :], sems.at[0]),
-        pltpu.make_async_copy(rope_hbm, rope_buf, sems.at[1]),
-        pltpu.make_async_copy(cached_hbm, cached_buf, sems.at[2]),
-    ]
-    for copy in copies:
-        copy.start()
-    note_ref[part : part + GROUP, :] = jnp.zeros((GROUP, DC), BF16)
-    groups = part // GROUP
-    live = jnp.broadcast_to(length_ref[...], (GROUP, LANES)).astype(F32).astype(BF16)
-    note_ref[part : part + GROUP, groups * LANES : (groups + 1) * LANES] = live
-    copies[1].wait()
-    for k in range(groups):
-        note_ref[part : part + GROUP, k * LANES : k * LANES + DR] = rope_buf[k * GROUP : (k + 1) * GROUP, :]
-    copies[2].wait()
-    note_ref[part + GROUP :, :slots] = cached_buf[: DR // 2, :]
-    note_ref[part + GROUP :, slots:] = cached_buf[DR // 2 :, :]
-    copies[0].wait()
-
-
-def pack(fresh, rope, cached_rope, length):
-    part = fresh.shape[0]
-    return pl.pallas_call(
-        pack_kernel,
-        out_shape=pltpu.VMEM((part + GROUP + DR // 2, DC), BF16),
-        in_specs=[HBM, HBM, HBM, VMEM],
-        out_specs=VMEM,
-        scratch_shapes=[
-            pltpu.VMEM(rope.shape, BF16),
-            pltpu.VMEM(cached_rope.shape, BF16),
-            pltpu.SemaphoreType.DMA((3,)),
-        ],
-        compiler_params=params(),
-        cost_estimate=cost(COSTS["pack"]),
-        name="pack",
-    )(in_hbm(fresh), in_hbm(rope), in_hbm(cached_rope), length)
-
-
-def queries_kernel(q_hbm, r_hbm, w_hbm, out_ref, q_buf, r_buf, w_buf, sems):
     count = q_buf.shape[0]
     heads = out_ref.shape[0] // count
     me = lax.axis_index("ctx")
     q_first = pl.multiple_of(me * (heads * DH), LANES)
     r_first = pl.multiple_of(me * (heads * DR), LANES)
-    q_copy = pltpu.make_async_copy(q_hbm.at[0, :, pl.ds(q_first, heads * DH)], q_buf, sems.at[0])
-    r_copy = pltpu.make_async_copy(r_hbm.at[0, :, pl.ds(r_first, heads * DR)], r_buf, sems.at[1])
-    q_copy.start()
     width = HEADS_STEP * DH
-    w_copies = []
+    pairs = [
+        (q_hbm.at[0, :, pl.ds(q_first, heads * DH)], q_buf),
+        (fresh_hbm, note_ref.at[:part, :]),
+        (rope_hbm, rope_buf),
+        (cached_hbm, cached_buf),
+        (r_hbm.at[0, :, pl.ds(r_first, heads * DR)], r_buf),
+    ]
     for step in range(heads // HEADS_STEP):
         cols = pl.ds(step * width, width)
-        w_copies.append(pltpu.make_async_copy(w_hbm.at[:, cols], w_buf.at[:, cols], sems.at[2 + step]))
-        w_copies[-1].start()
-    r_copy.start()
-    q_copy.wait()
-    for head in range(heads):
-        if head % HEADS_STEP == 0:
-            w_copies[head // HEADS_STEP].wait()
-        cols = slice(head * DH, (head + 1) * DH)
-        out_ref[head * count : (head + 1) * count, :DC] = dot_t(q_buf[:, cols], w_buf[:, cols]).astype(BF16)
+        pairs.append((w_hbm.at[:, cols], w_buf.at[:, cols]))
+    pairs.append((lat_hbm, lat_ref))
+    copies = [pltpu.make_async_copy(source, target, sems.at[k]) for k, (source, target) in enumerate(pairs)]
+    for copy in copies:
+        copy.start()
+    q_copy, fresh_copy, rope_copy, cached_copy, r_copy = copies[:5]
+    w_copies, lat_copy = copies[5:-1], copies[-1]
+
+    groups = part // GROUP
+    note_ref[part : part + GROUP, :] = jnp.zeros((GROUP, DC), BF16)
+    live = jnp.broadcast_to(length_ref[...], (GROUP, LANES)).astype(F32).astype(BF16)
+    note_ref[part : part + GROUP, groups * LANES : (groups + 1) * LANES] = live
+    rope_copy.wait()
+    for k in range(groups):
+        note_ref[part : part + GROUP, k * LANES : k * LANES + DR] = rope_buf[k * GROUP : (k + 1) * GROUP, :]
+    cached_copy.wait()
+    note_ref[part + GROUP :, :slots] = cached_buf[: DR // 2, :]
+    note_ref[part + GROUP :, slots:] = cached_buf[DR // 2 :, :]
+
     r_copy.wait()
     lane = iota((count, LANES), 1)
     side = jnp.where(lane == DR, 1.0, 0.0)
@@ -128,29 +124,42 @@
         both = r_buf[:, pair * LANES : (pair + 1) * LANES].astype(F32)
         for odd in range(2):
             one = pltpu.roll(both, DR, 1) if odd else both
-            head = 2 * pair + odd
-            out_ref[head * count : (head + 1) * count, DC:] = jnp.where(lane < DR, one, side).astype(BF16)
-
-
-def make_queries(q_nope, q_rope, w_key):
+            out_ref[span(2 * pair + odd, count), DC:] = jnp.where(lane < DR, one, side).astype(BF16)
+    q_copy.wait()
+    for head in range(heads):
+        if head % HEADS_STEP == 0:
+            w_copies[head // HEADS_STEP].wait()
+        cols = span(head, DH)
+        out_ref[span(head, count), :DC] = dot_t(q_buf[:, cols], w_buf[:, cols]).astype(BF16)
+    fresh_copy.wait()
+    lat_copy.wait()
+
+
+def prepare(q_nope, q_rope, w_key, lat, fresh, rope, cached_rope, length):
     count = q_nope.shape[1]
     heads = w_key.shape[1] // DH
-    rows = heads * count
-    return pl.pallas_call(
-        queries_kernel,
-        out_shape=pltpu.VMEM((rows, KEY), BF16),
-        in_specs=[HBM, HBM, HBM],
-        out_specs=VMEM,
+    part = fresh.shape[0]
+    return pl.pallas_call(
+        prepare_kernel,
+        out_shape=(
+            pltpu.VMEM((part + GROUP + DR // 2, DC), BF16),
+            pltpu.VMEM((heads * count, KEY), BF16),
+            pltpu.VMEM(lat.shape, BF16),
+        ),
+        in_specs=[HBM] * 7 + [VMEM],
+        out_specs=(VMEM, VMEM, VMEM),
         scratch_shapes=[
             pltpu.VMEM((count, heads * DH), BF16),
             pltpu.VMEM((count, heads * DR), BF16),
             pltpu.VMEM(w_key.shape, BF16),
-            pltpu.SemaphoreType.DMA((2 + heads // HEADS_STEP,)),
+            pltpu.VMEM(rope.shape, BF16),
+            pltpu.VMEM(cached_rope.shape, BF16),
+            pltpu.SemaphoreType.DMA((6 + heads // HEADS_STEP,)),
         ],
         compiler_params=params(),
-        cost_estimate=cost(COSTS["latent_queries"]),
-        name="latent_queries",
-    )(in_hbm(q_nope), in_hbm(q_rope), in_hbm(w_key))
+        cost_estimate=cost(COSTS["prepare"]),
+        name="prepare",
+    )(*[in_hbm(array) for array in (q_nope, q_rope, w_key, lat, fresh, rope, cached_rope)], length)
 
 
 def pass_kernel(array_ref, token_ref, out_ref):
@@ -171,15 +180,18 @@
 
 def put_cached(key_buf, first, lat_ref, note_ref):
     slots = lat_ref.shape[0]
+    key_buf[first : first + slots, :DC] = lat_ref[...]
+    key_buf[first : first + slots, DC:] = masked_rope(note_ref, slots)
+
+
+def masked_rope(note_ref, slots):
     part = note_ref.shape[0] - GROUP - DR // 2
     lane = part // GROUP * LANES
     live = note_ref[part : part + 1, lane : lane + 1].astype(F32)
     blocked = jnp.where(iota((LANES - DR, slots), 1).astype(F32) < live, 0.0, BLOCKED)
     blocked = jnp.where(iota((LANES - DR, slots), 0) == 0, blocked, 0.0)
     rope = note_ref[part + GROUP :, :].astype(F32)
-    both = jnp.concatenate([rope[:, :slots], rope[:, slots:], blocked], axis=0)
-    key_buf[first : first + slots, :DC] = lat_ref[...]
-    key_buf[first : first + slots, DC:] = both.T.astype(BF16)
+    return jnp.concatenate([rope[:, :slots], rope[:, slots:], blocked], axis=0).T.astype(BF16)
 
 
 def put_fresh(key_buf, first, note_refs):
@@ -220,10 +232,6 @@
     return jnp.concatenate(parts, axis=1), total
 
 
-def span(step, size, first=0):
-    return slice(first + step * size, first + (step + 1) * size)
-
-
 def state_shapes(rows):
     return (pltpu.VMEM((rows, DC), F32), pltpu.VMEM((rows, LANES), F32), pltpu.VMEM((rows, LANES), F32))
 
@@ -265,12 +273,31 @@
     )(q, *[array for block in blocks for array in block])
 
 
-def advance(q_ref, key_buf, state_in, state_out, size):
-    acc_in, sum_in, max_in = state_in
-    acc_ref, sum_ref, max_ref = state_out
+def scores_kernel(q_ref, lat_ref, out_ref, *, size):
+    for step in range(q_ref.shape[0] // size):
+        rows = span(step, size)
+        out_ref[rows, :] = dot_t(q_ref[rows, :DC], lat_ref[...])
+
+
+def lat_scores(q, lat, count):
+    rows = q.shape[0]
+    return pl.pallas_call(
+        functools.partial(scores_kernel, size=HEADS_STEP * count),
+        out_shape=pltpu.VMEM((rows, lat.shape[0]), F32),
+        in_specs=[VMEM] * 2,
+        out_specs=VMEM,
+        compiler_params=params(),
+        cost_estimate=cost(COSTS["lat_scores"]),
+        name="lat_scores",
+    )(q, lat)
+
+
+def far_kernel(q_ref, lat_ref, note_ref, s_ref, acc_in, sum_in, max_in, acc_ref, sum_ref, max_ref, ext_buf, *, size):
+    ext_buf[...] = masked_rope(note_ref, lat_ref.shape[0])
 
     def scores(step):
-        return dot_t(q_ref[span(step, size), :], key_buf[...])
+        rows = span(step, size)
+        return s_ref[rows, :] + dot_t(q_ref[rows, DC:], ext_buf[...])
 
     def weigh(step, s):
         rows = span(step, size)
@@ -284,31 +311,26 @@
 
     def collect(step, p, factor):
         rows = span(step, size)
-        grown = dot(p, key_buf[:, :DC])
+        grown = dot(p, lat_ref[...])
         for k in range(DC // LANES):
-            cols = slice(k * LANES, (k + 1) * LANES)
+            cols = span(k, LANES)
             acc_ref[rows, cols] = acc_in[rows, cols] * factor + grown[:, cols]
 
     pipeline(q_ref.shape[0] // size, scores, weigh, collect)
 
 
-def far_kernel(q_ref, lat_ref, note_ref, *refs, size):
-    put_cached(refs[6], 0, lat_ref, note_ref)
-    advance(q_ref, refs[6], refs[:3], refs[3:6], size)
-
-
-def far_pass(q, lat, note, state, count):
+def far_pass(q, lat, note, lat_part, state, count):
     rows = q.shape[0]
     return pl.pallas_call(
         functools.partial(far_kernel, size=HEADS_STEP * count),
         out_shape=state_shapes(rows),
-        in_specs=[VMEM] * 6,
+        in_specs=[VMEM] * 7,
         out_specs=(VMEM, VMEM, VMEM),
-        scratch_shapes=[pltpu.VMEM((lat.shape[0], KEY), BF16)],
+        scratch_shapes=[pltpu.VMEM((lat.shape[0], LANES), BF16)],
         compiler_params=params(),
         cost_estimate=cost(COSTS["far_rows"]),
         name="far_rows",
-    )(q, lat, note, *state)
+    )(q, lat, note, lat_part, *state)
 
 
 def last_kernel(q_ref, lat_ref, *refs, blocks, size):
@@ -321,11 +343,11 @@
     bias = jnp.concatenate([causal(count // blocks, blocks)] * HEADS_STEP, axis=0)
 
     def scores(step):
-        return dot_t(q_ref[span(step, size), :], key_buf[...])
+        s = dot_t(q_ref[span(step, size), :], key_buf[...])
+        return jnp.concatenate([s[:, :slots], s[:, slots:] + bias], axis=1)
 
     def weigh(step, s):
         rows = span(step, size)
-        s = jnp.concatenate([s[:, :slots], s[:, slots:] + bias], axis=1)
         before = max_in[rows, :]
         level = jnp.maximum(before, jnp.max(s, axis=1, keepdims=True))
         factor = jnp.exp2((before - level) * EXP_SCALE)
@@ -371,15 +393,17 @@
     count = q_nope.shape[1]
     lat = cache_latent[0]
     far_lat, near_lat = hop(lat, 2), hop(lat, 1)
-    note = pack(new_latent[0], new_rope[0], cache_rope[0].T, lengths)
-    near_note = hop(note, 1)
-    q = make_queries(q_nope, q_rope, w_key)
-    far_note = hop(after(note, q), 2)
+    note, q, lat = prepare(
+        q_nope, q_rope, w_key, lat, new_latent[0], new_rope[0], cache_rope[0].T, lengths
+    )
+    far_note, near_note = hop(note, 2), hop(note, 1)
     state = near_pass(q, [(lat, note), (near_lat, near_note)], count)
     last_lat = hop(after(far_lat, state[2]), 1)
-    last_note = hop(after(far_note, state[2]), 1)
-    state = far_pass(q, far_lat, far_note, state, count)
-    return last_pass(q, last_lat, [note, near_note, far_note, last_note], state, w_value, count)[None]
+    far_part = lat_scores(q, far_lat, count)
+    last_note = hop(after(far_note, far_part), 1)
+    state = far_pass(q, far_lat, far_note, far_part, state, count)
+    notes = [note, near_note, far_note, last_note]
+    return last_pass(q, last_lat, notes, state, w_value, count)[None]
 
 
 def solution(mesh):

time: 19.3 us -> 18.3 us (0.948)
  local copies, waits for them, and re-layouts: 0.58 us -> 0.05 us
  Pallas kernels: 12.8 us -> 12.4 us
    unnamed x4 -> x2, local copies, waits for them, and re-layouts: 0.58 us -> 0.05 us
    pallas_call x1, Pallas kernels: 1.79 us -> 1.51 us  [far_pass(): pl.pallas_call(functools.partial(far_kernel, size=HEADS_STEP * count), ou...]
  transfers between devices with their start and end apart: 6 -> 6, of which waited for: 1 -> 2; matrix products, arithmetic and copies ran while one was open for 0% -> 0% of each run, Pallas kernels for 44% -> 44%
where the time goes in v3:
time: 18.3 us; the launch traced here: 18.2 us
  Pallas kernels  12.4 us (68%)
  starting transfers between devices  3.99 us (22%)
  waiting for transfers between devices  0.96 us (5%)
  between operations  0.71 us (4%)
    pallas_call x1, Pallas kernels, last_pass(): pl.pallas_call(functools.partial(last_kernel, blocks=len(notes), size=HEA...  4.51 us
    ppermute x6, starting transfers between devices, hop(): return lax.ppermute(array, 'ctx', [(k, k ^ bit) for k in range(size)])  3.99 us
    pallas_call x1, Pallas kernels, near_pass(): pl.pallas_call(functools.partial(near_kernel, cached=len(blocks), size=HE...  2.97 us
    pallas_call x1, Pallas kernels, prepare(): pl.pallas_call(prepare_kernel, out_shape=(pltpu.VMEM((part + GROUP + DR /...  2.68 us
    pallas_call x1, Pallas kernels, far_pass(): pl.pallas_call(functools.partial(far_kernel, size=HEADS_STEP * count), ou...  1.51 us
    ppermute x6, waiting for transfers between devices, hop(): return lax.ppermute(array, 'ctx', [(k, k ^ bit) for k in range(size)])  0.96 us
    pallas_call x1, Pallas kernels, lat_scores(): pl.pallas_call(functools.partial(scores_kernel, size=HEADS_STEP * count),...  0.74 us
  transfers between devices with their start and end apart: 6, of which 2 were waited for; matrix products, arithmetic and copies ran while one was open for 0% of the time, Pallas kernels for 44%

profile of v3, /device:TPU:0, one launch (start us, length us, event | category | flops | bytes accessed | tf_op | source)
XLA Modules:
  0.0 18.2 jit_solution(10670032150933324419)
XLA Ops:
  0.0 0.5 %collective-permute-start.1 = (bf16[256,512]{1,0:T(8,128)(2,1)}, bf16[256,512]{1,0:T(8,128)(2,1)S(1)}, u32[]{:S(2)}, u32[]{:S(2)}) collective-permute-start(bf16[256,512]{1,0:T(8,128)(2,1)} %bitcast.7), channel_id=1, source_target_pairs={{0,1},{1,0},{2,3},{3,2},{4,5},{5,4},{6,7},{7,6},{8,9},{9,8},{10,11... | collective-permute-start | bytes 786440 | tf_op jit(solution)/shard_map/ppermute | solution.py:389
  0.5 2.5 %collective-permute-start = (bf16[256,512]{1,0:T(8,128)(2,1)}, bf16[256,512]{1,0:T(8,128)(2,1)S(1)}, u32[]{:S(2)}, u32[]{:S(2)}) collective-permute-start(bf16[256,512]{1,0:T(8,128)(2,1)} %bitcast.8), channel_id=1, source_target_pairs={{0,2},{1,3},{2,0},{3,1},{4,6},{5,7},{6,4},{7,5},{8,10},{9,11},{10,... | collective-permute-start | bytes 786440 | tf_op jit(solution)/shard_map/ppermute | solution.py:389
  3.6 2.7 %prepare.1 = (bf16[80,512]{1,0:T(8,128)(2,1)S(1)}, bf16[2048,640]{1,0:T(8,128)(2,1)S(1)}, bf16[256,512]{1,0:T(8,128)(2,1)S(1)}) custom-call(bf16[1,128,8192]{2,1,0:T(8,128)(2,1)} %q_hbm.1, bf16[1,128,4096]{2,1,0:T(8,128)(2,1)} %r_hbm.1, bf16[512,2048]{1,0:T(8,128)(2,1)} %w_hbm.1, bf16[256,512]{1,0:T(8,128)(2,1)} %bitcast.9, bf16[32,512]{1,0:T(8,128)(2,1)} %bitcast.10, ...), custom_call_target="tpu_custom_call" | custom-call | flops 1000000 | bytes 1024 | tf_op jit(solution)/shard_map/prepare/pallas_call | solution.py:142
  6.3 0.3 %collective-permute-start.2 = (bf16[80,512]{1,0:T(8,128)(2,1)S(1)}, bf16[80,512]{1,0:T(8,128)(2,1)S(1)}, u32[]{:S(2)}, u32[]{:S(2)}) collective-permute-start(bf16[80,512]{1,0:T(8,128)(2,1)S(1)} %get-tuple-element.16.refs_1_.refs_0_), channel_id=1, source_target_pairs={{0,1},{1,0},{2,3},{3,2},{4,5},{5,4},{6,7},{7,6},{8,9},{9,8},{10,11... | collective-permute-start | bytes 245768 | tf_op jit(solution)/shard_map/ppermute | solution.py:389
  6.6 0.3 %collective-permute-start.4 = (bf16[80,512]{1,0:T(8,128)(2,1)S(1)}, bf16[80,512]{1,0:T(8,128)(2,1)S(1)}, u32[]{:S(2)}, u32[]{:S(2)}) collective-permute-start(bf16[80,512]{1,0:T(8,128)(2,1)S(1)} %get-tuple-element.16.refs_1_.refs_0_), channel_id=1, source_target_pairs={{0,2},{1,3},{2,0},{3,1},{4,6},{5,7},{6,4},{7,5},{8,10},{9,11},{10,... | collective-permute-start | bytes 245768 | tf_op jit(solution)/shard_map/ppermute | solution.py:389
  6.9 0.8 %collective-permute-done.2.refs_3_.refs_1_ = bf16[80,512]{1,0:T(8,128)(2,1)S(1)} collective-permute-done((bf16[80,512]{1,0:T(8,128)(2,1)S(1)}, bf16[80,512]{1,0:T(8,128)(2,1)S(1)}, u32[]{:S(2)}, u32[]{:S(2)}) %collective-permute-start.2) | collective-permute-done | bytes 81952 | tf_op jit(solution)/shard_map/ppermute | solution.py:389
  7.6 0.0 collective-permute-done.1.refs_2_
  7.6 3.0 %near_rows.1 = (f32[2048,512]{1,0:T(8,128)S(1)}, f32[2048,128]{1,0:T(8,128)S(1)}, f32[2048,128]{1,0:T(8,128)S(1)}) custom-call(bf16[2048,640]{1,0:T(8,128)(2,1)S(1)} %get-tuple-element.14.q_ref, bf16[256,512]{1,0:T(8,128)(2,1)S(1)} %get-tuple-element.15.refs_0_, bf16[80,512]{1,0:T(8,128)(2,1)S(1)} %get-tuple-element.16.refs_1_.refs_0_, ...), custom_call_target="tpu_custom_call" | custom-call | flops 1000000000 | bytes 1024 | tf_op jit(solution)/shard_map/near_rows/pallas_call | solution.py:264
  10.6 0.0 collective-permute-done.array_ref.lat_ref
  10.6 0.3 %collective-permute-start.3 = (bf16[256,512]{1,0:T(8,128)(2,1)S(1)}, bf16[256,512]{1,0:T(8,128)(2,1)S(1)}, u32[]{:S(2)}, u32[]{:S(2)}) collective-permute-start(bf16[256,512]{1,0:T(8,128)(2,1)S(1)} %pass_on.2), channel_id=1, source_target_pairs={{0,1},{1,0},{2,3},{3,2},{4,5},{5,4},{6,7},{7,6},{8,9},{9,8},{10,11... | collective-permute-start | bytes 786440 | tf_op jit(solution)/shard_map/ppermute | solution.py:389
  10.9 0.7 %lat_scores.1.token_ref.s_ref = f32[2048,256]{1,0:T(8,128)S(1)} custom-call(bf16[2048,640]{1,0:T(8,128)(2,1)S(1)} %get-tuple-element.14.q_ref, bf16[256,512]{1,0:T(8,128)(2,1)S(1)} %collective-permute-done.array_ref.lat_ref), custom_call_target="tpu_custom_call" | custom-call | flops 1000000000 | bytes 1024 | tf_op jit(solution)/shard_map/lat_scores/pallas_call | solution.py:284
  11.7 0.2 %collective-permute-done.4.array_ref.note_ref.refs_2_ = bf16[80,512]{1,0:T(8,128)(2,1)S(1)} collective-permute-done((bf16[80,512]{1,0:T(8,128)(2,1)S(1)}, bf16[80,512]{1,0:T(8,128)(2,1)S(1)}, u32[]{:S(2)}, u32[]{:S(2)}) %collective-permute-start.4) | collective-permute-done | bytes 81952 | tf_op jit(solution)/shard_map/ppermute | solution.py:389
  11.9 0.2 collective-permute-start.5
  12.1 0.0 copy-start
  12.1 1.5 %far_rows.1 = (f32[2048,512]{1,0:T(8,128)S(1)}, f32[2048,128]{1,0:T(8,128)S(1)}, f32[2048,128]{1,0:T(8,128)S(1)}) custom-call(bf16[2048,640]{1,0:T(8,128)(2,1)S(1)} %get-tuple-element.14.q_ref, bf16[256,512]{1,0:T(8,128)(2,1)S(1)} %collective-permute-done.array_ref.lat_ref, bf16[80,512]{1,0:T(8,128)(2,1)S(1)} %collective-permute-done.4.array_ref.note_ref.refs_2_, ...), custom_call_target="tpu_custom_call" | custom-call | flops 3000000000 | bytes 1024 | tf_op jit(solution)/shard_map/far_rows/pallas_call | solution.py:324
  13.6 0.0 collective-permute-done.5.refs_3_
  13.6 0.0 collective-permute-done.3.lat_ref
  13.6 0.1 copy-done
  13.6 4.5 %last_rows.1 = bf16[128,2048]{1,0:T(8,128)(2,1)} custom-call(bf16[2048,640]{1,0:T(8,128)(2,1)S(1)} %get-tuple-element.14.q_ref, bf16[256,512]{1,0:T(8,128)(2,1)S(1)} %collective-permute-done.3.lat_ref, bf16[80,512]{1,0:T(8,128)(2,1)S(1)} %get-tuple-element.16.refs_1_.refs_0_, bf16[80,512]{1,0:T(8,128)(2,1)S(1)} %collective-permute-done.2.refs_3_.refs_1_, ...), custom_call_target="tpu_custom_call" | custom-call | flops 1000000 | bytes 1024 | tf_op jit(solution)/shard_map/last_rows/pallas_call | solution.py:375
  (2 shorter events, 0.0 us)
Async XLA Ops:
  0.0 7.6 %collective-permute-start.1 = (bf16[256,512]{1,0:T(8,128)(2,1)}, bf16[256,512]{1,0:T(8,128)(2,1)S(1)}, u32[]{:S(2)}, u32[]{:S(2)}) collective-permute-start(bf16[256,512]{1,0:T(8,128)(2,1)} %bitcast.7), channel_id=1, source_target_pairs={{0,1},{1,0},{2,3},{3,2},{4,5},{5,4},{6,7},{7,6},{8,9},{9,8},{10,11... | collective-permute-start | bytes 786440 | tf_op jit(solution)/shard_map/ppermute | solution.py:389
  0.5 10.2 %collective-permute-start = (bf16[256,512]{1,0:T(8,128)(2,1)}, bf16[256,512]{1,0:T(8,128)(2,1)S(1)}, u32[]{:S(2)}, u32[]{:S(2)}) collective-permute-start(bf16[256,512]{1,0:T(8,128)(2,1)} %bitcast.8), channel_id=1, source_target_pairs={{0,2},{1,3},{2,0},{3,1},{4,6},{5,7},{6,4},{7,5},{8,10},{9,11},{10,... | collective-permute-start | bytes 786440 | tf_op jit(solution)/shard_map/ppermute | solution.py:389
  6.3 1.3 %collective-permute-start.2 = (bf16[80,512]{1,0:T(8,128)(2,1)S(1)}, bf16[80,512]{1,0:T(8,128)(2,1)S(1)}, u32[]{:S(2)}, u32[]{:S(2)}) collective-permute-start(bf16[80,512]{1,0:T(8,128)(2,1)S(1)} %get-tuple-element.16.refs_1_.refs_0_), channel_id=1, source_target_pairs={{0,1},{1,0},{2,3},{3,2},{4,5},{5,4},{6,7},{7,6},{8,9},{9,8},{10,11... | collective-permute-start | bytes 245768 | tf_op jit(solution)/shard_map/ppermute | solution.py:389
  6.6 5.3 %collective-permute-start.4 = (bf16[80,512]{1,0:T(8,128)(2,1)S(1)}, bf16[80,512]{1,0:T(8,128)(2,1)S(1)}, u32[]{:S(2)}, u32[]{:S(2)}) collective-permute-start(bf16[80,512]{1,0:T(8,128)(2,1)S(1)} %get-tuple-element.16.refs_1_.refs_0_), channel_id=1, source_target_pairs={{0,2},{1,3},{2,0},{3,1},{4,6},{5,7},{6,4},{7,5},{8,10},{9,11},{10,... | collective-permute-start | bytes 245768 | tf_op jit(solution)/shard_map/ppermute | solution.py:389
  10.6 2.9 %collective-permute-start.3 = (bf16[256,512]{1,0:T(8,128)(2,1)S(1)}, bf16[256,512]{1,0:T(8,128)(2,1)S(1)}, u32[]{:S(2)}, u32[]{:S(2)}) collective-permute-start(bf16[256,512]{1,0:T(8,128)(2,1)S(1)} %pass_on.2), channel_id=1, source_target_pairs={{0,1},{1,0},{2,3},{3,2},{4,5},{5,4},{6,7},{7,6},{8,9},{9,8},{10,11... | collective-permute-start | bytes 786440 | tf_op jit(solution)/shard_map/ppermute | solution.py:389
  11.9 1.7 %collective-permute-start.5 = (bf16[80,512]{1,0:T(8,128)(2,1)S(1)}, bf16[80,512]{1,0:T(8,128)(2,1)S(1)}, u32[]{:S(2)}, u32[]{:S(2)}) collective-permute-start(bf16[80,512]{1,0:T(8,128)(2,1)S(1)} %pass_on.3), channel_id=1, source_target_pairs={{0,1},{1,0},{2,3},{3,2},{4,5},{5,4},{6,7},{7,6},{8,9},{9,8},{10,11... | collective-permute-start | bytes 245768 | tf_op jit(solution)/shard_map/ppermute | solution.py:389
  12.1 1.6 %copy-start = (bf16[512,2048]{1,0:T(8,128)(2,1)S(1)}, bf16[512,2048]{1,0:T(8,128)(2,1)}, u32[]{:S(2)}) copy-start(bf16[512,2048]{1,0:T(8,128)(2,1)} %refs_7_.1) | copy-start | bytes 6291460

commit v4 on v3

v4 whole, which is shorter than its diff:
```python
import functools
import math

import jax
import jax.numpy as jnp
from jax import lax
from jax.experimental import pallas as pl
from jax.experimental.pallas import tpu as pltpu
from jax.sharding import PartitionSpec as P

DC = 512
DR = 64
DH = 128
DV = 128
LANES = 128
KEY = DC + LANES
BLOCKED = -1e30
EXP_SCALE = math.log2(math.e) / math.sqrt(DH + DR)
HEADS_STEP = 8
GROUP = 16
COSTS = {"pack": 5.0, "latent_queries": 0.001, "pass_on": 0.001, "near_rows": 1.0, "early": 3.0, "far_rows": 3.0, "last_rows": 0.001}
VMEM_LIMIT = 20 * 1024 * 1024


def cost(micros):
    return pl.CostEstimate(flops=int(micros * 1e9), bytes_accessed=1024, transcendentals=0)


BF16 = jnp.bfloat16
F32 = jnp.float32

VMEM = pl.BlockSpec(memory_space=pltpu.VMEM)
HBM = pl.BlockSpec(memory_space=pltpu.HBM)
ANYWHERE = pl.BlockSpec(memory_space=pl.ANY)


def iota(shape, dim):
    return lax.broadcasted_iota(jnp.int32, shape, dim)


def span(step, size, first=0):
    return slice(first + step * size, first + (step + 1) * size)


def params():
    return pltpu.CompilerParams(vmem_limit_bytes=VMEM_LIMIT)


def in_vmem(array):
    return pltpu.with_memory_space_constraint(array, pltpu.VMEM)


def dot(a, b):
    return jnp.dot(a, b, preferred_element_type=F32)


def dot_t(a, b):
    return lax.dot_general(a, b, (((1,), (1,)), ((), ())), preferred_element_type=F32)


def in_hbm(array):
    return pltpu.with_memory_space_constraint(array, pltpu.HBM)


def pack_kernel(
    fresh_hbm,
    rope_hbm,
    cached_hbm,
    lat_hbm,
    q_hbm,
    r_hbm,
    length_ref,
    note_ref,
    lat_ref,
    q_ref,
    r_ref,
    rope_buf,
    cached_buf,
    sems,
):
    part = fresh_hbm.shape[0]
    slots = cached_hbm.shape[1]
    me = lax.axis_index("ctx")
    q_first = pl.multiple_of(me * q_ref.shape[1], LANES)
    r_first = pl.multiple_of(me * r_ref.shape[1], LANES)
    pairs = [
        (rope_hbm, rope_buf),
        (cached_hbm, cached_buf),
        (fresh_hbm, note_ref.at[:part, :]),
        (q_hbm.at[0, :, pl.ds(q_first, q_ref.shape[1])], q_ref),
        (r_hbm.at[0, :, pl.ds(r_first, r_ref.shape[1])], r_ref),
        (lat_hbm, lat_ref),
    ]
    copies = [pltpu.make_async_copy(source, target, sems.at[k]) for k, (source, target) in enumerate(pairs)]
    for copy in copies:
        copy.start()
    groups = part // GROUP
    note_ref[part : part + GROUP, :] = jnp.zeros((GROUP, DC), BF16)
    live = jnp.broadcast_to(length_ref[...], (GROUP, LANES)).astype(F32).astype(BF16)
    note_ref[part : part + GROUP, groups * LANES : (groups + 1) * LANES] = live
    copies[0].wait()
    for k in range(groups):
        note_ref[part : part + GROUP, k * LANES : k * LANES + DR] = rope_buf[span(k, GROUP), :]
    copies[1].wait()
    note_ref[part + GROUP :, :slots] = cached_buf[: DR // 2, :]
    note_ref[part + GROUP :, slots:] = cached_buf[DR // 2 :, :]
    for copy in copies[2:]:
        copy.wait()


def pack(fresh, rope, cached_rope, lat, q_nope, q_rope, length, heads):
    part = fresh.shape[0]
    count = q_nope.shape[1]
    return pl.pallas_call(
        pack_kernel,
        out_shape=(
            pltpu.VMEM((part + GROUP + DR // 2, DC), BF16),
            pltpu.VMEM(lat.shape, BF16),
            pltpu.VMEM((count, heads * DH), BF16),
            pltpu.VMEM((count, heads * DR), BF16),
        ),
        in_specs=[HBM] * 6 + [VMEM],
        out_specs=(VMEM, VMEM, VMEM, VMEM),
        scratch_shapes=[
            pltpu.VMEM(rope.shape, BF16),
            pltpu.VMEM(cached_rope.shape, BF16),
            pltpu.SemaphoreType.DMA((6,)),
        ],
        compiler_params=params(),
        cost_estimate=cost(COSTS["pack"]),
        name="pack",
    )(*[in_hbm(array) for array in (fresh, rope, cached_rope, lat, q_nope, q_rope)], length)


def queries_kernel(q_ref, r_ref, w_ref, out_ref):
    count = q_ref.shape[0]
    heads = out_ref.shape[0] // count
    lane = iota((count, LANES), 1)
    side = jnp.where(lane == DR, 1.0, 0.0)
    for pair in range(heads // 2):
        both = r_ref[:, span(pair, LANES)].astype(F32)
        for odd in range(2):
            head = 2 * pair + odd
            one = pltpu.roll(both, DR, 1) if odd else both
            out_ref[span(head, count), :DC] = dot_t(q_ref[:, span(head, DH)], w_ref[:, span(head, DH)]).astype(BF16)
            out_ref[span(head, count), DC:] = jnp.where(lane < DR, one, side).astype(BF16)


def make_queries(q, r, w_key):
    count = q.shape[0]
    heads = w_key.shape[1] // DH
    return pl.pallas_call(
        queries_kernel,
        out_shape=pltpu.VMEM((heads * count, KEY), BF16),
        in_specs=[VMEM] * 3,
        out_specs=VMEM,
        compiler_params=params(),
        cost_estimate=cost(COSTS["latent_queries"]),
        name="latent_queries",
    )(q, r, in_vmem(w_key))


def pass_kernel(array_ref, token_ref, out_ref):
    out_ref[...] = array_ref[...]


def after(array, token):
    return pl.pallas_call(
        pass_kernel,
        out_shape=pltpu.VMEM(array.shape, BF16),
        in_specs=[VMEM, ANYWHERE],
        out_specs=VMEM,
        compiler_params=params(),
        cost_estimate=cost(COSTS["pass_on"]),
        name="pass_on",
    )(array, token)


def put_cached(key_buf, first, lat_ref, note_ref):
    slots = lat_ref.shape[0]
    key_buf[first : first + slots, :DC] = lat_ref[...]
    key_buf[first : first + slots, DC:] = masked_rope(note_ref, slots)


def masked_rope(note_ref, slots):
    part = note_ref.shape[0] - GROUP - DR // 2
    lane = part // GROUP * LANES
    live = note_ref[part : part + 1, lane : lane + 1].astype(F32)
    blocked = jnp.where(iota((LANES - DR, slots), 1).astype(F32) < live, 0.0, BLOCKED)
    blocked = jnp.where(iota((LANES - DR, slots), 0) == 0, blocked, 0.0)
    rope = note_ref[part + GROUP :, :].astype(F32)
    return jnp.concatenate([rope[:, :slots], rope[:, slots:], blocked], axis=0).T.astype(BF16)


def put_fresh(key_buf, first, note_refs):
    part = note_refs[0].shape[0] - GROUP - DR // 2
    for index, note_ref in enumerate(note_refs):
        key_buf[first + index * part : first + (index + 1) * part, :DC] = note_ref[:part, :]
        for k in range(part // GROUP):
            rows = span(k, GROUP, first + index * part)
            key_buf[rows, DC:] = note_ref[part : part + GROUP, k * LANES : (k + 1) * LANES]


def causal(part, blocks):
    count = part * blocks
    me = lax.axis_index("ctx")
    col = iota((count, count), 1)
    origin = jnp.bitwise_xor(jnp.full((count, count), me, jnp.int32), col // part)
    return jnp.where(origin * part + col % part <= iota((count, count), 0), 0.0, BLOCKED)


def pipeline(steps, scores, weigh, collect):
    upcoming, previous = scores(0), None
    for step in range(steps):
        now = upcoming
        if step + 1 < steps:
            upcoming = scores(step + 1)
        if previous is not None:
            collect(step - 1, *previous)
        previous = weigh(step, now)
    collect(steps - 1, *previous)


def exponents(s, level, total):
    parts = []
    for k in range(s.shape[1] // LANES):
        p = jnp.exp2((s[:, k * LANES : (k + 1) * LANES] - level) * EXP_SCALE)
        total = p if total is None else total + p
        parts.append(p.astype(BF16))
    return jnp.concatenate(parts, axis=1), total


def state_shapes(rows):
    return (pltpu.VMEM((rows, DV), F32), pltpu.VMEM((rows, LANES), F32), pltpu.VMEM((rows, LANES), F32))


def near_kernel(q_ref, *refs, cached, size):
    w_hbm, out_ref, sum_ref, max_ref, w_ref, key_buf, sem = refs[2 * cached :]
    copy = pltpu.make_async_copy(w_hbm, w_ref, sem)
    copy.start()
    slots = refs[0].shape[0]
    for k in range(cached):
        put_cached(key_buf, k * slots, refs[2 * k], refs[2 * k + 1])
    count = size // HEADS_STEP

    def scores(step):
        return dot_t(q_ref[span(step, size), :], key_buf[...])

    def weigh(step, s):
        level = jnp.max(s, axis=1, keepdims=True)
        p, total = exponents(s, level, None)
        sum_ref[span(step, size), :] = total
        max_ref[span(step, size), :] = jnp.broadcast_to(level, (size, LANES))
        return (p,)

    def collect(step, p):
        mixed = dot(p, key_buf[:, :DC]).astype(BF16)
        if step == 0:
            copy.wait()
        for k in range(HEADS_STEP):
            head = step * HEADS_STEP + k
            out_ref[span(head, count), :] = dot(mixed[span(k, count), :], w_ref[:, span(head, DV)])

    pipeline(q_ref.shape[0] // size, scores, weigh, collect)


def near_pass(q, blocks, w_value, count):
    rows = q.shape[0]
    keys = sum(block[0].shape[0] for block in blocks)
    return pl.pallas_call(
        functools.partial(near_kernel, cached=len(blocks), size=HEADS_STEP * count),
        out_shape=(*state_shapes(rows), pltpu.VMEM(w_value.shape, BF16)),
        in_specs=[VMEM] * (1 + 2 * len(blocks)) + [HBM],
        out_specs=(VMEM, VMEM, VMEM, VMEM),
        scratch_shapes=[pltpu.VMEM((keys, KEY), BF16), pltpu.SemaphoreType.DMA],
        compiler_params=params(),
        cost_estimate=cost(COSTS["near_rows"]),
        name="near_rows",
    )(q, *[array for block in blocks for array in block], in_hbm(w_value))


def early_kernel(q_ref, lat_ref, w_ref, out_ref, value_ref, *, size):
    for step in range(q_ref.shape[0] // size):
        rows = span(step, size)
        out_ref[rows, :] = dot_t(q_ref[rows, :DC], lat_ref[...])
        cols = span(step, HEADS_STEP * DV)
        value_ref[:, cols] = dot(lat_ref[...], w_ref[:, cols]).astype(BF16)


def early_pass(q, lat, w_value, count):
    rows = q.shape[0]
    slots = lat.shape[0]
    return pl.pallas_call(
        functools.partial(early_kernel, size=HEADS_STEP * count),
        out_shape=(pltpu.VMEM((rows, slots), F32), pltpu.VMEM((slots, w_value.shape[1]), BF16)),
        in_specs=[VMEM] * 3,
        out_specs=(VMEM, VMEM),
        compiler_params=params(),
        cost_estimate=cost(COSTS["early"]),
        name="early",
    )(q, lat, w_value)


def far_kernel(
    q_ref,
    note_ref,
    s_ref,
    value_ref,
    out_in,
    sum_in,
    max_in,
    lat_ref,
    w_ref,
    out_ref,
    sum_ref,
    max_ref,
    next_ref,
    ext_buf,
    *,
    size,
):
    ext_buf[...] = masked_rope(note_ref, value_ref.shape[0])
    count = size // HEADS_STEP

    def scores(step):
        rows = span(step, size)
        return s_ref[rows, :] + dot_t(q_ref[rows, DC:], ext_buf[...])

    def weigh(step, s):
        rows = span(step, size)
        before = max_in[rows, :]
        level = jnp.maximum(before, jnp.max(s, axis=1, keepdims=True))
        factor = jnp.exp2((before - level) * EXP_SCALE)
        p, total = exponents(s, level, sum_in[rows, :] * factor)
        sum_ref[rows, :] = total
        max_ref[rows, :] = level
        return p, factor

    def collect(step, p, factor):
        cols = span(step, HEADS_STEP * DV)
        next_ref[:, cols] = dot(lat_ref[...], w_ref[:, cols]).astype(BF16)
        for k in range(HEADS_STEP):
            head = step * HEADS_STEP + k
            grown = dot(p[span(k, count), :], value_ref[:, span(head, DV)])
            out_ref[span(head, count), :] = out_in[span(head, count), :] * factor[span(k, count), :] + grown

    pipeline(q_ref.shape[0] // size, scores, weigh, collect)


def far_pass(q, note, scores, values, state, next_lat, w_value, count):
    rows = q.shape[0]
    return pl.pallas_call(
        functools.partial(far_kernel, size=HEADS_STEP * count),
        out_shape=(*state_shapes(rows), pltpu.VMEM((next_lat.shape[0], w_value.shape[1]), BF16)),
        in_specs=[VMEM] * 9,
        out_specs=(VMEM, VMEM, VMEM, VMEM),
        scratch_shapes=[pltpu.VMEM((values.shape[0], LANES), BF16)],
        compiler_params=params(),
        cost_estimate=cost(COSTS["far_rows"]),
        name="far_rows",
    )(q, note, scores, values, *state, next_lat, w_value)


def last_kernel(q_ref, lat_ref, value_ref, *refs, blocks, size):
    notes, refs = refs[:blocks], refs[blocks:]
    out_in, sum_in, max_in, w_ref, out_hbm, key_buf, out_buf, sems = refs
    slots = lat_ref.shape[0]
    count = out_hbm.shape[0]
    put_cached(key_buf, 0, lat_ref, notes[-1])
    put_fresh(key_buf, slots, notes)
    bias = jnp.concatenate([causal(count // blocks, blocks)] * HEADS_STEP, axis=0)
    copies = []

    def scores(step):
        s = dot_t(q_ref[span(step, size), :], key_buf[...])
        return jnp.concatenate([s[:, :slots], s[:, slots:] + bias], axis=1)

    def weigh(step, s):
        rows = span(step, size)
        before = max_in[rows, :]
        level = jnp.maximum(before, jnp.max(s, axis=1, keepdims=True))
        factor = jnp.exp2((before - level) * EXP_SCALE)
        p, total = exponents(s, level, sum_in[rows, :] * factor)
        inverse = 1.0 / jnp.sum(total, axis=1, keepdims=True)
        return p, factor * inverse, inverse

    def collect(step, p, factor, inverse):
        fresh = dot(key_buf[slots:, :DC], w_ref[:, span(step, HEADS_STEP * DV)]).astype(BF16)
        for k in range(HEADS_STEP):
            head = step * HEADS_STEP + k
            part = span(k, count)
            grown = dot(p[part, :slots], value_ref[:, span(head, DV)]) + dot(p[part, slots:], fresh[:, span(k, DV)])
            whole = out_in[span(head, count), :] * factor[part, :] + grown * inverse[part, :]
            out_buf[:, span(head, DV)] = whole.astype(BF16)
        cols = span(step, HEADS_STEP * DV)
        copies.append(pltpu.make_async_copy(out_buf.at[:, cols], out_hbm.at[:, cols], sems.at[step]))
        copies[-1].start()

    pipeline(q_ref.shape[0] // size, scores, weigh, collect)
    for copy in copies:
        copy.wait()


def last_pass(q, lat, values, notes, state, w_value, count):
    rows = q.shape[0]
    shape = (count, w_value.shape[1])
    return pl.pallas_call(
        functools.partial(last_kernel, blocks=len(notes), size=HEADS_STEP * count),
        out_shape=jax.ShapeDtypeStruct(shape, BF16),
        in_specs=[VMEM] * (7 + len(notes)),
        out_specs=HBM,
        scratch_shapes=[
            pltpu.VMEM((lat.shape[0] + count, KEY), BF16),
            pltpu.VMEM(shape, BF16),
            pltpu.SemaphoreType.DMA((rows // (HEADS_STEP * count),)),
        ],
        compiler_params=params(),
        cost_estimate=cost(COSTS["last_rows"]),
        name="last_rows",
    )(q, lat, values, *notes, *state, w_value)


def hop(array, bit):
    size = lax.axis_size("ctx")
    return lax.ppermute(array, "ctx", [(k, k ^ bit) for k in range(size)])


def shards(q_nope, q_rope, cache_latent, cache_rope, new_latent, new_rope, lengths, w_key, w_value):
    count = q_nope.shape[1]
    lat = cache_latent[0]
    far_lat, near_lat = hop(lat, 2), hop(lat, 1)
    heads = w_key.shape[1] // DH
    note, lat, own_q, own_r = pack(
        new_latent[0], new_rope[0], cache_rope[0].T, lat, q_nope, q_rope, lengths, heads
    )
    near_note = hop(note, 1)
    q = make_queries(own_q, own_r, w_key)
    far_note = hop(after(note, q), 2)
    *state, w_value = near_pass(q, [(lat, note), (near_lat, near_note)], w_value, count)
    last_lat = hop(after(far_lat, state[2]), 1)
    scores, values = early_pass(q, far_lat, w_value, count)
    last_note = hop(after(far_note, scores), 1)
    *state, values = far_pass(q, far_note, scores, values, state, last_lat, w_value, count)
    notes = [note, near_note, far_note, last_note]
    return last_pass(q, last_lat, values, notes, state, w_value, count)[None]


def solution(mesh):
    return jax.shard_map(
        shards,
        mesh=mesh,
        in_specs=(
            P("req", None, None),
            P("req", None, None),
            P("req", "ctx", None),
            P("req", "ctx", None),
            P("req", "ctx", None),
            P("req", "ctx", None),
            P("req", "ctx"),
            P(None, "ctx"),
            P(None, "ctx"),
        ),
        out_specs=P("req", None, "ctx"),
        check_vma=False,
    )
```

time: 18.3 us -> 18 us (0.984)
  waiting for transfers between devices: 0.96 us -> 0.02 us
  Pallas kernels: 12.4 us -> 12.9 us
    pallas_call x1, Pallas kernels: 2.97 us -> 3.94 us  [near_pass(): pl.pallas_call(functools.partial(near_kernel, cached=len(blocks), size=HE...]
    ppermute x6, waiting for transfers between devices: 0.96 us -> 0.02 us  [hop(): return lax.ppermute(array, 'ctx', [(k, k ^ bit) for k in range(size)])]
    pallas_call x1, Pallas kernels: 4.51 us -> 3.68 us  [last_pass(): pl.pallas_call(functools.partial(last_kernel, blocks=len(notes), size=HEA...]
    pallas_call x1, Pallas kernels: 1.51 us -> 1.72 us  [far_pass(): pl.pallas_call(functools.partial(far_kernel, size=HEADS_STEP * count), ou...]
    pallas_call x2 -> x3, Pallas kernels: 3.42 us -> 3.48 us  [the longest x1 1.44 us: pack(): pl.pallas_call(pack_kernel, out_shape=(pltpu.VMEM((part + GROUP + DR // 2...]
  transfers between devices with their start and end apart: 6 -> 6, of which waited for: 2 -> 0; matrix products, arithmetic and copies ran while one was open for 0% -> 0% of each run, Pallas kernels for 44% -> 51%
where the time goes in v4:
time: 18 us; the launch traced here: 17.9 us
  Pallas kernels  12.9 us (72%)
  starting transfers between devices  4.02 us (22%)
  between operations  0.75 us (4%)
  local copies, waits for them, and re-layouts  0.21 us (1%)
    ppermute x6, starting transfers between devices, hop(): return lax.ppermute(array, 'ctx', [(k, k ^ bit) for k in range(size)])  4.02 us
    pallas_call x1, Pallas kernels, near_pass(): pl.pallas_call(functools.partial(near_kernel, cached=len(blocks), size=HE...  3.94 us
    pallas_call x1, Pallas kernels, last_pass(): pl.pallas_call(functools.partial(last_kernel, blocks=len(notes), size=HEA...  3.68 us
    pallas_call x1, Pallas kernels, far_pass(): pl.pallas_call(functools.partial(far_kernel, size=HEADS_STEP * count), ou...  1.72 us
    pallas_call x1, Pallas kernels, pack(): pl.pallas_call(pack_kernel, out_shape=(pltpu.VMEM((part + GROUP + DR // 2...  1.44 us
    pallas_call x1, Pallas kernels, early_pass(): pl.pallas_call(functools.partial(early_kernel, size=HEADS_STEP * count),...  1.26 us
    pallas_call x1, Pallas kernels, make_queries(): pl.pallas_call(queries_kernel, out_shape=pltpu.VMEM((heads * count, KEY),...  0.78 us
  transfers between devices with their start and end apart: 6, of which 0 were waited for; matrix products, arithmetic and copies ran while one was open for 0% of the time, Pallas kernels for 51%

profile of v4, /device:TPU:0, one launch (start us, length us, event | category | flops | bytes accessed | tf_op | source)
XLA Modules:
  0.0 17.9 jit_solution(14940279398163570620)
XLA Ops:
  0.0 0.5 %collective-permute-start.1 = (bf16[256,512]{1,0:T(8,128)(2,1)}, bf16[256,512]{1,0:T(8,128)(2,1)S(1)}, u32[]{:S(2)}, u32[]{:S(2)}) collective-permute-start(bf16[256,512]{1,0:T(8,128)(2,1)} %bitcast.7), channel_id=1, source_target_pairs={{0,1},{1,0},{2,3},{3,2},{4,5},{5,4},{6,7},{7,6},{8,9},{9,8},{10,11... | collective-permute-start | bytes 786440 | tf_op jit(solution)/shard_map/ppermute | solution.py:425
  0.5 2.5 %collective-permute-start = (bf16[256,512]{1,0:T(8,128)(2,1)}, bf16[256,512]{1,0:T(8,128)(2,1)S(1)}, u32[]{:S(2)}, u32[]{:S(2)}) collective-permute-start(bf16[256,512]{1,0:T(8,128)(2,1)} %bitcast.8), channel_id=1, source_target_pairs={{0,2},{1,3},{2,0},{3,1},{4,6},{5,7},{6,4},{7,5},{8,10},{9,11},{10,... | collective-permute-start | bytes 786440 | tf_op jit(solution)/shard_map/ppermute | solution.py:425
  3.6 0.0 copy-start
  3.6 1.4 %pack.1 = (bf16[80,512]{1,0:T(8,128)(2,1)S(1)}, bf16[256,512]{1,0:T(8,128)(2,1)S(1)}, bf16[128,2048]{1,0:T(8,128)(2,1)S(1)}, bf16[128,1024]{1,0:T(8,128)(2,1)S(1)}) custom-call(bf16[32,512]{1,0:T(8,128)(2,1)} %bitcast.10, bf16[32,64]{1,0:T(8,128)(2,1)} %bitcast.12, bf16[64,256]{1,0:T(8,128)(2,1)} %bitcast.11, bf16[256,512]{1,0:T(8,128)(2,1)} %bitcast.9, ...), custom_call_target="tpu_custom_call" | custom-call | flops 5000000000 | bytes 1024 | tf_op jit(solution)/shard_map/pack/pallas_call | solution.py:114
  5.1 0.3 %collective-permute-start.2 = (bf16[80,512]{1,0:T(8,128)(2,1)S(1)}, bf16[80,512]{1,0:T(8,128)(2,1)S(1)}, u32[]{:S(2)}, u32[]{:S(2)}) collective-permute-start(bf16[80,512]{1,0:T(8,128)(2,1)S(1)} %get-tuple-element.22.refs_1_.array_ref.refs_0_), channel_id=1, source_target_pairs={{0,1},{1,0},{2,3},{3,2},{4,5},{5,4},{6,7},{7,6},{8,9},{9,8},{10,11... | collective-permute-start | bytes 245768 | tf_op jit(solution)/shard_map/ppermute | solution.py:425
  5.3 0.2 %copy-done = bf16[512,2048]{1,0:T(8,128)(2,1)S(1)} copy-done((bf16[512,2048]{1,0:T(8,128)(2,1)S(1)}, bf16[512,2048]{1,0:T(8,128)(2,1)}, u32[]{:S(2)}) %copy-start) | copy-done | bytes 2097176
  5.5 0.8 %latent_queries.1.q_ref.token_ref = bf16[2048,640]{1,0:T(8,128)(2,1)S(1)} custom-call(bf16[128,2048]{1,0:T(8,128)(2,1)S(1)} %get-tuple-element.19.q_ref, bf16[128,1024]{1,0:T(8,128)(2,1)S(1)} %get-tuple-element.20.r_ref, bf16[512,2048]{1,0:T(8,128)(2,1)S(1)} %copy-done), custom_call_target="tpu_custom_call" | custom-call | flops 1000000 | bytes 1024 | tf_op jit(solution)/shard_map/latent_queries/pallas_call | solution.py:152
  6.4 0.1 collective-permute-start.4
  6.5 0.0 collective-permute-done.2.refs_3_.refs_1_
  6.5 0.0 collective-permute-done.1.refs_2_
  6.5 3.9 %near_rows.1 = (f32[2048,128]{1,0:T(8,128)S(1)}, f32[2048,128]{1,0:T(8,128)S(1)}, f32[2048,128]{1,0:T(8,128)S(1)}, bf16[512,2048]{1,0:T(8,128)(2,1)S(1)}) custom-call(bf16[2048,640]{1,0:T(8,128)(2,1)S(1)} %latent_queries.1.q_ref.token_ref, bf16[256,512]{1,0:T(8,128)(2,1)S(1)} %get-tuple-element.21.refs_0_, ...), custom_call_target="tpu_custom_call" | custom-call | flops 1000000000 | bytes 1024 | tf_op jit(solution)/shard_map/near_rows/pallas_call | solution.py:270
  10.5 0.0 collective-permute-done.array_ref.lat_ref
  10.5 0.2 %collective-permute-start.3 = (bf16[256,512]{1,0:T(8,128)(2,1)S(1)}, bf16[256,512]{1,0:T(8,128)(2,1)S(1)}, u32[]{:S(2)}, u32[]{:S(2)}) collective-permute-start(bf16[256,512]{1,0:T(8,128)(2,1)S(1)} %pass_on.3), channel_id=1, source_target_pairs={{0,1},{1,0},{2,3},{3,2},{4,5},{5,4},{6,7},{7,6},{8,9},{9,8},{10,11... | collective-permute-start | bytes 786440 | tf_op jit(solution)/shard_map/ppermute | solution.py:425
  10.7 1.3 %early.1 = (f32[2048,256]{1,0:T(8,128)S(1)}, bf16[256,2048]{1,0:T(8,128)(2,1)S(1)}) custom-call(bf16[2048,640]{1,0:T(8,128)(2,1)S(1)} %latent_queries.1.q_ref.token_ref, bf16[256,512]{1,0:T(8,128)(2,1)S(1)} %collective-permute-done.array_ref.lat_ref, bf16[512,2048]{1,0:T(8,128)(2,1)S(1)} %get-tuple-element.24.w_ref.refs_7_), custom_call_target="tpu_custom_call" | custom-call | flops 3000000000 | bytes 1024 | tf_op jit(solution)/shard_map/early/pallas_call | solution.py:293
  12.0 0.0 collective-permute-done.4.note_ref.array_ref.refs_2_
  12.0 0.4 %collective-permute-start.5 = (bf16[80,512]{1,0:T(8,128)(2,1)S(1)}, bf16[80,512]{1,0:T(8,128)(2,1)S(1)}, u32[]{:S(2)}, u32[]{:S(2)}) collective-permute-start(bf16[80,512]{1,0:T(8,128)(2,1)S(1)} %pass_on.5), channel_id=1, source_target_pairs={{0,1},{1,0},{2,3},{3,2},{4,5},{5,4},{6,7},{7,6},{8,9},{9,8},{10,11... | collective-permute-start | bytes 245768 | tf_op jit(solution)/shard_map/ppermute | solution.py:425
  12.4 0.0 collective-permute-done.3.lat_ref
  12.4 1.7 %far_rows.1 = (f32[2048,128]{1,0:T(8,128)S(1)}, f32[2048,128]{1,0:T(8,128)S(1)}, f32[2048,128]{1,0:T(8,128)S(1)}, bf16[256,2048]{1,0:T(8,128)(2,1)S(1)}) custom-call(bf16[2048,640]{1,0:T(8,128)(2,1)S(1)} %latent_queries.1.q_ref.token_ref, bf16[80,512]{1,0:T(8,128)(2,1)S(1)} %collective-permute-done.4.note_ref.array_ref.refs_2_, ...), custom_call_target="tpu_custom_call" | custom-call | flops 3000000000 | bytes 1024 | tf_op jit(solution)/shard_map/far_rows/pallas_call | solution.py:352
  14.2 0.0 collective-permute-done.5.refs_3_
  14.2 3.7 %last_rows.1 = bf16[128,2048]{1,0:T(8,128)(2,1)} custom-call(bf16[2048,640]{1,0:T(8,128)(2,1)S(1)} %latent_queries.1.q_ref.token_ref, bf16[256,512]{1,0:T(8,128)(2,1)S(1)} %collective-permute-done.3.lat_ref, bf16[256,2048]{1,0:T(8,128)(2,1)S(1)} %get-tuple-element.29.value_ref, bf16[80,512]{1,0:T(8,128)(2,1)S(1)} %get-tuple-element.22.refs_1_.array_ref.refs_0_, ...), custom_call_target="tpu_custom_call" | custom-call | flops 1000000 | bytes 1024 | tf_op jit(solution)/shard_map/last_rows/pallas_call | solution.py:407
  (3 shorter events, 0.0 us)
Async XLA Ops:
  0.0 6.5 %collective-permute-start.1 = (bf16[256,512]{1,0:T(8,128)(2,1)}, bf16[256,512]{1,0:T(8,128)(2,1)S(1)}, u32[]{:S(2)}, u32[]{:S(2)}) collective-permute-start(bf16[256,512]{1,0:T(8,128)(2,1)} %bitcast.7), channel_id=1, source_target_pairs={{0,1},{1,0},{2,3},{3,2},{4,5},{5,4},{6,7},{7,6},{8,9},{9,8},{10,11... | collective-permute-start | bytes 786440 | tf_op jit(solution)/shard_map/ppermute | solution.py:425
  0.5 10.0 %collective-permute-start = (bf16[256,512]{1,0:T(8,128)(2,1)}, bf16[256,512]{1,0:T(8,128)(2,1)S(1)}, u32[]{:S(2)}, u32[]{:S(2)}) collective-permute-start(bf16[256,512]{1,0:T(8,128)(2,1)} %bitcast.8), channel_id=1, source_target_pairs={{0,2},{1,3},{2,0},{3,1},{4,6},{5,7},{6,4},{7,5},{8,10},{9,11},{10,... | collective-permute-start | bytes 786440 | tf_op jit(solution)/shard_map/ppermute | solution.py:425
  3.6 2.0 %copy-start = (bf16[512,2048]{1,0:T(8,128)(2,1)S(1)}, bf16[512,2048]{1,0:T(8,128)(2,1)}, u32[]{:S(2)}) copy-start(bf16[512,2048]{1,0:T(8,128)(2,1)} %w_ref.1) | copy-start | bytes 6291460
  5.1 1.4 %collective-permute-start.2 = (bf16[80,512]{1,0:T(8,128)(2,1)S(1)}, bf16[80,512]{1,0:T(8,128)(2,1)S(1)}, u32[]{:S(2)}, u32[]{:S(2)}) collective-permute-start(bf16[80,512]{1,0:T(8,128)(2,1)S(1)} %get-tuple-element.22.refs_1_.array_ref.refs_0_), channel_id=1, source_target_pairs={{0,1},{1,0},{2,3},{3,2},{4,5},{5,4},{6,7},{7,6},{8,9},{9,8},{10,11... | collective-permute-start | bytes 245768 | tf_op jit(solution)/shard_map/ppermute | solution.py:425
  6.4 5.7 %collective-permute-start.4 = (bf16[80,512]{1,0:T(8,128)(2,1)S(1)}, bf16[80,512]{1,0:T(8,128)(2,1)S(1)}, u32[]{:S(2)}, u32[]{:S(2)}) collective-permute-start(bf16[80,512]{1,0:T(8,128)(2,1)S(1)} %pass_on.4), channel_id=1, source_target_pairs={{0,2},{1,3},{2,0},{3,1},{4,6},{5,7},{6,4},{7,5},{8,10},{9,11},{10,... | collective-permute-start | bytes 245768 | tf_op jit(solution)/shard_map/ppermute | solution.py:425
  10.5 1.9 %collective-permute-start.3 = (bf16[256,512]{1,0:T(8,128)(2,1)S(1)}, bf16[256,512]{1,0:T(8,128)(2,1)S(1)}, u32[]{:S(2)}, u32[]{:S(2)}) collective-permute-start(bf16[256,512]{1,0:T(8,128)(2,1)S(1)} %pass_on.3), channel_id=1, source_target_pairs={{0,1},{1,0},{2,3},{3,2},{4,5},{5,4},{6,7},{7,6},{8,9},{9,8},{10,11... | collective-permute-start | bytes 786440 | tf_op jit(solution)/shard_map/ppermute | solution.py:425
  12.0 2.1 %collective-permute-start.5 = (bf16[80,512]{1,0:T(8,128)(2,1)S(1)}, bf16[80,512]{1,0:T(8,128)(2,1)S(1)}, u32[]{:S(2)}, u32[]{:S(2)}) collective-permute-start(bf16[80,512]{1,0:T(8,128)(2,1)S(1)} %pass_on.5), channel_id=1, source_target_pairs={{0,1},{1,0},{2,3},{3,2},{4,5},{5,4},{6,7},{7,6},{8,9},{9,8},{10,11... | collective-permute-start | bytes 245768 | tf_op jit(solution)/shard_map/ppermute | solution.py:425

commit v5 on v4

--- a/solution.py
+++ b/solution.py
@@ -16,9 +16,9 @@
 KEY = DC + LANES
 BLOCKED = -1e30
 EXP_SCALE = math.log2(math.e) / math.sqrt(DH + DR)
-HEADS_STEP = 8
+HEADS_STEP = 4
 GROUP = 16
-COSTS = {"pack": 5.0, "latent_queries": 0.001, "pass_on": 0.001, "near_rows": 1.0, "early": 3.0, "far_rows": 3.0, "last_rows": 0.001}
+COSTS = {"pack": 0.6, "latent_queries": 0.001, "pass_on": 0.001, "near_rows": 1.0, "early": 3.0, "far_rows": 3.0, "last_rows": 0.001}
 VMEM_LIMIT = 20 * 1024 * 1024
 
 
@@ -334,11 +334,11 @@
         p, total = exponents(s, level, sum_in[rows, :] * factor)
         sum_ref[rows, :] = total
         max_ref[rows, :] = level
-        return p, factor
-
-    def collect(step, p, factor):
         cols = span(step, HEADS_STEP * DV)
         next_ref[:, cols] = dot(lat_ref[...], w_ref[:, cols]).astype(BF16)
+        return p, factor
+
+    def collect(step, p, factor):
         for k in range(HEADS_STEP):
             head = step * HEADS_STEP + k
             grown = dot(p[span(k, count), :], value_ref[:, span(head, DV)])
@@ -382,10 +382,10 @@
         factor = jnp.exp2((before - level) * EXP_SCALE)
         p, total = exponents(s, level, sum_in[rows, :] * factor)
         inverse = 1.0 / jnp.sum(total, axis=1, keepdims=True)
-        return p, factor * inverse, inverse
-
-    def collect(step, p, factor, inverse):
         fresh = dot(key_buf[slots:, :DC], w_ref[:, span(step, HEADS_STEP * DV)]).astype(BF16)
+        return p, factor * inverse, inverse, fresh
+
+    def collect(step, p, factor, inverse, fresh):
         for k in range(HEADS_STEP):
             head = step * HEADS_STEP + k
             part = span(k, count)

time: 18 us -> 17.8 us (0.989)
  Pallas kernels: 12.9 us -> 12.5 us
  local copies, waits for them, and re-layouts: 0.21 us -> 0.01 us
    unnamed x2, local copies, waits for them, and re-layouts: 0.21 us -> 0.01 us
  transfers between devices with their start and end apart: 6 -> 6, of which waited for: 0 -> 2; matrix products, arithmetic and copies ran while one was open for 0% -> 0% of each run, Pallas kernels for 51% -> 51%
where the time goes in v5:
time: 17.8 us; the launch traced here: 17.6 us
  Pallas kernels  12.5 us (70%)
  starting transfers between devices  4.16 us (23%)
  between operations  0.72 us (4%)
    ppermute x6, starting transfers between devices, hop(): return lax.ppermute(array, 'ctx', [(k, k ^ bit) for k in range(size)])  4.16 us
    pallas_call x1, Pallas kernels, near_pass(): pl.pallas_call(functools.partial(near_kernel, cached=len(blocks), size=HE...  3.95 us
    pallas_call x1, Pallas kernels, last_pass(): pl.pallas_call(functools.partial(last_kernel, blocks=len(notes), size=HEA...  3.6 us
    pallas_call x1, Pallas kernels, far_pass(): pl.pallas_call(functools.partial(far_kernel, size=HEADS_STEP * count), ou...  1.62 us
    pallas_call x1, Pallas kernels, pack(): pl.pallas_call(pack_kernel, out_shape=(pltpu.VMEM((part + GROUP + DR // 2...  1.3 us
    pallas_call x1, Pallas kernels, early_pass(): pl.pallas_call(functools.partial(early_kernel, size=HEADS_STEP * count),...  1.26 us
    pallas_call x1, Pallas kernels, make_queries(): pl.pallas_call(queries_kernel, out_shape=pltpu.VMEM((heads * count, KEY),...  0.78 us
  transfers between devices with their start and end apart: 6, of which 2 were waited for; matrix products, arithmetic and copies ran while one was open for 0% of the time, Pallas kernels for 51%

profile of v5, /device:TPU:0, one launch (start us, length us, event | category | flops | bytes accessed | tf_op | source)
XLA Modules:
  0.0 17.6 jit_solution(15697259301844210091)
XLA Ops:
  0.0 0.0 copy-start
  0.0 0.5 %collective-permute-start.1 = (bf16[256,512]{1,0:T(8,128)(2,1)}, bf16[256,512]{1,0:T(8,128)(2,1)S(1)}, u32[]{:S(2)}, u32[]{:S(2)}) collective-permute-start(bf16[256,512]{1,0:T(8,128)(2,1)} %bitcast.7), channel_id=1, source_target_pairs={{0,1},{1,0},{2,3},{3,2},{4,5},{5,4},{6,7},{7,6},{8,9},{9,8},{10,11... | collective-permute-start | bytes 786440 | tf_op jit(solution)/shard_map/ppermute | solution.py:425
  0.5 2.5 %collective-permute-start = (bf16[256,512]{1,0:T(8,128)(2,1)}, bf16[256,512]{1,0:T(8,128)(2,1)S(1)}, u32[]{:S(2)}, u32[]{:S(2)}) collective-permute-start(bf16[256,512]{1,0:T(8,128)(2,1)} %bitcast.8), channel_id=1, source_target_pairs={{0,2},{1,3},{2,0},{3,1},{4,6},{5,7},{6,4},{7,5},{8,10},{9,11},{10,... | collective-permute-start | bytes 786440 | tf_op jit(solution)/shard_map/ppermute | solution.py:425
  3.7 1.3 %pack.1 = (bf16[80,512]{1,0:T(8,128)(2,1)S(1)}, bf16[256,512]{1,0:T(8,128)(2,1)S(1)}, bf16[128,2048]{1,0:T(8,128)(2,1)S(1)}, bf16[128,1024]{1,0:T(8,128)(2,1)S(1)}) custom-call(bf16[32,512]{1,0:T(8,128)(2,1)} %bitcast.10, bf16[32,64]{1,0:T(8,128)(2,1)} %bitcast.12, bf16[64,256]{1,0:T(8,128)(2,1)} %bitcast.11, bf16[256,512]{1,0:T(8,128)(2,1)} %bitcast.9, ...), custom_call_target="tpu_custom_call" | custom-call | flops 600000000 | bytes 1024 | tf_op jit(solution)/shard_map/pack/pallas_call | solution.py:114
  5.0 0.2 %collective-permute-start.2 = (bf16[80,512]{1,0:T(8,128)(2,1)S(1)}, bf16[80,512]{1,0:T(8,128)(2,1)S(1)}, u32[]{:S(2)}, u32[]{:S(2)}) collective-permute-start(bf16[80,512]{1,0:T(8,128)(2,1)S(1)} %get-tuple-element.22.refs_1_.array_ref.refs_0_), channel_id=1, source_target_pairs={{0,1},{1,0},{2,3},{3,2},{4,5},{5,4},{6,7},{7,6},{8,9},{9,8},{10,11... | collective-permute-start | bytes 245768 | tf_op jit(solution)/shard_map/ppermute | solution.py:425
  5.2 0.0 copy-done
  5.2 0.8 %latent_queries.1.q_ref.token_ref = bf16[2048,640]{1,0:T(8,128)(2,1)S(1)} custom-call(bf16[128,2048]{1,0:T(8,128)(2,1)S(1)} %get-tuple-element.19.q_ref, bf16[128,1024]{1,0:T(8,128)(2,1)S(1)} %get-tuple-element.20.r_ref, bf16[512,2048]{1,0:T(8,128)(2,1)S(1)} %copy-done), custom_call_target="tpu_custom_call" | custom-call | flops 1000000 | bytes 1024 | tf_op jit(solution)/shard_map/latent_queries/pallas_call | solution.py:152
  6.0 0.3 %collective-permute-start.4 = (bf16[80,512]{1,0:T(8,128)(2,1)S(1)}, bf16[80,512]{1,0:T(8,128)(2,1)S(1)}, u32[]{:S(2)}, u32[]{:S(2)}) collective-permute-start(bf16[80,512]{1,0:T(8,128)(2,1)S(1)} %pass_on.4), channel_id=1, source_target_pairs={{0,2},{1,3},{2,0},{3,1},{4,6},{5,7},{6,4},{7,5},{8,10},{9,11},{10,... | collective-permute-start | bytes 245768 | tf_op jit(solution)/shard_map/ppermute | solution.py:425
  6.3 0.0 collective-permute-done.2.refs_3_.refs_1_
  6.3 0.0 collective-permute-done.1.refs_2_
  6.3 4.0 %near_rows.1 = (f32[2048,128]{1,0:T(8,128)S(1)}, f32[2048,128]{1,0:T(8,128)S(1)}, f32[2048,128]{1,0:T(8,128)S(1)}, bf16[512,2048]{1,0:T(8,128)(2,1)S(1)}) custom-call(bf16[2048,640]{1,0:T(8,128)(2,1)S(1)} %latent_queries.1.q_ref.token_ref, bf16[256,512]{1,0:T(8,128)(2,1)S(1)} %get-tuple-element.21.refs_0_, ...), custom_call_target="tpu_custom_call" | custom-call | flops 1000000000 | bytes 1024 | tf_op jit(solution)/shard_map/near_rows/pallas_call | solution.py:270
  10.3 0.1 collective-permute-done.array_ref.lat_ref
  10.4 0.1 collective-permute-start.3
  10.5 1.3 %early.1 = (f32[2048,256]{1,0:T(8,128)S(1)}, bf16[256,2048]{1,0:T(8,128)(2,1)S(1)}) custom-call(bf16[2048,640]{1,0:T(8,128)(2,1)S(1)} %latent_queries.1.q_ref.token_ref, bf16[256,512]{1,0:T(8,128)(2,1)S(1)} %collective-permute-done.array_ref.lat_ref, bf16[512,2048]{1,0:T(8,128)(2,1)S(1)} %get-tuple-element.24.w_ref.refs_7_), custom_call_target="tpu_custom_call" | custom-call | flops 3000000000 | bytes 1024 | tf_op jit(solution)/shard_map/early/pallas_call | solution.py:293
  11.8 0.1 collective-permute-done.4.note_ref.array_ref.refs_2_
  11.9 0.4 %collective-permute-start.5 = (bf16[80,512]{1,0:T(8,128)(2,1)S(1)}, bf16[80,512]{1,0:T(8,128)(2,1)S(1)}, u32[]{:S(2)}, u32[]{:S(2)}) collective-permute-start(bf16[80,512]{1,0:T(8,128)(2,1)S(1)} %pass_on.5), channel_id=1, source_target_pairs={{0,1},{1,0},{2,3},{3,2},{4,5},{5,4},{6,7},{7,6},{8,9},{9,8},{10,11... | collective-permute-start | bytes 245768 | tf_op jit(solution)/shard_map/ppermute | solution.py:425
  12.3 0.0 collective-permute-done.3.lat_ref
  12.3 1.6 %far_rows.1 = (f32[2048,128]{1,0:T(8,128)S(1)}, f32[2048,128]{1,0:T(8,128)S(1)}, f32[2048,128]{1,0:T(8,128)S(1)}, bf16[256,2048]{1,0:T(8,128)(2,1)S(1)}) custom-call(bf16[2048,640]{1,0:T(8,128)(2,1)S(1)} %latent_queries.1.q_ref.token_ref, bf16[80,512]{1,0:T(8,128)(2,1)S(1)} %collective-permute-done.4.note_ref.array_ref.refs_2_, ...), custom_call_target="tpu_custom_call" | custom-call | flops 3000000000 | bytes 1024 | tf_op jit(solution)/shard_map/far_rows/pallas_call | solution.py:352
  14.0 0.0 collective-permute-done.5.refs_3_
  14.0 3.6 %last_rows.1 = bf16[128,2048]{1,0:T(8,128)(2,1)} custom-call(bf16[2048,640]{1,0:T(8,128)(2,1)S(1)} %latent_queries.1.q_ref.token_ref, bf16[256,512]{1,0:T(8,128)(2,1)S(1)} %collective-permute-done.3.lat_ref, bf16[256,2048]{1,0:T(8,128)(2,1)S(1)} %get-tuple-element.29.value_ref, bf16[80,512]{1,0:T(8,128)(2,1)S(1)} %get-tuple-element.22.refs_1_.array_ref.refs_0_, ...), custom_call_target="tpu_custom_call" | custom-call | flops 1000000 | bytes 1024 | tf_op jit(solution)/shard_map/last_rows/pallas_call | solution.py:407
  (3 shorter events, 0.0 us)
Async XLA Ops:
  0.0 5.2 %copy-start = (bf16[512,2048]{1,0:T(8,128)(2,1)S(1)}, bf16[512,2048]{1,0:T(8,128)(2,1)}, u32[]{:S(2)}) copy-start(bf16[512,2048]{1,0:T(8,128)(2,1)} %w_ref.1) | copy-start | bytes 6291460
  0.0 6.3 %collective-permute-start.1 = (bf16[256,512]{1,0:T(8,128)(2,1)}, bf16[256,512]{1,0:T(8,128)(2,1)S(1)}, u32[]{:S(2)}, u32[]{:S(2)}) collective-permute-start(bf16[256,512]{1,0:T(8,128)(2,1)} %bitcast.7), channel_id=1, source_target_pairs={{0,1},{1,0},{2,3},{3,2},{4,5},{5,4},{6,7},{7,6},{8,9},{9,8},{10,11... | collective-permute-start | bytes 786440 | tf_op jit(solution)/shard_map/ppermute | solution.py:425
  0.5 9.9 %collective-permute-start = (bf16[256,512]{1,0:T(8,128)(2,1)}, bf16[256,512]{1,0:T(8,128)(2,1)S(1)}, u32[]{:S(2)}, u32[]{:S(2)}) collective-permute-start(bf16[256,512]{1,0:T(8,128)(2,1)} %bitcast.8), channel_id=1, source_target_pairs={{0,2},{1,3},{2,0},{3,1},{4,6},{5,7},{6,4},{7,5},{8,10},{9,11},{10,... | collective-permute-start | bytes 786440 | tf_op jit(solution)/shard_map/ppermute | solution.py:425
  5.0 1.4 %collective-permute-start.2 = (bf16[80,512]{1,0:T(8,128)(2,1)S(1)}, bf16[80,512]{1,0:T(8,128)(2,1)S(1)}, u32[]{:S(2)}, u32[]{:S(2)}) collective-permute-start(bf16[80,512]{1,0:T(8,128)(2,1)S(1)} %get-tuple-element.22.refs_1_.array_ref.refs_0_), channel_id=1, source_target_pairs={{0,1},{1,0},{2,3},{3,2},{4,5},{5,4},{6,7},{7,6},{8,9},{9,8},{10,11... | collective-permute-start | bytes 245768 | tf_op jit(solution)/shard_map/ppermute | solution.py:425
  6.0 5.9 %collective-permute-start.4 = (bf16[80,512]{1,0:T(8,128)(2,1)S(1)}, bf16[80,512]{1,0:T(8,128)(2,1)S(1)}, u32[]{:S(2)}, u32[]{:S(2)}) collective-permute-start(bf16[80,512]{1,0:T(8,128)(2,1)S(1)} %pass_on.4), channel_id=1, source_target_pairs={{0,2},{1,3},{2,0},{3,1},{4,6},{5,7},{6,4},{7,5},{8,10},{9,11},{10,... | collective-permute-start | bytes 245768 | tf_op jit(solution)/shard_map/ppermute | solution.py:425
  10.4 1.9 %collective-permute-start.3 = (bf16[256,512]{1,0:T(8,128)(2,1)S(1)}, bf16[256,512]{1,0:T(8,128)(2,1)S(1)}, u32[]{:S(2)}, u32[]{:S(2)}) collective-permute-start(bf16[256,512]{1,0:T(8,128)(2,1)S(1)} %pass_on.3), channel_id=1, source_target_pairs={{0,1},{1,0},{2,3},{3,2},{4,5},{5,4},{6,7},{7,6},{8,9},{9,8},{10,11... | collective-permute-start | bytes 786440 | tf_op jit(solution)/shard_map/ppermute | solution.py:425
  11.9 2.1 %collective-permute-start.5 = (bf16[80,512]{1,0:T(8,128)(2,1)S(1)}, bf16[80,512]{1,0:T(8,128)(2,1)S(1)}, u32[]{:S(2)}, u32[]{:S(2)}) collective-permute-start(bf16[80,512]{1,0:T(8,128)(2,1)S(1)} %pass_on.5), channel_id=1, source_target_pairs={{0,1},{1,0},{2,3},{3,2},{4,5},{5,4},{6,7},{7,6},{8,9},{9,8},{10,11... | collective-permute-start | bytes 245768 | tf_op jit(solution)/shard_map/ppermute | solution.py:425

commit v6 on v5

--- a/solution.py
+++ b/solution.py
@@ -244,7 +244,8 @@
     count = size // HEADS_STEP
 
     def scores(step):
-        return dot_t(q_ref[span(step, size), :], key_buf[...])
+        q = q_ref[span(step, size), :]
+        return jnp.concatenate([dot_t(q, key_buf[span(k, slots), :]) for k in range(cached)], axis=1)
 
     def weigh(step, s):
         level = jnp.max(s, axis=1, keepdims=True)
@@ -366,14 +367,15 @@
     out_in, sum_in, max_in, w_ref, out_hbm, key_buf, out_buf, sems = refs
     slots = lat_ref.shape[0]
     count = out_hbm.shape[0]
+    put_fresh(key_buf, slots, notes)
     put_cached(key_buf, 0, lat_ref, notes[-1])
-    put_fresh(key_buf, slots, notes)
     bias = jnp.concatenate([causal(count // blocks, blocks)] * HEADS_STEP, axis=0)
     copies = []
 
     def scores(step):
-        s = dot_t(q_ref[span(step, size), :], key_buf[...])
-        return jnp.concatenate([s[:, :slots], s[:, slots:] + bias], axis=1)
+        q = q_ref[span(step, size), :]
+        fresh = dot_t(q, key_buf[slots:, :]) + bias
+        return jnp.concatenate([dot_t(q, key_buf[:slots, :]), fresh], axis=1)
 
     def weigh(step, s):
         rows = span(step, size)
@@ -435,7 +437,7 @@
     )
     near_note = hop(note, 1)
     q = make_queries(own_q, own_r, w_key)
-    far_note = hop(after(note, q), 2)
+    far_note = hop(note, 2)
     *state, w_value = near_pass(q, [(lat, note), (near_lat, near_note)], w_value, count)
     last_lat = hop(after(far_lat, state[2]), 1)
     scores, values = early_pass(q, far_lat, w_value, count)

time: 17.8 us -> 17.8 us (level)
  no operation moved by 1% of the time
where the time goes in v6:
time: 17.8 us; the launch traced here: 17.5 us
  Pallas kernels  12.5 us (70%)
  starting transfers between devices  4.1 us (23%)
  between operations  0.71 us (4%)
  waiting for transfers between devices  0.23 us (1%)
    ppermute x6, starting transfers between devices, hop(): return lax.ppermute(array, 'ctx', [(k, k ^ bit) for k in range(size)])  4.1 us
    pallas_call x1, Pallas kernels, near_pass(): pl.pallas_call(functools.partial(near_kernel, cached=len(blocks), size=HE...  3.96 us
    pallas_call x1, Pallas kernels, last_pass(): pl.pallas_call(functools.partial(last_kernel, blocks=len(notes), size=HEA...  3.57 us
    pallas_call x1, Pallas kernels, far_pass(): pl.pallas_call(functools.partial(far_kernel, size=HEADS_STEP * count), ou...  1.62 us
    pallas_call x1, Pallas kernels, pack(): pl.pallas_call(pack_kernel, out_shape=(pltpu.VMEM((part + GROUP + DR // 2...  1.3 us
    pallas_call x1, Pallas kernels, early_pass(): pl.pallas_call(functools.partial(early_kernel, size=HEADS_STEP * count),...  1.26 us
    pallas_call x1, Pallas kernels, make_queries(): pl.pallas_call(queries_kernel, out_shape=pltpu.VMEM((heads * count, KEY),...  0.77 us
  transfers between devices with their start and end apart: 6, of which 2 were waited for; matrix products, arithmetic and copies ran while one was open for 0% of the time, Pallas kernels for 51%

profile of v6, /device:TPU:0, one launch (start us, length us, event | category | flops | bytes accessed | tf_op | source)
XLA Modules:
  0.0 17.5 jit_solution(13775241734628352899)
XLA Ops:
  0.0 0.0 copy-start
  0.0 0.5 %collective-permute-start.1 = (bf16[256,512]{1,0:T(8,128)(2,1)}, bf16[256,512]{1,0:T(8,128)(2,1)S(1)}, u32[]{:S(2)}, u32[]{:S(2)}) collective-permute-start(bf16[256,512]{1,0:T(8,128)(2,1)} %bitcast.7), channel_id=1, source_target_pairs={{0,1},{1,0},{2,3},{3,2},{4,5},{5,4},{6,7},{7,6},{8,9},{9,8},{10,11... | collective-permute-start | bytes 786440 | tf_op jit(solution)/shard_map/ppermute | solution.py:427
  0.5 2.5 %collective-permute-start = (bf16[256,512]{1,0:T(8,128)(2,1)}, bf16[256,512]{1,0:T(8,128)(2,1)S(1)}, u32[]{:S(2)}, u32[]{:S(2)}) collective-permute-start(bf16[256,512]{1,0:T(8,128)(2,1)} %bitcast.8), channel_id=1, source_target_pairs={{0,2},{1,3},{2,0},{3,1},{4,6},{5,7},{6,4},{7,5},{8,10},{9,11},{10,... | collective-permute-start | bytes 786440 | tf_op jit(solution)/shard_map/ppermute | solution.py:427
  3.7 1.3 %pack.1 = (bf16[80,512]{1,0:T(8,128)(2,1)S(1)}, bf16[256,512]{1,0:T(8,128)(2,1)S(1)}, bf16[128,2048]{1,0:T(8,128)(2,1)S(1)}, bf16[128,1024]{1,0:T(8,128)(2,1)S(1)}) custom-call(bf16[32,512]{1,0:T(8,128)(2,1)} %bitcast.10, bf16[32,64]{1,0:T(8,128)(2,1)} %bitcast.12, bf16[64,256]{1,0:T(8,128)(2,1)} %bitcast.11, bf16[256,512]{1,0:T(8,128)(2,1)} %bitcast.9, ...), custom_call_target="tpu_custom_call" | custom-call | flops 600000000 | bytes 1024 | tf_op jit(solution)/shard_map/pack/pallas_call | solution.py:114
  5.0 0.2 %collective-permute-start.2 = (bf16[80,512]{1,0:T(8,128)(2,1)S(1)}, bf16[80,512]{1,0:T(8,128)(2,1)S(1)}, u32[]{:S(2)}, u32[]{:S(2)}) collective-permute-start(bf16[80,512]{1,0:T(8,128)(2,1)S(1)} %get-tuple-element.22.refs_1_.refs_0_), channel_id=1, source_target_pairs={{0,1},{1,0},{2,3},{3,2},{4,5},{5,4},{6,7},{7,6},{8,9},{9,8},{10,11... | collective-permute-start | bytes 245768 | tf_op jit(solution)/shard_map/ppermute | solution.py:427
  5.2 0.3 %collective-permute-start.4 = (bf16[80,512]{1,0:T(8,128)(2,1)S(1)}, bf16[80,512]{1,0:T(8,128)(2,1)S(1)}, u32[]{:S(2)}, u32[]{:S(2)}) collective-permute-start(bf16[80,512]{1,0:T(8,128)(2,1)S(1)} %get-tuple-element.22.refs_1_.refs_0_), channel_id=1, source_target_pairs={{0,2},{1,3},{2,0},{3,1},{4,6},{5,7},{6,4},{7,5},{8,10},{9,11},{10,... | collective-permute-start | bytes 245768 | tf_op jit(solution)/shard_map/ppermute | solution.py:427
  5.5 0.0 copy-done
  5.5 0.8 %latent_queries.1.q_ref = bf16[2048,640]{1,0:T(8,128)(2,1)S(1)} custom-call(bf16[128,2048]{1,0:T(8,128)(2,1)S(1)} %get-tuple-element.19.q_ref, bf16[128,1024]{1,0:T(8,128)(2,1)S(1)} %get-tuple-element.20.r_ref, bf16[512,2048]{1,0:T(8,128)(2,1)S(1)} %copy-done), custom_call_target="tpu_custom_call" | custom-call | flops 1000000 | bytes 1024 | tf_op jit(solution)/shard_map/latent_queries/pallas_call | solution.py:152
  6.3 0.0 collective-permute-done.2.refs_3_.refs_1_
  6.3 0.0 collective-permute-done.1.refs_2_
  6.3 4.0 %near_rows.1 = (f32[2048,128]{1,0:T(8,128)S(1)}, f32[2048,128]{1,0:T(8,128)S(1)}, f32[2048,128]{1,0:T(8,128)S(1)}, bf16[512,2048]{1,0:T(8,128)(2,1)S(1)}) custom-call(bf16[2048,640]{1,0:T(8,128)(2,1)S(1)} %latent_queries.1.q_ref, bf16[256,512]{1,0:T(8,128)(2,1)S(1)} %get-tuple-element.21.refs_0_, bf16[80,512]{1,0:T(8,128)(2,1)S(1)} %get-tuple-element.22.refs_1_.refs_0_, ...), custom_call_target="tpu_custom_call" | custom-call | flops 1000000000 | bytes 1024 | tf_op jit(solution)/shard_map/near_rows/pallas_call | solution.py:271
  10.3 0.1 collective-permute-done.array_ref.lat_ref
  10.4 0.1 collective-permute-start.3
  10.5 1.3 %early.1 = (f32[2048,256]{1,0:T(8,128)S(1)}, bf16[256,2048]{1,0:T(8,128)(2,1)S(1)}) custom-call(bf16[2048,640]{1,0:T(8,128)(2,1)S(1)} %latent_queries.1.q_ref, bf16[256,512]{1,0:T(8,128)(2,1)S(1)} %collective-permute-done.array_ref.lat_ref, bf16[512,2048]{1,0:T(8,128)(2,1)S(1)} %get-tuple-element.24.w_ref.refs_7_), custom_call_target="tpu_custom_call" | custom-call | flops 3000000000 | bytes 1024 | tf_op jit(solution)/shard_map/early/pallas_call | solution.py:294
  11.8 0.1 collective-permute-done.4.note_ref.array_ref.refs_2_
  11.9 0.4 %collective-permute-start.5 = (bf16[80,512]{1,0:T(8,128)(2,1)S(1)}, bf16[80,512]{1,0:T(8,128)(2,1)S(1)}, u32[]{:S(2)}, u32[]{:S(2)}) collective-permute-start(bf16[80,512]{1,0:T(8,128)(2,1)S(1)} %pass_on.3), channel_id=1, source_target_pairs={{0,1},{1,0},{2,3},{3,2},{4,5},{5,4},{6,7},{7,6},{8,9},{9,8},{10,11... | collective-permute-start | bytes 245768 | tf_op jit(solution)/shard_map/ppermute | solution.py:427
  12.3 0.0 collective-permute-done.3.lat_ref
  12.3 1.6 %far_rows.1 = (f32[2048,128]{1,0:T(8,128)S(1)}, f32[2048,128]{1,0:T(8,128)S(1)}, f32[2048,128]{1,0:T(8,128)S(1)}, bf16[256,2048]{1,0:T(8,128)(2,1)S(1)}) custom-call(bf16[2048,640]{1,0:T(8,128)(2,1)S(1)} %latent_queries.1.q_ref, bf16[80,512]{1,0:T(8,128)(2,1)S(1)} %collective-permute-done.4.note_ref.array_ref.refs_2_, ...), custom_call_target="tpu_custom_call" | custom-call | flops 3000000000 | bytes 1024 | tf_op jit(solution)/shard_map/far_rows/pallas_call | solution.py:353
  14.0 0.0 collective-permute-done.5.refs_3_
  14.0 3.6 %last_rows.1 = bf16[128,2048]{1,0:T(8,128)(2,1)} custom-call(bf16[2048,640]{1,0:T(8,128)(2,1)S(1)} %latent_queries.1.q_ref, bf16[256,512]{1,0:T(8,128)(2,1)S(1)} %collective-permute-done.3.lat_ref, bf16[256,2048]{1,0:T(8,128)(2,1)S(1)} %get-tuple-element.29.value_ref, bf16[80,512]{1,0:T(8,128)(2,1)S(1)} %get-tuple-element.22.refs_1_.refs_0_, ...), custom_call_target="tpu_custom_call" | custom-call | flops 1000000 | bytes 1024 | tf_op jit(solution)/shard_map/last_rows/pallas_call | solution.py:409
  (2 shorter events, 0.0 us)
Async XLA Ops:
  0.0 5.5 %copy-start = (bf16[512,2048]{1,0:T(8,128)(2,1)S(1)}, bf16[512,2048]{1,0:T(8,128)(2,1)}, u32[]{:S(2)}) copy-start(bf16[512,2048]{1,0:T(8,128)(2,1)} %w_ref.1) | copy-start | bytes 6291460
  0.0 6.3 %collective-permute-start.1 = (bf16[256,512]{1,0:T(8,128)(2,1)}, bf16[256,512]{1,0:T(8,128)(2,1)S(1)}, u32[]{:S(2)}, u32[]{:S(2)}) collective-permute-start(bf16[256,512]{1,0:T(8,128)(2,1)} %bitcast.7), channel_id=1, source_target_pairs={{0,1},{1,0},{2,3},{3,2},{4,5},{5,4},{6,7},{7,6},{8,9},{9,8},{10,11... | collective-permute-start | bytes 786440 | tf_op jit(solution)/shard_map/ppermute | solution.py:427
  0.5 9.9 %collective-permute-start = (bf16[256,512]{1,0:T(8,128)(2,1)}, bf16[256,512]{1,0:T(8,128)(2,1)S(1)}, u32[]{:S(2)}, u32[]{:S(2)}) collective-permute-start(bf16[256,512]{1,0:T(8,128)(2,1)} %bitcast.8), channel_id=1, source_target_pairs={{0,2},{1,3},{2,0},{3,1},{4,6},{5,7},{6,4},{7,5},{8,10},{9,11},{10,... | collective-permute-start | bytes 786440 | tf_op jit(solution)/shard_map/ppermute | solution.py:427
  5.0 1.3 %collective-permute-start.2 = (bf16[80,512]{1,0:T(8,128)(2,1)S(1)}, bf16[80,512]{1,0:T(8,128)(2,1)S(1)}, u32[]{:S(2)}, u32[]{:S(2)}) collective-permute-start(bf16[80,512]{1,0:T(8,128)(2,1)S(1)} %get-tuple-element.22.refs_1_.refs_0_), channel_id=1, source_target_pairs={{0,1},{1,0},{2,3},{3,2},{4,5},{5,4},{6,7},{7,6},{8,9},{9,8},{10,11... | collective-permute-start | bytes 245768 | tf_op jit(solution)/shard_map/ppermute | solution.py:427
  5.2 6.7 %collective-permute-start.4 = (bf16[80,512]{1,0:T(8,128)(2,1)S(1)}, bf16[80,512]{1,0:T(8,128)(2,1)S(1)}, u32[]{:S(2)}, u32[]{:S(2)}) collective-permute-start(bf16[80,512]{1,0:T(8,128)(2,1)S(1)} %get-tuple-element.22.refs_1_.refs_0_), channel_id=1, source_target_pairs={{0,2},{1,3},{2,0},{3,1},{4,6},{5,7},{6,4},{7,5},{8,10},{9,11},{10,... | collective-permute-start | bytes 245768 | tf_op jit(solution)/shard_map/ppermute | solution.py:427
  10.4 1.9 %collective-permute-start.3 = (bf16[256,512]{1,0:T(8,128)(2,1)S(1)}, bf16[256,512]{1,0:T(8,128)(2,1)S(1)}, u32[]{:S(2)}, u32[]{:S(2)}) collective-permute-start(bf16[256,512]{1,0:T(8,128)(2,1)S(1)} %pass_on.2), channel_id=1, source_target_pairs={{0,1},{1,0},{2,3},{3,2},{4,5},{5,4},{6,7},{7,6},{8,9},{9,8},{10,11... | collective-permute-start | bytes 786440 | tf_op jit(solution)/shard_map/ppermute | solution.py:427
  11.9 2.1 %collective-permute-start.5 = (bf16[80,512]{1,0:T(8,128)(2,1)S(1)}, bf16[80,512]{1,0:T(8,128)(2,1)S(1)}, u32[]{:S(2)}, u32[]{:S(2)}) collective-permute-start(bf16[80,512]{1,0:T(8,128)(2,1)S(1)} %pass_on.3), channel_id=1, source_target_pairs={{0,1},{1,0},{2,3},{3,2},{4,5},{5,4},{6,7},{7,6},{8,9},{9,8},{10,11... | collective-permute-start | bytes 245768 | tf_op jit(solution)/shard_map/ppermute | solution.py:427

commit v7 on v6

--- a/solution.py
+++ b/solution.py
@@ -17,6 +17,7 @@
 BLOCKED = -1e30
 EXP_SCALE = math.log2(math.e) / math.sqrt(DH + DR)
 HEADS_STEP = 4
+HEADS_LAST = 8
 GROUP = 16
 COSTS = {"pack": 0.6, "latent_queries": 0.001, "pass_on": 0.001, "near_rows": 1.0, "early": 3.0, "far_rows": 3.0, "last_rows": 0.001}
 VMEM_LIMIT = 20 * 1024 * 1024
@@ -369,7 +370,7 @@
     count = out_hbm.shape[0]
     put_fresh(key_buf, slots, notes)
     put_cached(key_buf, 0, lat_ref, notes[-1])
-    bias = jnp.concatenate([causal(count // blocks, blocks)] * HEADS_STEP, axis=0)
+    bias = jnp.concatenate([causal(count // blocks, blocks)] * HEADS_LAST, axis=0)
     copies = []
 
     def scores(step):
@@ -384,17 +385,17 @@
         factor = jnp.exp2((before - level) * EXP_SCALE)
         p, total = exponents(s, level, sum_in[rows, :] * factor)
         inverse = 1.0 / jnp.sum(total, axis=1, keepdims=True)
-        fresh = dot(key_buf[slots:, :DC], w_ref[:, span(step, HEADS_STEP * DV)]).astype(BF16)
+        fresh = dot(key_buf[slots:, :DC], w_ref[:, span(step, HEADS_LAST * DV)]).astype(BF16)
         return p, factor * inverse, inverse, fresh
 
     def collect(step, p, factor, inverse, fresh):
-        for k in range(HEADS_STEP):
-            head = step * HEADS_STEP + k
+        for k in range(HEADS_LAST):
+            head = step * HEADS_LAST + k
             part = span(k, count)
             grown = dot(p[part, :slots], value_ref[:, span(head, DV)]) + dot(p[part, slots:], fresh[:, span(k, DV)])
             whole = out_in[span(head, count), :] * factor[part, :] + grown * inverse[part, :]
             out_buf[:, span(head, DV)] = whole.astype(BF16)
-        cols = span(step, HEADS_STEP * DV)
+        cols = span(step, HEADS_LAST * DV)
         copies.append(pltpu.make_async_copy(out_buf.at[:, cols], out_hbm.at[:, cols], sems.at[step]))
         copies[-1].start()
 
@@ -407,14 +408,14 @@
     rows = q.shape[0]
     shape = (count, w_value.shape[1])
     return pl.pallas_call(
-        functools.partial(last_kernel, blocks=len(notes), size=HEADS_STEP * count),
+        functools.partial(last_kernel, blocks=len(notes), size=HEADS_LAST * count),
         out_shape=jax.ShapeDtypeStruct(shape, BF16),
         in_specs=[VMEM] * (7 + len(notes)),
         out_specs=HBM,
         scratch_shapes=[
             pltpu.VMEM((lat.shape[0] + count, KEY), BF16),
             pltpu.VMEM(shape, BF16),
-            pltpu.SemaphoreType.DMA((rows // (HEADS_STEP * count),)),
+            pltpu.SemaphoreType.DMA((rows // (HEADS_LAST * count),)),
         ],
         compiler_params=params(),
         cost_estimate=cost(COSTS["last_rows"]),

time: 17.8 us -> 17.7 us (level)
  no operation moved by 1% of the time
where the time goes in v7:
time: 17.7 us; the launch traced here: 17.5 us
  Pallas kernels  12.4 us (70%)
  starting transfers between devices  4.1 us (23%)
  between operations  0.71 us (4%)
  waiting for transfers between devices  0.23 us (1%)
    ppermute x6, starting transfers between devices, hop(): return lax.ppermute(array, 'ctx', [(k, k ^ bit) for k in range(size)])  4.1 us
    pallas_call x1, Pallas kernels, near_pass(): pl.pallas_call(functools.partial(near_kernel, cached=len(blocks), size=HE...  3.96 us
    pallas_call x1, Pallas kernels, last_pass(): pl.pallas_call(functools.partial(last_kernel, blocks=len(notes), size=HEA...  3.51 us
    pallas_call x1, Pallas kernels, far_pass(): pl.pallas_call(functools.partial(far_kernel, size=HEADS_STEP * count), ou...  1.62 us
    pallas_call x1, Pallas kernels, pack(): pl.pallas_call(pack_kernel, out_shape=(pltpu.VMEM((part + GROUP + DR // 2...  1.3 us
    pallas_call x1, Pallas kernels, early_pass(): pl.pallas_call(functools.partial(early_kernel, size=HEADS_STEP * count),...  1.26 us
    pallas_call x1, Pallas kernels, make_queries(): pl.pallas_call(queries_kernel, out_shape=pltpu.VMEM((heads * count, KEY),...  0.77 us
  transfers between devices with their start and end apart: 6, of which 2 were waited for; matrix products, arithmetic and copies ran while one was open for 0% of the time, Pallas kernels for 51%

profile of v7, /device:TPU:0, one launch (start us, length us, event | category | flops | bytes accessed | tf_op | source)
XLA Modules:
  0.0 17.5 jit_solution(6991955603472864780)
XLA Ops:
  0.0 0.0 copy-start
  0.0 0.5 %collective-permute-start.1 = (bf16[256,512]{1,0:T(8,128)(2,1)}, bf16[256,512]{1,0:T(8,128)(2,1)S(1)}, u32[]{:S(2)}, u32[]{:S(2)}) collective-permute-start(bf16[256,512]{1,0:T(8,128)(2,1)} %bitcast.7), channel_id=1, source_target_pairs={{0,1},{1,0},{2,3},{3,2},{4,5},{5,4},{6,7},{7,6},{8,9},{9,8},{10,11... | collective-permute-start | bytes 786440 | tf_op jit(solution)/shard_map/ppermute | solution.py:428
  0.5 2.5 %collective-permute-start = (bf16[256,512]{1,0:T(8,128)(2,1)}, bf16[256,512]{1,0:T(8,128)(2,1)S(1)}, u32[]{:S(2)}, u32[]{:S(2)}) collective-permute-start(bf16[256,512]{1,0:T(8,128)(2,1)} %bitcast.8), channel_id=1, source_target_pairs={{0,2},{1,3},{2,0},{3,1},{4,6},{5,7},{6,4},{7,5},{8,10},{9,11},{10,... | collective-permute-start | bytes 786440 | tf_op jit(solution)/shard_map/ppermute | solution.py:428
  3.7 1.3 %pack.1 = (bf16[80,512]{1,0:T(8,128)(2,1)S(1)}, bf16[256,512]{1,0:T(8,128)(2,1)S(1)}, bf16[128,2048]{1,0:T(8,128)(2,1)S(1)}, bf16[128,1024]{1,0:T(8,128)(2,1)S(1)}) custom-call(bf16[32,512]{1,0:T(8,128)(2,1)} %bitcast.10, bf16[32,64]{1,0:T(8,128)(2,1)} %bitcast.12, bf16[64,256]{1,0:T(8,128)(2,1)} %bitcast.11, bf16[256,512]{1,0:T(8,128)(2,1)} %bitcast.9, ...), custom_call_target="tpu_custom_call" | custom-call | flops 600000000 | bytes 1024 | tf_op jit(solution)/shard_map/pack/pallas_call | solution.py:115
  5.0 0.2 %collective-permute-start.2 = (bf16[80,512]{1,0:T(8,128)(2,1)S(1)}, bf16[80,512]{1,0:T(8,128)(2,1)S(1)}, u32[]{:S(2)}, u32[]{:S(2)}) collective-permute-start(bf16[80,512]{1,0:T(8,128)(2,1)S(1)} %get-tuple-element.22.refs_1_.refs_0_), channel_id=1, source_target_pairs={{0,1},{1,0},{2,3},{3,2},{4,5},{5,4},{6,7},{7,6},{8,9},{9,8},{10,11... | collective-permute-start | bytes 245768 | tf_op jit(solution)/shard_map/ppermute | solution.py:428
  5.2 0.3 %collective-permute-start.4 = (bf16[80,512]{1,0:T(8,128)(2,1)S(1)}, bf16[80,512]{1,0:T(8,128)(2,1)S(1)}, u32[]{:S(2)}, u32[]{:S(2)}) collective-permute-start(bf16[80,512]{1,0:T(8,128)(2,1)S(1)} %get-tuple-element.22.refs_1_.refs_0_), channel_id=1, source_target_pairs={{0,2},{1,3},{2,0},{3,1},{4,6},{5,7},{6,4},{7,5},{8,10},{9,11},{10,... | collective-permute-start | bytes 245768 | tf_op jit(solution)/shard_map/ppermute | solution.py:428
  5.5 0.0 copy-done
  5.5 0.8 %latent_queries.1.q_ref = bf16[2048,640]{1,0:T(8,128)(2,1)S(1)} custom-call(bf16[128,2048]{1,0:T(8,128)(2,1)S(1)} %get-tuple-element.19.q_ref, bf16[128,1024]{1,0:T(8,128)(2,1)S(1)} %get-tuple-element.20.r_ref, bf16[512,2048]{1,0:T(8,128)(2,1)S(1)} %copy-done), custom_call_target="tpu_custom_call" | custom-call | flops 1000000 | bytes 1024 | tf_op jit(solution)/shard_map/latent_queries/pallas_call | solution.py:153
  6.3 0.0 collective-permute-done.2.refs_3_.refs_1_
  6.3 0.0 collective-permute-done.1.refs_2_
  6.3 4.0 %near_rows.1 = (f32[2048,128]{1,0:T(8,128)S(1)}, f32[2048,128]{1,0:T(8,128)S(1)}, f32[2048,128]{1,0:T(8,128)S(1)}, bf16[512,2048]{1,0:T(8,128)(2,1)S(1)}) custom-call(bf16[2048,640]{1,0:T(8,128)(2,1)S(1)} %latent_queries.1.q_ref, bf16[256,512]{1,0:T(8,128)(2,1)S(1)} %get-tuple-element.21.refs_0_, bf16[80,512]{1,0:T(8,128)(2,1)S(1)} %get-tuple-element.22.refs_1_.refs_0_, ...), custom_call_target="tpu_custom_call" | custom-call | flops 1000000000 | bytes 1024 | tf_op jit(solution)/shard_map/near_rows/pallas_call | solution.py:272
  10.3 0.1 collective-permute-done.array_ref.lat_ref
  10.4 0.1 collective-permute-start.3
  10.5 1.3 %early.1 = (f32[2048,256]{1,0:T(8,128)S(1)}, bf16[256,2048]{1,0:T(8,128)(2,1)S(1)}) custom-call(bf16[2048,640]{1,0:T(8,128)(2,1)S(1)} %latent_queries.1.q_ref, bf16[256,512]{1,0:T(8,128)(2,1)S(1)} %collective-permute-done.array_ref.lat_ref, bf16[512,2048]{1,0:T(8,128)(2,1)S(1)} %get-tuple-element.24.w_ref.refs_7_), custom_call_target="tpu_custom_call" | custom-call | flops 3000000000 | bytes 1024 | tf_op jit(solution)/shard_map/early/pallas_call | solution.py:295
  11.8 0.1 collective-permute-done.4.note_ref.array_ref.refs_2_
  11.9 0.4 %collective-permute-start.5 = (bf16[80,512]{1,0:T(8,128)(2,1)S(1)}, bf16[80,512]{1,0:T(8,128)(2,1)S(1)}, u32[]{:S(2)}, u32[]{:S(2)}) collective-permute-start(bf16[80,512]{1,0:T(8,128)(2,1)S(1)} %pass_on.3), channel_id=1, source_target_pairs={{0,1},{1,0},{2,3},{3,2},{4,5},{5,4},{6,7},{7,6},{8,9},{9,8},{10,11... | collective-permute-start | bytes 245768 | tf_op jit(solution)/shard_map/ppermute | solution.py:428
  12.3 0.0 collective-permute-done.3.lat_ref
  12.3 1.6 %far_rows.1 = (f32[2048,128]{1,0:T(8,128)S(1)}, f32[2048,128]{1,0:T(8,128)S(1)}, f32[2048,128]{1,0:T(8,128)S(1)}, bf16[256,2048]{1,0:T(8,128)(2,1)S(1)}) custom-call(bf16[2048,640]{1,0:T(8,128)(2,1)S(1)} %latent_queries.1.q_ref, bf16[80,512]{1,0:T(8,128)(2,1)S(1)} %collective-permute-done.4.note_ref.array_ref.refs_2_, ...), custom_call_target="tpu_custom_call" | custom-call | flops 3000000000 | bytes 1024 | tf_op jit(solution)/shard_map/far_rows/pallas_call | solution.py:354
  14.0 0.0 collective-permute-done.5.refs_3_
  14.0 3.5 %last_rows.1 = bf16[128,2048]{1,0:T(8,128)(2,1)} custom-call(bf16[2048,640]{1,0:T(8,128)(2,1)S(1)} %latent_queries.1.q_ref, bf16[256,512]{1,0:T(8,128)(2,1)S(1)} %collective-permute-done.3.lat_ref, bf16[256,2048]{1,0:T(8,128)(2,1)S(1)} %get-tuple-element.29.value_ref, bf16[80,512]{1,0:T(8,128)(2,1)S(1)} %get-tuple-element.22.refs_1_.refs_0_, ...), custom_call_target="tpu_custom_call" | custom-call | flops 1000000 | bytes 1024 | tf_op jit(solution)/shard_map/last_rows/pallas_call | solution.py:410
  (2 shorter events, 0.0 us)
Async XLA Ops:
  0.0 5.5 %copy-start = (bf16[512,2048]{1,0:T(8,128)(2,1)S(1)}, bf16[512,2048]{1,0:T(8,128)(2,1)}, u32[]{:S(2)}) copy-start(bf16[512,2048]{1,0:T(8,128)(2,1)} %w_ref.1) | copy-start | bytes 6291460
  0.0 6.3 %collective-permute-start.1 = (bf16[256,512]{1,0:T(8,128)(2,1)}, bf16[256,512]{1,0:T(8,128)(2,1)S(1)}, u32[]{:S(2)}, u32[]{:S(2)}) collective-permute-start(bf16[256,512]{1,0:T(8,128)(2,1)} %bitcast.7), channel_id=1, source_target_pairs={{0,1},{1,0},{2,3},{3,2},{4,5},{5,4},{6,7},{7,6},{8,9},{9,8},{10,11... | collective-permute-start | bytes 786440 | tf_op jit(solution)/shard_map/ppermute | solution.py:428
  0.5 9.9 %collective-permute-start = (bf16[256,512]{1,0:T(8,128)(2,1)}, bf16[256,512]{1,0:T(8,128)(2,1)S(1)}, u32[]{:S(2)}, u32[]{:S(2)}) collective-permute-start(bf16[256,512]{1,0:T(8,128)(2,1)} %bitcast.8), channel_id=1, source_target_pairs={{0,2},{1,3},{2,0},{3,1},{4,6},{5,7},{6,4},{7,5},{8,10},{9,11},{10,... | collective-permute-start | bytes 786440 | tf_op jit(solution)/shard_map/ppermute | solution.py:428
  5.0 1.3 %collective-permute-start.2 = (bf16[80,512]{1,0:T(8,128)(2,1)S(1)}, bf16[80,512]{1,0:T(8,128)(2,1)S(1)}, u32[]{:S(2)}, u32[]{:S(2)}) collective-permute-start(bf16[80,512]{1,0:T(8,128)(2,1)S(1)} %get-tuple-element.22.refs_1_.refs_0_), channel_id=1, source_target_pairs={{0,1},{1,0},{2,3},{3,2},{4,5},{5,4},{6,7},{7,6},{8,9},{9,8},{10,11... | collective-permute-start | bytes 245768 | tf_op jit(solution)/shard_map/ppermute | solution.py:428
  5.2 6.7 %collective-permute-start.4 = (bf16[80,512]{1,0:T(8,128)(2,1)S(1)}, bf16[80,512]{1,0:T(8,128)(2,1)S(1)}, u32[]{:S(2)}, u32[]{:S(2)}) collective-permute-start(bf16[80,512]{1,0:T(8,128)(2,1)S(1)} %get-tuple-element.22.refs_1_.refs_0_), channel_id=1, source_target_pairs={{0,2},{1,3},{2,0},{3,1},{4,6},{5,7},{6,4},{7,5},{8,10},{9,11},{10,... | collective-permute-start | bytes 245768 | tf_op jit(solution)/shard_map/ppermute | solution.py:428
  10.4 1.9 %collective-permute-start.3 = (bf16[256,512]{1,0:T(8,128)(2,1)S(1)}, bf16[256,512]{1,0:T(8,128)(2,1)S(1)}, u32[]{:S(2)}, u32[]{:S(2)}) collective-permute-start(bf16[256,512]{1,0:T(8,128)(2,1)S(1)} %pass_on.2), channel_id=1, source_target_pairs={{0,1},{1,0},{2,3},{3,2},{4,5},{5,4},{6,7},{7,6},{8,9},{9,8},{10,11... | collective-permute-start | bytes 786440 | tf_op jit(solution)/shard_map/ppermute | solution.py:428
  11.9 2.1 %collective-permute-start.5 = (bf16[80,512]{1,0:T(8,128)(2,1)S(1)}, bf16[80,512]{1,0:T(8,128)(2,1)S(1)}, u32[]{:S(2)}, u32[]{:S(2)}) collective-permute-start(bf16[80,512]{1,0:T(8,128)(2,1)S(1)} %pass_on.3), channel_id=1, source_target_pairs={{0,1},{1,0},{2,3},{3,2},{4,5},{5,4},{6,7},{7,6},{8,9},{9,8},{10,11... | collective-permute-start | bytes 245768 | tf_op jit(solution)/shard_map/ppermute | solution.py:428

commit v8 on v7

--- a/solution.py
+++ b/solution.py
@@ -18,6 +18,7 @@
 EXP_SCALE = math.log2(math.e) / math.sqrt(DH + DR)
 HEADS_STEP = 4
 HEADS_LAST = 8
+HEADS_SENT = 2
 GROUP = 16
 COSTS = {"pack": 0.6, "latent_queries": 0.001, "pass_on": 0.001, "near_rows": 1.0, "early": 3.0, "far_rows": 3.0, "last_rows": 0.001}
 VMEM_LIMIT = 20 * 1024 * 1024
@@ -395,9 +396,11 @@
             grown = dot(p[part, :slots], value_ref[:, span(head, DV)]) + dot(p[part, slots:], fresh[:, span(k, DV)])
             whole = out_in[span(head, count), :] * factor[part, :] + grown * inverse[part, :]
             out_buf[:, span(head, DV)] = whole.astype(BF16)
-        cols = span(step, HEADS_LAST * DV)
-        copies.append(pltpu.make_async_copy(out_buf.at[:, cols], out_hbm.at[:, cols], sems.at[step]))
-        copies[-1].start()
+            if head % HEADS_SENT == HEADS_SENT - 1:
+                piece = head // HEADS_SENT
+                cols = span(piece, HEADS_SENT * DV)
+                copies.append(pltpu.make_async_copy(out_buf.at[:, cols], out_hbm.at[:, cols], sems.at[piece]))
+                copies[-1].start()
 
     pipeline(q_ref.shape[0] // size, scores, weigh, collect)
     for copy in copies:
@@ -415,7 +418,7 @@
         scratch_shapes=[
             pltpu.VMEM((lat.shape[0] + count, KEY), BF16),
             pltpu.VMEM(shape, BF16),
-            pltpu.SemaphoreType.DMA((rows // (HEADS_LAST * count),)),
+            pltpu.SemaphoreType.DMA((rows // (HEADS_SENT * count),)),
         ],
         compiler_params=params(),
         cost_estimate=cost(COSTS["last_rows"]),

time: 17.7 us -> 17.7 us (level)
  no operation moved by 1% of the time
where the time goes in v8:
time: 17.7 us; the launch traced here: 17.5 us
  Pallas kernels  12.4 us (70%)
  starting transfers between devices  4.1 us (23%)
  between operations  0.71 us (4%)
  waiting for transfers between devices  0.23 us (1%)
    ppermute x6, starting transfers between devices, hop(): return lax.ppermute(array, 'ctx', [(k, k ^ bit) for k in range(size)])  4.1 us
    pallas_call x1, Pallas kernels, near_pass(): pl.pallas_call(functools.partial(near_kernel, cached=len(blocks), size=HE...  3.96 us
    pallas_call x1, Pallas kernels, last_pass(): pl.pallas_call(functools.partial(last_kernel, blocks=len(notes), size=HEA...  3.49 us
    pallas_call x1, Pallas kernels, far_pass(): pl.pallas_call(functools.partial(far_kernel, size=HEADS_STEP * count), ou...  1.62 us
    pallas_call x1, Pallas kernels, pack(): pl.pallas_call(pack_kernel, out_shape=(pltpu.VMEM((part + GROUP + DR // 2...  1.3 us
    pallas_call x1, Pallas kernels, early_pass(): pl.pallas_call(functools.partial(early_kernel, size=HEADS_STEP * count),...  1.26 us
    pallas_call x1, Pallas kernels, make_queries(): pl.pallas_call(queries_kernel, out_shape=pltpu.VMEM((heads * count, KEY),...  0.77 us
  transfers between devices with their start and end apart: 6, of which 2 were waited for; matrix products, arithmetic and copies ran while one was open for 0% of the time, Pallas kernels for 51%

profile of v8, /device:TPU:0, one launch (start us, length us, event | category | flops | bytes accessed | tf_op | source)
XLA Modules:
  0.0 17.5 jit_solution(7481301504671630400)
XLA Ops:
  0.0 0.0 copy-start
  0.0 0.5 %collective-permute-start.1 = (bf16[256,512]{1,0:T(8,128)(2,1)}, bf16[256,512]{1,0:T(8,128)(2,1)S(1)}, u32[]{:S(2)}, u32[]{:S(2)}) collective-permute-start(bf16[256,512]{1,0:T(8,128)(2,1)} %bitcast.7), channel_id=1, source_target_pairs={{0,1},{1,0},{2,3},{3,2},{4,5},{5,4},{6,7},{7,6},{8,9},{9,8},{10,11... | collective-permute-start | bytes 786440 | tf_op jit(solution)/shard_map/ppermute | solution.py:431
  0.5 2.5 %collective-permute-start = (bf16[256,512]{1,0:T(8,128)(2,1)}, bf16[256,512]{1,0:T(8,128)(2,1)S(1)}, u32[]{:S(2)}, u32[]{:S(2)}) collective-permute-start(bf16[256,512]{1,0:T(8,128)(2,1)} %bitcast.8), channel_id=1, source_target_pairs={{0,2},{1,3},{2,0},{3,1},{4,6},{5,7},{6,4},{7,5},{8,10},{9,11},{10,... | collective-permute-start | bytes 786440 | tf_op jit(solution)/shard_map/ppermute | solution.py:431
  3.7 1.3 %pack.1 = (bf16[80,512]{1,0:T(8,128)(2,1)S(1)}, bf16[256,512]{1,0:T(8,128)(2,1)S(1)}, bf16[128,2048]{1,0:T(8,128)(2,1)S(1)}, bf16[128,1024]{1,0:T(8,128)(2,1)S(1)}) custom-call(bf16[32,512]{1,0:T(8,128)(2,1)} %bitcast.10, bf16[32,64]{1,0:T(8,128)(2,1)} %bitcast.12, bf16[64,256]{1,0:T(8,128)(2,1)} %bitcast.11, bf16[256,512]{1,0:T(8,128)(2,1)} %bitcast.9, ...), custom_call_target="tpu_custom_call" | custom-call | flops 600000000 | bytes 1024 | tf_op jit(solution)/shard_map/pack/pallas_call | solution.py:116
  5.0 0.2 %collective-permute-start.2 = (bf16[80,512]{1,0:T(8,128)(2,1)S(1)}, bf16[80,512]{1,0:T(8,128)(2,1)S(1)}, u32[]{:S(2)}, u32[]{:S(2)}) collective-permute-start(bf16[80,512]{1,0:T(8,128)(2,1)S(1)} %get-tuple-element.22.refs_1_.refs_0_), channel_id=1, source_target_pairs={{0,1},{1,0},{2,3},{3,2},{4,5},{5,4},{6,7},{7,6},{8,9},{9,8},{10,11... | collective-permute-start | bytes 245768 | tf_op jit(solution)/shard_map/ppermute | solution.py:431
  5.2 0.3 %collective-permute-start.4 = (bf16[80,512]{1,0:T(8,128)(2,1)S(1)}, bf16[80,512]{1,0:T(8,128)(2,1)S(1)}, u32[]{:S(2)}, u32[]{:S(2)}) collective-permute-start(bf16[80,512]{1,0:T(8,128)(2,1)S(1)} %get-tuple-element.22.refs_1_.refs_0_), channel_id=1, source_target_pairs={{0,2},{1,3},{2,0},{3,1},{4,6},{5,7},{6,4},{7,5},{8,10},{9,11},{10,... | collective-permute-start | bytes 245768 | tf_op jit(solution)/shard_map/ppermute | solution.py:431
  5.5 0.0 copy-done
  5.5 0.8 %latent_queries.1.q_ref = bf16[2048,640]{1,0:T(8,128)(2,1)S(1)} custom-call(bf16[128,2048]{1,0:T(8,128)(2,1)S(1)} %get-tuple-element.19.q_ref, bf16[128,1024]{1,0:T(8,128)(2,1)S(1)} %get-tuple-element.20.r_ref, bf16[512,2048]{1,0:T(8,128)(2,1)S(1)} %copy-done), custom_call_target="tpu_custom_call" | custom-call | flops 1000000 | bytes 1024 | tf_op jit(solution)/shard_map/latent_queries/pallas_call | solution.py:154
  6.3 0.0 collective-permute-done.2.refs_3_.refs_1_
  6.3 0.0 collective-permute-done.1.refs_2_
  6.3 4.0 %near_rows.1 = (f32[2048,128]{1,0:T(8,128)S(1)}, f32[2048,128]{1,0:T(8,128)S(1)}, f32[2048,128]{1,0:T(8,128)S(1)}, bf16[512,2048]{1,0:T(8,128)(2,1)S(1)}) custom-call(bf16[2048,640]{1,0:T(8,128)(2,1)S(1)} %latent_queries.1.q_ref, bf16[256,512]{1,0:T(8,128)(2,1)S(1)} %get-tuple-element.21.refs_0_, bf16[80,512]{1,0:T(8,128)(2,1)S(1)} %get-tuple-element.22.refs_1_.refs_0_, ...), custom_call_target="tpu_custom_call" | custom-call | flops 1000000000 | bytes 1024 | tf_op jit(solution)/shard_map/near_rows/pallas_call | solution.py:273
  10.3 0.1 collective-permute-done.array_ref.lat_ref
  10.4 0.1 collective-permute-start.3
  10.5 1.3 %early.1 = (f32[2048,256]{1,0:T(8,128)S(1)}, bf16[256,2048]{1,0:T(8,128)(2,1)S(1)}) custom-call(bf16[2048,640]{1,0:T(8,128)(2,1)S(1)} %latent_queries.1.q_ref, bf16[256,512]{1,0:T(8,128)(2,1)S(1)} %collective-permute-done.array_ref.lat_ref, bf16[512,2048]{1,0:T(8,128)(2,1)S(1)} %get-tuple-element.24.w_ref.refs_7_), custom_call_target="tpu_custom_call" | custom-call | flops 3000000000 | bytes 1024 | tf_op jit(solution)/shard_map/early/pallas_call | solution.py:296
  11.8 0.1 collective-permute-done.4.note_ref.array_ref.refs_2_
  11.9 0.4 %collective-permute-start.5 = (bf16[80,512]{1,0:T(8,128)(2,1)S(1)}, bf16[80,512]{1,0:T(8,128)(2,1)S(1)}, u32[]{:S(2)}, u32[]{:S(2)}) collective-permute-start(bf16[80,512]{1,0:T(8,128)(2,1)S(1)} %pass_on.3), channel_id=1, source_target_pairs={{0,1},{1,0},{2,3},{3,2},{4,5},{5,4},{6,7},{7,6},{8,9},{9,8},{10,11... | collective-permute-start | bytes 245768 | tf_op jit(solution)/shard_map/ppermute | solution.py:431
  12.3 0.0 collective-permute-done.3.lat_ref
  12.3 1.6 %far_rows.1 = (f32[2048,128]{1,0:T(8,128)S(1)}, f32[2048,128]{1,0:T(8,128)S(1)}, f32[2048,128]{1,0:T(8,128)S(1)}, bf16[256,2048]{1,0:T(8,128)(2,1)S(1)}) custom-call(bf16[2048,640]{1,0:T(8,128)(2,1)S(1)} %latent_queries.1.q_ref, bf16[80,512]{1,0:T(8,128)(2,1)S(1)} %collective-permute-done.4.note_ref.array_ref.refs_2_, ...), custom_call_target="tpu_custom_call" | custom-call | flops 3000000000 | bytes 1024 | tf_op jit(solution)/shard_map/far_rows/pallas_call | solution.py:355
  14.0 0.0 collective-permute-done.5.refs_3_
  14.0 3.5 %last_rows.1 = bf16[128,2048]{1,0:T(8,128)(2,1)} custom-call(bf16[2048,640]{1,0:T(8,128)(2,1)S(1)} %latent_queries.1.q_ref, bf16[256,512]{1,0:T(8,128)(2,1)S(1)} %collective-permute-done.3.lat_ref, bf16[256,2048]{1,0:T(8,128)(2,1)S(1)} %get-tuple-element.29.value_ref, bf16[80,512]{1,0:T(8,128)(2,1)S(1)} %get-tuple-element.22.refs_1_.refs_0_, ...), custom_call_target="tpu_custom_call" | custom-call | flops 1000000 | bytes 1024 | tf_op jit(solution)/shard_map/last_rows/pallas_call | solution.py:413
  (2 shorter events, 0.0 us)
Async XLA Ops:
  0.0 5.5 %copy-start = (bf16[512,2048]{1,0:T(8,128)(2,1)S(1)}, bf16[512,2048]{1,0:T(8,128)(2,1)}, u32[]{:S(2)}) copy-start(bf16[512,2048]{1,0:T(8,128)(2,1)} %w_ref.1) | copy-start | bytes 6291460
  0.0 6.3 %collective-permute-start.1 = (bf16[256,512]{1,0:T(8,128)(2,1)}, bf16[256,512]{1,0:T(8,128)(2,1)S(1)}, u32[]{:S(2)}, u32[]{:S(2)}) collective-permute-start(bf16[256,512]{1,0:T(8,128)(2,1)} %bitcast.7), channel_id=1, source_target_pairs={{0,1},{1,0},{2,3},{3,2},{4,5},{5,4},{6,7},{7,6},{8,9},{9,8},{10,11... | collective-permute-start | bytes 786440 | tf_op jit(solution)/shard_map/ppermute | solution.py:431
  0.5 9.9 %collective-permute-start = (bf16[256,512]{1,0:T(8,128)(2,1)}, bf16[256,512]{1,0:T(8,128)(2,1)S(1)}, u32[]{:S(2)}, u32[]{:S(2)}) collective-permute-start(bf16[256,512]{1,0:T(8,128)(2,1)} %bitcast.8), channel_id=1, source_target_pairs={{0,2},{1,3},{2,0},{3,1},{4,6},{5,7},{6,4},{7,5},{8,10},{9,11},{10,... | collective-permute-start | bytes 786440 | tf_op jit(solution)/shard_map/ppermute | solution.py:431
  5.0 1.3 %collective-permute-start.2 = (bf16[80,512]{1,0:T(8,128)(2,1)S(1)}, bf16[80,512]{1,0:T(8,128)(2,1)S(1)}, u32[]{:S(2)}, u32[]{:S(2)}) collective-permute-start(bf16[80,512]{1,0:T(8,128)(2,1)S(1)} %get-tuple-element.22.refs_1_.refs_0_), channel_id=1, source_target_pairs={{0,1},{1,0},{2,3},{3,2},{4,5},{5,4},{6,7},{7,6},{8,9},{9,8},{10,11... | collective-permute-start | bytes 245768 | tf_op jit(solution)/shard_map/ppermute | solution.py:431
  5.2 6.7 %collective-permute-start.4 = (bf16[80,512]{1,0:T(8,128)(2,1)S(1)}, bf16[80,512]{1,0:T(8,128)(2,1)S(1)}, u32[]{:S(2)}, u32[]{:S(2)}) collective-permute-start(bf16[80,512]{1,0:T(8,128)(2,1)S(1)} %get-tuple-element.22.refs_1_.refs_0_), channel_id=1, source_target_pairs={{0,2},{1,3},{2,0},{3,1},{4,6},{5,7},{6,4},{7,5},{8,10},{9,11},{10,... | collective-permute-start | bytes 245768 | tf_op jit(solution)/shard_map/ppermute | solution.py:431
  10.4 1.9 %collective-permute-start.3 = (bf16[256,512]{1,0:T(8,128)(2,1)S(1)}, bf16[256,512]{1,0:T(8,128)(2,1)S(1)}, u32[]{:S(2)}, u32[]{:S(2)}) collective-permute-start(bf16[256,512]{1,0:T(8,128)(2,1)S(1)} %pass_on.2), channel_id=1, source_target_pairs={{0,1},{1,0},{2,3},{3,2},{4,5},{5,4},{6,7},{7,6},{8,9},{9,8},{10,11... | collective-permute-start | bytes 786440 | tf_op jit(solution)/shard_map/ppermute | solution.py:431
  11.9 2.1 %collective-permute-start.5 = (bf16[80,512]{1,0:T(8,128)(2,1)S(1)}, bf16[80,512]{1,0:T(8,128)(2,1)S(1)}, u32[]{:S(2)}, u32[]{:S(2)}) collective-permute-start(bf16[80,512]{1,0:T(8,128)(2,1)S(1)} %pass_on.3), channel_id=1, source_target_pairs={{0,1},{1,0},{2,3},{3,2},{4,5},{5,4},{6,7},{7,6},{8,9},{9,8},{10,11... | collective-permute-start | bytes 245768 | tf_op jit(solution)/shard_map/ppermute | solution.py:431

commit v9 on v8

--- a/solution.py
+++ b/solution.py
@@ -18,7 +18,7 @@
 EXP_SCALE = math.log2(math.e) / math.sqrt(DH + DR)
 HEADS_STEP = 4
 HEADS_LAST = 8
-HEADS_SENT = 2
+HEADS_SENT = 4
 GROUP = 16
 COSTS = {"pack": 0.6, "latent_queries": 0.001, "pass_on": 0.001, "near_rows": 1.0, "early": 3.0, "far_rows": 3.0, "last_rows": 0.001}
 VMEM_LIMIT = 20 * 1024 * 1024

time: 17.7 us -> 17.7 us (level)
  no operation moved by 1% of the time
where the time goes in v9:
time: 17.7 us; the launch traced here: 17.4 us
  Pallas kernels  12.4 us (70%)
  starting transfers between devices  4.1 us (23%)
  between operations  0.71 us (4%)
  waiting for transfers between devices  0.23 us (1%)
    ppermute x6, starting transfers between devices, hop(): return lax.ppermute(array, 'ctx', [(k, k ^ bit) for k in range(size)])  4.1 us
    pallas_call x1, Pallas kernels, near_pass(): pl.pallas_call(functools.partial(near_kernel, cached=len(blocks), size=HE...  3.96 us
    pallas_call x1, Pallas kernels, last_pass(): pl.pallas_call(functools.partial(last_kernel, blocks=len(notes), size=HEA...  3.47 us
    pallas_call x1, Pallas kernels, far_pass(): pl.pallas_call(functools.partial(far_kernel, size=HEADS_STEP * count), ou...  1.62 us
    pallas_call x1, Pallas kernels, pack(): pl.pallas_call(pack_kernel, out_shape=(pltpu.VMEM((part + GROUP + DR // 2...  1.3 us
    pallas_call x1, Pallas kernels, early_pass(): pl.pallas_call(functools.partial(early_kernel, size=HEADS_STEP * count),...  1.26 us
    pallas_call x1, Pallas kernels, make_queries(): pl.pallas_call(queries_kernel, out_shape=pltpu.VMEM((heads * count, KEY),...  0.77 us
  transfers between devices with their start and end apart: 6, of which 2 were waited for; matrix products, arithmetic and copies ran while one was open for 0% of the time, Pallas kernels for 51%

profile of v9, /device:TPU:0, one launch (start us, length us, event | category | flops | bytes accessed | tf_op | source)
XLA Modules:
  0.0 17.4 jit_solution(36863143949325656)
XLA Ops:
  0.0 0.0 copy-start
  0.0 0.5 %collective-permute-start.1 = (bf16[256,512]{1,0:T(8,128)(2,1)}, bf16[256,512]{1,0:T(8,128)(2,1)S(1)}, u32[]{:S(2)}, u32[]{:S(2)}) collective-permute-start(bf16[256,512]{1,0:T(8,128)(2,1)} %bitcast.7), channel_id=1, source_target_pairs={{0,1},{1,0},{2,3},{3,2},{4,5},{5,4},{6,7},{7,6},{8,9},{9,8},{10,11... | collective-permute-start | bytes 786440 | tf_op jit(solution)/shard_map/ppermute | solution.py:431
  0.5 2.5 %collective-permute-start = (bf16[256,512]{1,0:T(8,128)(2,1)}, bf16[256,512]{1,0:T(8,128)(2,1)S(1)}, u32[]{:S(2)}, u32[]{:S(2)}) collective-permute-start(bf16[256,512]{1,0:T(8,128)(2,1)} %bitcast.8), channel_id=1, source_target_pairs={{0,2},{1,3},{2,0},{3,1},{4,6},{5,7},{6,4},{7,5},{8,10},{9,11},{10,... | collective-permute-start | bytes 786440 | tf_op jit(solution)/shard_map/ppermute | solution.py:431
  3.7 1.3 %pack.1 = (bf16[80,512]{1,0:T(8,128)(2,1)S(1)}, bf16[256,512]{1,0:T(8,128)(2,1)S(1)}, bf16[128,2048]{1,0:T(8,128)(2,1)S(1)}, bf16[128,1024]{1,0:T(8,128)(2,1)S(1)}) custom-call(bf16[32,512]{1,0:T(8,128)(2,1)} %bitcast.10, bf16[32,64]{1,0:T(8,128)(2,1)} %bitcast.12, bf16[64,256]{1,0:T(8,128)(2,1)} %bitcast.11, bf16[256,512]{1,0:T(8,128)(2,1)} %bitcast.9, ...), custom_call_target="tpu_custom_call" | custom-call | flops 600000000 | bytes 1024 | tf_op jit(solution)/shard_map/pack/pallas_call | solution.py:116
  5.0 0.2 %collective-permute-start.2 = (bf16[80,512]{1,0:T(8,128)(2,1)S(1)}, bf16[80,512]{1,0:T(8,128)(2,1)S(1)}, u32[]{:S(2)}, u32[]{:S(2)}) collective-permute-start(bf16[80,512]{1,0:T(8,128)(2,1)S(1)} %get-tuple-element.22.refs_1_.refs_0_), channel_id=1, source_target_pairs={{0,1},{1,0},{2,3},{3,2},{4,5},{5,4},{6,7},{7,6},{8,9},{9,8},{10,11... | collective-permute-start | bytes 245768 | tf_op jit(solution)/shard_map/ppermute | solution.py:431
  5.2 0.3 %collective-permute-start.4 = (bf16[80,512]{1,0:T(8,128)(2,1)S(1)}, bf16[80,512]{1,0:T(8,128)(2,1)S(1)}, u32[]{:S(2)}, u32[]{:S(2)}) collective-permute-start(bf16[80,512]{1,0:T(8,128)(2,1)S(1)} %get-tuple-element.22.refs_1_.refs_0_), channel_id=1, source_target_pairs={{0,2},{1,3},{2,0},{3,1},{4,6},{5,7},{6,4},{7,5},{8,10},{9,11},{10,... | collective-permute-start | bytes 245768 | tf_op jit(solution)/shard_map/ppermute | solution.py:431
  5.5 0.0 copy-done
  5.5 0.8 %latent_queries.1.q_ref = bf16[2048,640]{1,0:T(8,128)(2,1)S(1)} custom-call(bf16[128,2048]{1,0:T(8,128)(2,1)S(1)} %get-tuple-element.19.q_ref, bf16[128,1024]{1,0:T(8,128)(2,1)S(1)} %get-tuple-element.20.r_ref, bf16[512,2048]{1,0:T(8,128)(2,1)S(1)} %copy-done), custom_call_target="tpu_custom_call" | custom-call | flops 1000000 | bytes 1024 | tf_op jit(solution)/shard_map/latent_queries/pallas_call | solution.py:154
  6.3 0.0 collective-permute-done.2.refs_3_.refs_1_
  6.3 0.0 collective-permute-done.1.refs_2_
  6.3 4.0 %near_rows.1 = (f32[2048,128]{1,0:T(8,128)S(1)}, f32[2048,128]{1,0:T(8,128)S(1)}, f32[2048,128]{1,0:T(8,128)S(1)}, bf16[512,2048]{1,0:T(8,128)(2,1)S(1)}) custom-call(bf16[2048,640]{1,0:T(8,128)(2,1)S(1)} %latent_queries.1.q_ref, bf16[256,512]{1,0:T(8,128)(2,1)S(1)} %get-tuple-element.21.refs_0_, bf16[80,512]{1,0:T(8,128)(2,1)S(1)} %get-tuple-element.22.refs_1_.refs_0_, ...), custom_call_target="tpu_custom_call" | custom-call | flops 1000000000 | bytes 1024 | tf_op jit(solution)/shard_map/near_rows/pallas_call | solution.py:273
  10.3 0.1 collective-permute-done.array_ref.lat_ref
  10.4 0.1 collective-permute-start.3
  10.5 1.3 %early.1 = (f32[2048,256]{1,0:T(8,128)S(1)}, bf16[256,2048]{1,0:T(8,128)(2,1)S(1)}) custom-call(bf16[2048,640]{1,0:T(8,128)(2,1)S(1)} %latent_queries.1.q_ref, bf16[256,512]{1,0:T(8,128)(2,1)S(1)} %collective-permute-done.array_ref.lat_ref, bf16[512,2048]{1,0:T(8,128)(2,1)S(1)} %get-tuple-element.24.w_ref.refs_7_), custom_call_target="tpu_custom_call" | custom-call | flops 3000000000 | bytes 1024 | tf_op jit(solution)/shard_map/early/pallas_call | solution.py:296
  11.8 0.1 collective-permute-done.4.note_ref.array_ref.refs_2_
  11.9 0.4 %collective-permute-start.5 = (bf16[80,512]{1,0:T(8,128)(2,1)S(1)}, bf16[80,512]{1,0:T(8,128)(2,1)S(1)}, u32[]{:S(2)}, u32[]{:S(2)}) collective-permute-start(bf16[80,512]{1,0:T(8,128)(2,1)S(1)} %pass_on.3), channel_id=1, source_target_pairs={{0,1},{1,0},{2,3},{3,2},{4,5},{5,4},{6,7},{7,6},{8,9},{9,8},{10,11... | collective-permute-start | bytes 245768 | tf_op jit(solution)/shard_map/ppermute | solution.py:431
  12.3 0.0 collective-permute-done.3.lat_ref
  12.3 1.6 %far_rows.1 = (f32[2048,128]{1,0:T(8,128)S(1)}, f32[2048,128]{1,0:T(8,128)S(1)}, f32[2048,128]{1,0:T(8,128)S(1)}, bf16[256,2048]{1,0:T(8,128)(2,1)S(1)}) custom-call(bf16[2048,640]{1,0:T(8,128)(2,1)S(1)} %latent_queries.1.q_ref, bf16[80,512]{1,0:T(8,128)(2,1)S(1)} %collective-permute-done.4.note_ref.array_ref.refs_2_, ...), custom_call_target="tpu_custom_call" | custom-call | flops 3000000000 | bytes 1024 | tf_op jit(solution)/shard_map/far_rows/pallas_call | solution.py:355
  14.0 0.0 collective-permute-done.5.refs_3_
  14.0 3.5 %last_rows.1 = bf16[128,2048]{1,0:T(8,128)(2,1)} custom-call(bf16[2048,640]{1,0:T(8,128)(2,1)S(1)} %latent_queries.1.q_ref, bf16[256,512]{1,0:T(8,128)(2,1)S(1)} %collective-permute-done.3.lat_ref, bf16[256,2048]{1,0:T(8,128)(2,1)S(1)} %get-tuple-element.29.value_ref, bf16[80,512]{1,0:T(8,128)(2,1)S(1)} %get-tuple-element.22.refs_1_.refs_0_, ...), custom_call_target="tpu_custom_call" | custom-call | flops 1000000 | bytes 1024 | tf_op jit(solution)/shard_map/last_rows/pallas_call | solution.py:413
  (2 shorter events, 0.0 us)
Async XLA Ops:
  0.0 5.5 %copy-start = (bf16[512,2048]{1,0:T(8,128)(2,1)S(1)}, bf16[512,2048]{1,0:T(8,128)(2,1)}, u32[]{:S(2)}) copy-start(bf16[512,2048]{1,0:T(8,128)(2,1)} %w_ref.1) | copy-start | bytes 6291460
  0.0 6.3 %collective-permute-start.1 = (bf16[256,512]{1,0:T(8,128)(2,1)}, bf16[256,512]{1,0:T(8,128)(2,1)S(1)}, u32[]{:S(2)}, u32[]{:S(2)}) collective-permute-start(bf16[256,512]{1,0:T(8,128)(2,1)} %bitcast.7), channel_id=1, source_target_pairs={{0,1},{1,0},{2,3},{3,2},{4,5},{5,4},{6,7},{7,6},{8,9},{9,8},{10,11... | collective-permute-start | bytes 786440 | tf_op jit(solution)/shard_map/ppermute | solution.py:431
  0.5 9.9 %collective-permute-start = (bf16[256,512]{1,0:T(8,128)(2,1)}, bf16[256,512]{1,0:T(8,128)(2,1)S(1)}, u32[]{:S(2)}, u32[]{:S(2)}) collective-permute-start(bf16[256,512]{1,0:T(8,128)(2,1)} %bitcast.8), channel_id=1, source_target_pairs={{0,2},{1,3},{2,0},{3,1},{4,6},{5,7},{6,4},{7,5},{8,10},{9,11},{10,... | collective-permute-start | bytes 786440 | tf_op jit(solution)/shard_map/ppermute | solution.py:431
  5.0 1.3 %collective-permute-start.2 = (bf16[80,512]{1,0:T(8,128)(2,1)S(1)}, bf16[80,512]{1,0:T(8,128)(2,1)S(1)}, u32[]{:S(2)}, u32[]{:S(2)}) collective-permute-start(bf16[80,512]{1,0:T(8,128)(2,1)S(1)} %get-tuple-element.22.refs_1_.refs_0_), channel_id=1, source_target_pairs={{0,1},{1,0},{2,3},{3,2},{4,5},{5,4},{6,7},{7,6},{8,9},{9,8},{10,11... | collective-permute-start | bytes 245768 | tf_op jit(solution)/shard_map/ppermute | solution.py:431
  5.2 6.7 %collective-permute-start.4 = (bf16[80,512]{1,0:T(8,128)(2,1)S(1)}, bf16[80,512]{1,0:T(8,128)(2,1)S(1)}, u32[]{:S(2)}, u32[]{:S(2)}) collective-permute-start(bf16[80,512]{1,0:T(8,128)(2,1)S(1)} %get-tuple-element.22.refs_1_.refs_0_), channel_id=1, source_target_pairs={{0,2},{1,3},{2,0},{3,1},{4,6},{5,7},{6,4},{7,5},{8,10},{9,11},{10,... | collective-permute-start | bytes 245768 | tf_op jit(solution)/shard_map/ppermute | solution.py:431
  10.4 1.9 %collective-permute-start.3 = (bf16[256,512]{1,0:T(8,128)(2,1)S(1)}, bf16[256,512]{1,0:T(8,128)(2,1)S(1)}, u32[]{:S(2)}, u32[]{:S(2)}) collective-permute-start(bf16[256,512]{1,0:T(8,128)(2,1)S(1)} %pass_on.2), channel_id=1, source_target_pairs={{0,1},{1,0},{2,3},{3,2},{4,5},{5,4},{6,7},{7,6},{8,9},{9,8},{10,11... | collective-permute-start | bytes 786440 | tf_op jit(solution)/shard_map/ppermute | solution.py:431
  11.9 2.1 %collective-permute-start.5 = (bf16[80,512]{1,0:T(8,128)(2,1)S(1)}, bf16[80,512]{1,0:T(8,128)(2,1)S(1)}, u32[]{:S(2)}, u32[]{:S(2)}) collective-permute-start(bf16[80,512]{1,0:T(8,128)(2,1)S(1)} %pass_on.3), channel_id=1, source_target_pairs={{0,1},{1,0},{2,3},{3,2},{4,5},{5,4},{6,7},{7,6},{8,9},{9,8},{10,11... | collective-permute-start | bytes 245768 | tf_op jit(solution)/shard_map/ppermute | solution.py:431
